TPU v7x, 32 devices: a whole 2x2x4 slice. The times are simulated.
32 devices in a mesh: row: 4 (over x, core), col: 4 (over z), pair: 2 (over y).
Axes of the slice: x: 2, y: 2, z: 4, core: 2. Of those that a mesh axis runs over, the one named last changes fastest.
Arguments:
- factors: bfloat16 [1800, 512, 16], P('pair', ('row', 'col')), may hold values from -1 to 1
- amplitudes: bfloat16 [20, 16, 16], P('pair'), may hold values from -0.796875 to 0.796875
- virt_irreps: int32 [512], replicated, may hold values from 0 to 3
- win_irreps: int32 [16], replicated, may hold values from 0 to 3
- occ_irreps: int32 [120], replicated, may hold values from 0 to 3
- pair_list: int32 [20, 2], replicated, may hold values from 0 to 119
Outputs:
- ladder: float32 [20, 512, 4, 128], P('pair', 'row', None, 'col')
All inputs are finite; a program needn't handle non-finite values.
Results may differ from a plain program's by a relative error of at most 0.0003.
Values may be sent and summed in bfloat16 or wider, within the bound.
No kernel may reach another device: no remote copies, remote signals or barrier semaphores. Data moves between devices by JAX's collectives and lax.ppermute only.
A program may use at most 64 MiB of HBM per device.

v0:
```python
import jax
import jax.numpy as jnp
from jax import lax
from jax.sharding import PartitionSpec as P


def lookup_symmetry(occ_irreps, pair_list):
    labels = jnp.arange(occ_irreps.shape[0], dtype=jnp.int32)
    onehot = pair_list[:, :, None] == labels[None, None, :]
    picked = jnp.sum(jnp.where(onehot, occ_irreps[None, None, :], 0), axis=-1)
    return jnp.bitwise_xor(picked[:, 0], picked[:, 1])


def mask_amplitudes(amplitudes, win_irreps, symmetry):
    product = jnp.bitwise_xor(win_irreps[:, None], win_irreps[None, :])
    allowed = product[None, :, :] == symmetry[:, None, None]
    return jnp.where(allowed, amplitudes.astype(jnp.float32), 0.0)


def body(factors, amplitudes, virt_irreps, win_irreps, occ_irreps, pair_list):
    per_device = factors.shape[1]
    n_rows = lax.axis_size("row")
    n_cols = lax.axis_size("col")
    block_a = per_device * n_cols
    slab = amplitudes.shape[0]
    symmetry_all = lookup_symmetry(occ_irreps, pair_list)
    own_symmetry = lax.dynamic_slice_in_dim(symmetry_all, lax.axis_index("pair") * slab, slab)
    operand = lax.all_gather(factors, "pair", axis=0, tiled=True)
    weights = mask_amplitudes(amplitudes, win_irreps, own_symmetry)
    n_fitting = operand.shape[0]
    width = operand.shape[2]
    b_rows = lax.all_gather(operand, "row", axis=1, tiled=True)
    b_matrix = b_rows.reshape(n_fitting, n_rows * per_device * width)
    panel_rows = lax.all_gather(operand, "col", axis=1, tiled=True)
    count = panel_rows.shape[1]
    integral = lax.dot_general(
        panel_rows.reshape(n_fitting, count * width),
        b_matrix,
        (((0,), (0,)), ((), ())),
        preferred_element_type=jnp.float32,
    )
    integral = integral.reshape(count, width, n_rows * per_device, width)
    result = jnp.einsum("acbd,pcd->pab", integral, weights, precision=lax.Precision.HIGHEST)
    partial_sum = result.reshape(weights.shape[0], count, n_rows, per_device)
    a_labels = lax.dynamic_slice_in_dim(virt_irreps, lax.axis_index("row") * block_a, block_a)
    b_labels = lax.dynamic_slice_in_dim(
        virt_irreps.reshape(n_rows, -1), lax.axis_index("col") * per_device, per_device, 1
    )
    pair_sym = jnp.bitwise_xor(a_labels[:, None, None], b_labels[None, :, :])
    allowed = pair_sym[None, :, :, :] == own_symmetry[:, None, None, None]
    return jnp.where(allowed, partial_sum, 0.0)


def solution(mesh):
    in_specs = (P("pair", ("row", "col"), None), P("pair", None, None), P(), P(), P(), P())
    out_specs = P("pair", "row", None, "col")
    return jax.shard_map(body, mesh=mesh, in_specs=in_specs, out_specs=out_specs, check_vma=False)
```

profile of v0, /device:TPU:0, one launch (start us, length us, event | category | flops | bytes accessed | tf_op | source)
XLA Modules:
  0.0 376.2 jit_solution(17692180430424388559)
XLA Ops:
  6.5 7.2 %copy.39 = bf16[900,32,16]{1,2,0:T(8,128)(2,1)} copy(bf16[900,32,16]{0,2,1:T(8,128)(2,1)} %param.6) | data formatting | bytes 1843200 | tf_op args[0]
  13.8 0.0 all-gather.4.cloned.1.call-update
  13.8 0.0 all-gather.8.cloned.1.call-start
  13.9 95.4 %all-gather.4.cloned.1.call-done = bf16[1800,32,16]{1,2,0:T(8,128)(2,1)} async-done(((bf16[900,32,16]{1,2,0:T(8,128)(2,1)}), bf16[1800,32,16]{1,2,0:T(8,128)(2,1)}) %all-gather.4.cloned.1.call-update) | async-done | bytes 1843216 | tf_op jit(solution)/shard_map/all_gather | solution.py:28
  109.2 10.4 %copy.40 = bf16[1800,32,16]{0,2,1:T(8,128)(2,1)} copy(bf16[1800,32,16]{1,2,0:T(8,128)(2,1)} %all-gather.4.cloned.1.call-done) | data formatting | bytes 3686400 | tf_op jit(solution)/shard_map/all_gather | solution.py:28
  119.6 0.0 all-gather.8.cloned.1.call-update
  119.7 0.0 all-gather.6.cloned.1.call-start
  119.7 0.7 all-gather.6.cloned.1.call-update
  120.4 0.1 copy.38
  120.5 0.1 dynamic_slice.11
  120.6 0.5 fusion.10
  121.1 0.1 fusion.12
  121.2 0.1 fusion.11
  121.3 0.1 constant_dynamic-slice_fusion
  121.4 0.1 broadcast_xor_fusion.1
  121.4 0.1 broadcast_xor_fusion
  121.5 0.1 convert_select_fusion
  121.6 53.5 %all-gather.8.cloned.1.call-done = bf16[1800,128,16]{0,2,1:T(8,128)(2,1)} async-done(((bf16[1800,32,16]{0,2,1:T(8,128)(2,1)}), bf16[1800,128,16]{0,2,1:T(8,128)(2,1)}) %all-gather.8.cloned.1.call-update) | async-done | bytes 7372816 | tf_op jit(solution)/shard_map/all_gather | solution.py:32
  175.1 11.0 %copy.43 = bf16[128,16,1800]{0,2,1:T(8,128)(2,1)} copy(bf16[128,16,1800]{2,1,0:T(8,128)(2,1)} %bitcast.23) | data formatting | bytes 14745600 | tf_op jit(solution)/shard_map/dot_general | solution.py:36
  186.1 131.7 %all-gather.6.cloned.1.call-done = bf16[1800,128,16]{0,2,1:T(8,128)(2,1)} async-done(((bf16[1800,32,16]{0,2,1:T(8,128)(2,1)}), bf16[1800,128,16]{0,2,1:T(8,128)(2,1)}) %all-gather.6.cloned.1.call-update) | async-done | bytes 7372816 | tf_op jit(solution)/shard_map/all_gather | solution.py:34
  317.8 21.3 %fusion.2 = f32[128,16,128,16]{2,0,3,1:T(8,128)S(1)} fusion(bf16[128,16,1800,1]{2,1,0,3:T(8,128)(2,1)} %bitcast.26, bf16[128,16,1800]{0,2,1:T(8,128)(2,1)} %copy.43), kind=kOutput, calls=%fused_computation.2 | convolution fusion | flops 15099494400 | bytes 31522816 | tf_op jit(solution)/shard_map/dot_general | solution.py:36
  339.1 29.3 %fusion.5 = f32[10,128,128]{2,0,1:T(8,128)S(1)} fusion(f32[128,16,128,16]{2,0,3,1:T(8,128)S(1)} %fusion.2, f32[10,16,16]{2,1,0:T(8,128)S(1)} %convert_select_fusion), kind=kOutput, calls=%fused_computation.5 | convolution fusion | flops 503316480 | bytes 17442816 | tf_op jit(solution)/shard_map/acbd,pcd->pab/dot_general | solution.py:43
  368.4 0.3 copy.46
  368.7 1.0 compare_select_fusion
  (11 shorter events, 0.0 us)
Async XLA Ops:
  6.5 102.7 %all-gather.4.cloned.1.call-start = ((), (), s32[]{:S(2)}) async-start(), calls=%async_computation | async-start | bytes 11059200 | tf_op jit(solution)/shard_map/all_gather | solution.py:28
  13.8 106.7 %copy-start.3 = (s32[20,2]{0,1:T(2,128)S(1)}, s32[20,2]{0,1:T(2,128)}, u32[]{:S(2)}) copy-start(s32[20,2]{0,1:T(2,128)} %param.11) | copy-start | bytes 484
  13.8 106.8 %copy-start.2 = (s32[512]{0:T(512)S(1)}, s32[512]{0:T(512)}, u32[]{:S(2)}) copy-start(s32[512]{0:T(512)} %param.8) | copy-start | bytes 6148
  13.8 106.8 %copy-start.4 = (s32[120]{0:T(128)S(1)}, s32[120]{0:T(128)}, u32[]{:S(2)}) copy-start(s32[120]{0:T(128)} %param.10) | copy-start | bytes 1444
  13.8 107.6 %copy-start.1 = (s32[16]{0:T(128)S(1)}, s32[16]{0:T(128)}, u32[]{:S(2)}) copy-start(s32[16]{0:T(128)} %param.9) | copy-start | bytes 196
  13.8 107.7 %copy-start = (bf16[10,16,16]{2,1,0:T(8,128)(2,1)S(1)}, bf16[10,16,16]{2,1,0:T(8,128)(2,1)}, u32[]{:S(2)}) copy-start(bf16[10,16,16]{2,1,0:T(8,128)(2,1)} %param.7) | copy-start | bytes 15364
  13.8 161.3 %all-gather.8.cloned.1.call-start = ((), (), s32[]{:S(2)}) async-start(), calls=%async_computation.2 | async-start | bytes 9830400 | tf_op jit(solution)/shard_map/all_gather | solution.py:32
  119.7 198.2 %all-gather.6.cloned.1.call-start = ((), (), s32[]{:S(2)}) async-start(), calls=%async_computation.1 | async-start | bytes 9830400 | tf_op jit(solution)/shard_map/all_gather | solution.py:34
Sparse Core Ops, SparseCore 0:
  13.9 95.2 all-gather.3
  119.8 55.3 all-gather.7
  176.7 141.0 all-gather.5
where the time goes:
time: 377 us; the launch traced here: 376 us
  waiting for transfers between devices  281 us (75%)
  matrix products  50.5 us (13%)
  local copies, waits for them, and re-layouts  29.3 us (8%)
  between operations  13.2 us (4%)
    all_gather x1, waiting for transfers between devices, body(): panel_rows = lax.all_gather(operand, 'col', axis=1, tiled=True)  132 us
    all_gather x1, waiting for transfers between devices, body(): operand = lax.all_gather(factors, 'pair', axis=0, tiled=True)  95.4 us
    all_gather x1, waiting for transfers between devices, body(): b_rows = lax.all_gather(operand, 'row', axis=1, tiled=True)  53.5 us
    dot_general x1, matrix products, body(): jnp.einsum('acbd,pcd->pab', integral, weights, precision=lax.Precision.HI...  29.3 us
    dot_general x1, matrix products, body(): lax.dot_general(panel_rows.reshape(n_fitting, count * width), b_matrix, (...  21.3 us
    dot_general x1, local copies, waits for them, and re-layouts, body(): lax.dot_general(panel_rows.reshape(n_fitting, count * width), b_matrix, (...  11 us
    all_gather x1, local copies, waits for them, and re-layouts, body(): operand = lax.all_gather(factors, 'pair', axis=0, tiled=True)  10.4 us
  transfers between devices with their start and end apart: 3, of which 3 were waited for; matrix products, arithmetic and copies ran while one was open for 3% of the time, Pallas kernels for 0%

commit v1 on v0

v1 whole, which is shorter than its diff:
```python
import functools

import jax
import jax.numpy as jnp
from jax import lax
from jax.experimental import pallas as pl
from jax.experimental.pallas import tpu as pltpu
from jax.sharding import PartitionSpec as P

VMEM_LIMIT = 40 * 1024 * 1024
NT = (((1,), (1,)), ((), ()))
NN = (((1,), (0,)), ((), ()))


def lookup_symmetry(occ_irreps, pair_list):
    labels = jnp.arange(occ_irreps.shape[0], dtype=jnp.int32)
    onehot = pair_list[:, :, None] == labels[None, None, :]
    picked = jnp.sum(jnp.where(onehot, occ_irreps[None, None, :], 0), axis=-1)
    return jnp.bitwise_xor(picked[:, 0], picked[:, 1])


def mask_amplitudes(amplitudes, win_irreps, symmetry):
    product = jnp.bitwise_xor(win_irreps[:, None], win_irreps[None, :])
    allowed = product[None, :, :] == symmetry[:, None, None]
    return jnp.where(allowed, amplitudes, jnp.zeros_like(amplitudes))


def gathered_body(factors, amplitudes, virt_irreps, win_irreps, occ_irreps, pair_list):
    per_device = factors.shape[1]
    n_rows = lax.axis_size("row")
    n_cols = lax.axis_size("col")
    block_a = per_device * n_cols
    slab = amplitudes.shape[0]
    symmetry = lookup_symmetry(occ_irreps, pair_list)
    own_symmetry = lax.dynamic_slice_in_dim(symmetry, lax.axis_index("pair") * slab, slab)
    every = lax.all_gather(amplitudes, "pair", axis=0, tiled=True)
    weights = mask_amplitudes(every, win_irreps, symmetry).astype(jnp.float32)
    n_fitting, _, width = factors.shape
    b_rows = lax.all_gather(factors, "row", axis=1, tiled=True)
    a_rows = lax.all_gather(factors, "col", axis=1, tiled=True)
    integral = lax.dot_general(
        a_rows.reshape(n_fitting, block_a * width),
        b_rows.reshape(n_fitting, n_rows * per_device * width),
        (((0,), (0,)), ((), ())),
        preferred_element_type=jnp.float32,
    )
    integral = integral.reshape(block_a, width, n_rows * per_device, width)
    part = jnp.einsum("acbd,pcd->pab", integral, weights, precision=lax.Precision.HIGHEST)
    full = lax.psum_scatter(part, "pair", scatter_dimension=0, tiled=True)
    full = full.reshape(slab, block_a, n_rows, per_device)
    a_labels = lax.dynamic_slice_in_dim(virt_irreps, lax.axis_index("row") * block_a, block_a)
    b_labels = lax.dynamic_slice_in_dim(
        virt_irreps.reshape(n_rows, -1), lax.axis_index("col") * per_device, per_device, 1
    )
    pair_sym = jnp.bitwise_xor(a_labels[:, None, None], b_labels[None, :, :])
    allowed = pair_sym[None, :, :, :] == own_symmetry[:, None, None, None]
    return jnp.where(allowed, full, 0.0)


def is_middle():
    col = lax.axis_index("col")
    return jnp.logical_or(col == 1, col == 2)


def window_major(width, per_device):
    n = width * per_device
    into = lax.broadcasted_iota(jnp.int32, (n, n), 0)
    out_of = lax.broadcasted_iota(jnp.int32, (n, n), 1)
    wanted = lax.rem(into, per_device) * width + lax.div(into, per_device)
    return (wanted == out_of).astype(jnp.bfloat16)


def place_rows(panel, order, rows, k):
    width, _, per_device, n_fit = panel.shape
    moved = lax.dot_general(order, rows, NN, preferred_element_type=jnp.float32)
    panel[:, pl.ds(k, 1)] = moved.astype(panel.dtype).reshape(width, 1, per_device, n_fit)


def contract_block(rows, panel, weights, split, sums, keep, send):
    width, n_rows, per_device, n_fit = panel.shape
    n_b = n_rows * per_device
    n_a = rows.shape[0] // width
    half = keep.shape[0]
    n_p = weights.shape[0]

    def integrals(step, carry):
        two = panel[pl.ds(2 * step, 2)].reshape(2 * n_b, n_fit)
        acc = lax.dot_general(rows[...], two, NT, preferred_element_type=jnp.float32)
        high = acc.astype(jnp.bfloat16)
        low = (acc - high.astype(jnp.float32)).astype(jnp.bfloat16)
        for j in range(2):
            lanes = slice(j * n_b, (j + 1) * n_b)
            split[:, 0, pl.ds(2 * step + j, 1)] = high[:, lanes].reshape(n_a, 1, width, n_b)
            split[:, 1, pl.ds(2 * step + j, 1)] = low[:, lanes].reshape(n_a, 1, width, n_b)
        return carry

    lax.fori_loop(0, width // 2, integrals, 0)

    def ladder(step, carry):
        depth = 2 * width * width
        two = [split[2 * step + j].reshape(depth, n_b) for j in range(2)]
        both = jnp.concatenate(two, axis=1)
        res = lax.dot_general(weights[...], both, NN, preferred_element_type=jnp.float32)
        for j in range(2):
            sums[pl.ds((2 * step + j) * n_p, n_p), :] = res[:, j * n_b : (j + 1) * n_b]
        return carry

    lax.fori_loop(0, n_a // 2, ladder, 0)
    for p in range(half):
        keep[p] = sums[pl.ds(p, n_a, stride=n_p), :]
        send[p] = sums[pl.ds(n_p // 2 + p, n_a, stride=n_p), :]


def early_kernel(own, facing, middle, by_core, by_x, by_both, weights, keep, send, panel_out, panel, held, split, sums, sems):
    sources = (own, by_core, by_x, by_both, facing, middle)
    copies = [pltpu.make_async_copy(src, held.at[i], sems.at[i]) for i, src in enumerate(sources)]
    for copy in copies:
        copy.start()
    row = lax.axis_index("row")
    width, _, per_device, _ = panel.shape
    order = window_major(width, per_device)
    for i in range(4):
        copies[i].wait()
        place_rows(panel, order, held[i], jnp.bitwise_xor(row, i))
    back = pltpu.make_async_copy(panel, panel_out, sems.at[6])
    back.start()
    copies[4].wait()
    copies[5].wait()
    contract_block(held.at[0], panel, weights, split, sums, keep.at[0], send.at[0])
    contract_block(held.at[4], panel, weights, split, sums, keep.at[1], send.at[1])

    @pl.when(is_middle())
    def _():
        contract_block(held.at[5], panel, weights, split, sums, keep.at[2], send.at[2])

    back.wait()


def across_kernel(far, facing, by_core, by_x, by_both, weights, keep, send, panel, held, split, sums, sems):
    @pl.when(is_middle())
    def _():
        sources = (facing, by_core, by_x, by_both, far)
        copies = [pltpu.make_async_copy(src, held.at[i], sems.at[i]) for i, src in enumerate(sources)]
        for copy in copies:
            copy.start()
        row = lax.axis_index("row")
        width, _, per_device, _ = panel.shape
        order = window_major(width, per_device)
        for i in range(4):
            copies[i].wait()
            place_rows(panel, order, held[i], jnp.bitwise_xor(row, i))
        copies[4].wait()
        contract_block(held.at[4], panel, weights, split, sums, keep, send)


def late_kernel(far, passed, panel_in, weights, keep, send, panel, held, split, sums, sems):
    copy_panel = pltpu.make_async_copy(panel_in, panel, sems.at[0])
    copy_panel.start()

    @pl.when(is_middle())
    def _():
        copy = pltpu.make_async_copy(far, held, sems.at[1])
        copy.start()
        copy.wait()

    @pl.when(jnp.logical_not(is_middle()))
    def _():
        copy = pltpu.make_async_copy(passed, held, sems.at[1])
        copy.start()
        copy.wait()

    copy_panel.wait()
    contract_block(held, panel, weights, split, sums, keep, send)


def finish_kernel(symmetry, pair_sym, keep_early, got_early, keep_late, got_late, across, out, whole):
    col = lax.axis_index("col")
    middle = is_middle()
    lower = col < 2
    n_p, n_a, _ = keep_late.shape
    planes = (col, jnp.bitwise_xor(col, 1), jnp.where(lower, 2, 1), jnp.where(lower, 3, 0))

    def place(s):
        return pl.ds(pl.multiple_of(planes[s] * n_a, n_a), n_a)

    for s in range(2):
        whole[:, place(s), :] = keep_early[s] + got_early[s]

    @pl.when(middle)
    def _():
        whole[:, place(2), :] = keep_early[2] + got_early[2]
        whole[:, place(3), :] = keep_late[...] + got_late[...]

    @pl.when(jnp.logical_not(middle))
    def _():
        whole[:, place(2), :] = keep_late[...] + got_late[...]
        whole[:, place(3), :] = across[...]

    for p in range(n_p):
        out[p] = jnp.where(pair_sym[...] == symmetry[p], whole[p].T, 0.0)


def swap(array, axis, mask):
    size = lax.axis_size(axis)
    return lax.ppermute(array, axis, [(i, i ^ mask) for i in range(size)])


def staged_body(factors, amplitudes, virt_irreps, win_irreps, occ_irreps, pair_list):
    n_fit, per_device, width = factors.shape
    n_rows = lax.axis_size("row")
    n_cols = lax.axis_size("col")
    n_b = n_rows * per_device
    block_a = per_device * n_cols
    slab = amplitudes.shape[0]
    rows_shape = (per_device * width, n_fit)

    own = jnp.transpose(factors, (1, 2, 0)).reshape(rows_shape)
    facing = swap(own, "col", 1)
    middle = lax.ppermute(own, "col", [(1, 2), (2, 1)])
    by_x = swap(own, "row", 2)
    by_core = swap(own, "row", 1)
    other_amplitudes = swap(amplitudes, "pair", 1)

    far = lax.ppermute(facing, "col", [(1, 2), (2, 1)])
    passed = lax.ppermute(middle, "col", [(1, 0), (2, 3)])
    by_both = swap(by_x, "row", 1)

    def middle_swap(array, mask):
        pairs = [(r * n_cols + c, (r ^ mask) * n_cols + c) for r in range(n_rows) for c in (1, 2)]
        return lax.ppermute(array, ("row", "col"), pairs)

    facing_x = middle_swap(facing, 2)
    facing_core = middle_swap(facing, 1)
    facing_both = middle_swap(facing_x, 1)

    symmetry = lookup_symmetry(occ_irreps, pair_list)
    pair_index = lax.axis_index("pair")
    own_symmetry = lax.dynamic_slice_in_dim(symmetry, pair_index * slab, slab)
    other_symmetry = lax.dynamic_slice_in_dim(symmetry, (1 - pair_index) * slab, slab)
    padded = 16 * pl.cdiv(slab, 16)

    def weight_rows(array, sym):
        masked = jnp.transpose(mask_amplitudes(array, win_irreps, sym), (0, 2, 1)).reshape(slab, width * width)
        return jnp.pad(jnp.concatenate([masked, masked], axis=1), ((0, padded - slab), (0, 0)))

    weights = jnp.concatenate(
        [weight_rows(amplitudes, own_symmetry), weight_rows(other_amplitudes, other_symmetry)], axis=0
    )

    a_labels = lax.dynamic_slice_in_dim(virt_irreps, lax.axis_index("row") * block_a, block_a)
    b_labels = lax.dynamic_slice_in_dim(
        virt_irreps.reshape(n_rows, -1), lax.axis_index("col") * per_device, per_device, 1
    ).reshape(n_b)
    pair_sym = jnp.bitwise_xor(b_labels[:, None], a_labels[None, :])

    anywhere = pl.BlockSpec(memory_space=pl.ANY)
    vmem = pl.BlockSpec(memory_space=pltpu.VMEM)
    smem = pl.BlockSpec(memory_space=pltpu.SMEM)
    params = pltpu.CompilerParams(vmem_limit_bytes=VMEM_LIMIT)
    block = jax.ShapeDtypeStruct((slab, per_device, n_b), jnp.float32)
    blocks = jax.ShapeDtypeStruct((3, slab, per_device, n_b), jnp.float32)
    panel_shape = (width, n_rows, per_device, n_fit)
    panel_scratch = pltpu.VMEM(panel_shape, jnp.bfloat16)
    split_scratch = pltpu.VMEM((per_device, 2, width, width, n_b), jnp.bfloat16)
    sums_scratch = pltpu.VMEM((per_device * 2 * padded, n_b), jnp.float32)

    def cost(n_blocks):
        flops = 2 * n_blocks * rows_shape[0] * n_b * width * n_fit
        return pl.CostEstimate(flops=flops, bytes_accessed=8 * rows_shape[0] * n_fit, transcendentals=0)

    keep_early, send_early, panel = pl.pallas_call(
        early_kernel,
        out_shape=(blocks, blocks, jax.ShapeDtypeStruct(panel_shape, jnp.bfloat16)),
        in_specs=[anywhere] * 6 + [vmem],
        out_specs=(vmem, vmem, anywhere),
        scratch_shapes=[
            panel_scratch,
            pltpu.VMEM((6,) + rows_shape, jnp.bfloat16),
            split_scratch,
            sums_scratch,
            pltpu.SemaphoreType.DMA((7,)),
        ],
        compiler_params=params,
        cost_estimate=cost(4),
    )(own, facing, middle, by_core, by_x, by_both, weights)
    got_early = swap(send_early, "pair", 1)

    keep_across, send_across = pl.pallas_call(
        across_kernel,
        out_shape=(block, block),
        in_specs=[anywhere] * 5 + [vmem],
        out_specs=(vmem, vmem),
        scratch_shapes=[
            panel_scratch,
            pltpu.VMEM((5,) + rows_shape, jnp.bfloat16),
            split_scratch,
            sums_scratch,
            pltpu.SemaphoreType.DMA((5,)),
        ],
        compiler_params=params,
        cost_estimate=cost(1),
    )(far, facing, facing_core, facing_x, facing_both, weights)
    n_pair = lax.axis_size("pair")
    across_pairs = [(c * n_pair + y, c * n_pair + (y ^ 1)) for c in (1, 2) for y in range(n_pair)]
    got_across = lax.ppermute(send_across, ("col", "pair"), across_pairs)
    across = lax.ppermute(keep_across + got_across, "col", [(1, 0), (2, 3)])

    keep_late, send_late = pl.pallas_call(
        late_kernel,
        out_shape=(block, block),
        in_specs=[anywhere] * 3 + [vmem],
        out_specs=(vmem, vmem),
        scratch_shapes=[
            panel_scratch,
            pltpu.VMEM(rows_shape, jnp.bfloat16),
            split_scratch,
            sums_scratch,
            pltpu.SemaphoreType.DMA((2,)),
        ],
        compiler_params=params,
        cost_estimate=cost(1),
    )(far, passed, panel, weights)
    got_late = swap(send_late, "pair", 1)

    out = pl.pallas_call(
        finish_kernel,
        out_shape=jax.ShapeDtypeStruct((slab, n_b, block_a), jnp.float32),
        in_specs=[smem] + [vmem] * 6,
        out_specs=vmem,
        scratch_shapes=[pltpu.VMEM((slab, block_a, n_b), jnp.float32)],
        compiler_params=params,
    )(own_symmetry, pair_sym, keep_early, got_early, keep_late, got_late, across)
    return jnp.transpose(out.reshape(slab, n_rows, per_device, block_a), (0, 3, 1, 2))


def solution(mesh):
    staged = (mesh.shape["row"], mesh.shape["col"], mesh.shape["pair"]) == (4, 4, 2)
    body = staged_body if staged else gathered_body
    in_specs = (P("pair", ("row", "col"), None), P("pair", None, None), P(), P(), P(), P())
    out_specs = P("pair", "row", None, "col")
    return jax.shard_map(body, mesh=mesh, in_specs=in_specs, out_specs=out_specs, check_vma=False)
```

time: 377 us -> 138 us (0.37)
  waiting for transfers between devices: 281 us -> 51.4 us
  matrix products: 50.5 us -> 0 us
  Pallas kernels: 0 us -> 26.9 us
  starting transfers between devices: 0.09 us -> 19.8 us
  between operations: 13.2 us -> 0.22 us
  local copies, waits for them, and re-layouts: 29.3 us -> 35.4 us
    all_gather x3 -> x0, waiting for transfers between devices: 281 us -> none  [the longest x1 132 us: body(): panel_rows = lax.all_gather(operand, 'col', axis=1, tiled=True)]
    ppermute x0 -> x15, waiting for transfers between devices: none -> 51.4 us  [the longest x1 30.6 us: staged_body(): across = lax.ppermute(keep_across + got_across, 'col', [(1, 0), (2, 3)])]
    dot_general x2 -> x0, matrix products: 50.5 us -> none  [the longest x1 29.3 us: body(): jnp.einsum('acbd,pcd->pab', integral, weights, precision=lax.Precision.HI...]
    pallas_call x0 -> x4, Pallas kernels: none -> 26.9 us  [the longest x1 17.7 us: staged_body(): pl.pallas_call(early_kernel, out_shape=(blocks, blocks, jax.ShapeDtypeStr...]
    ppermute x0 -> x15, starting transfers between devices: none -> 19.8 us  [the longest x7 8.36 us: swap(): return lax.ppermute(array, axis, [(i, i ^ mask) for i in range(size)])]
    ppermute x0 -> x10, local copies, waits for them, and re-layouts: none -> 19.6 us  [the longest x4 8.3 us: swap(): return lax.ppermute(array, axis, [(i, i ^ mask) for i in range(size)])]
    dot_general x2 -> x0, local copies, waits for them, and re-layouts: 11.3 us -> none  [the longest x1 11 us: body(): lax.dot_general(panel_rows.reshape(n_fitting, count * width), b_matrix, (...]
    all_gather x1 -> x0, local copies, waits for them, and re-layouts: 10.4 us -> none  [body(): operand = lax.all_gather(factors, 'pair', axis=0, tiled=True)]
  transfers between devices with their start and end apart: 3 -> 15, of which waited for: 3 -> 3; matrix products, arithmetic and copies ran while one was open for 3% -> 19% of each run, Pallas kernels for 0% -> 18%
where the time goes in v1:
time: 138 us; the launch traced here: 137 us
  waiting for transfers between devices  51.4 us (37%)
  local copies, waits for them, and re-layouts  35.4 us (26%)
  Pallas kernels  26.9 us (19%)
  starting transfers between devices  19.8 us (14%)
  other arithmetic  3 us (2%)
    ppermute x1, waiting for transfers between devices, staged_body(): across = lax.ppermute(keep_across + got_across, 'col', [(1, 0), (2, 3)])  30.6 us
    ppermute x7, waiting for transfers between devices, swap(): return lax.ppermute(array, axis, [(i, i ^ mask) for i in range(size)])  20.8 us
    pallas_call x1, Pallas kernels, staged_body(): pl.pallas_call(early_kernel, out_shape=(blocks, blocks, jax.ShapeDtypeStr...  17.7 us
    unnamed x25, local copies, waits for them, and re-layouts  12.2 us
    ppermute x7, starting transfers between devices, swap(): return lax.ppermute(array, axis, [(i, i ^ mask) for i in range(size)])  8.36 us
    ppermute x4, local copies, waits for them, and re-layouts, swap(): return lax.ppermute(array, axis, [(i, i ^ mask) for i in range(size)])  8.3 us
    pallas_call x1, Pallas kernels, staged_body(): pl.pallas_call(late_kernel, out_shape=(block, block), in_specs=[anywhere]...  6.95 us
    ppermute x3, local copies, waits for them, and re-layouts, middle_swap(): return lax.ppermute(array, ('row', 'col'), pairs)  6.8 us
  transfers between devices with their start and end apart: 15, of which 3 were waited for; matrix products, arithmetic and copies ran while one was open for 19% of the time, Pallas kernels for 18%

profile of v1, /device:TPU:0, one launch (start us, length us, event | category | flops | bytes accessed | tf_op | source)
XLA Modules:
  0.0 136.7 jit_solution(10974452350760686697)
XLA Ops:
  0.0 1.5 %copy.49 = bf16[512,900]{0,1:T(8,128)(2,1)S(1)} copy(bf16[512,900]{1,0:T(8,128)(2,1)} %bitcast.11) | data formatting | bytes 1843200 | tf_op jit(solution)/shard_map/reshape | solution.py:217
  1.5 3.1 %collective-permute-start = (bf16[512,900]{0,1:T(8,128)(2,1)S(1)}, bf16[512,900]{0,1:T(8,128)(2,1)}, u32[]{:S(2)}, u32[]{:S(2)}) collective-permute-start(bf16[512,900]{0,1:T(8,128)(2,1)S(1)} %copy.49), channel_id=1, source_target_pairs={{0,2},{2,0},{4,6},{6,4},{1,3},{3,1},{5,7},{7,5},{8,10},{10,8},{12,... | collective-permute-start | bytes 2764808 | tf_op jit(solution)/shard_map/ppermute | solution.py:205
  4.6 1.5 %collective-permute-start.3 = (bf16[512,900]{0,1:T(8,128)(2,1)S(1)}, bf16[512,900]{0,1:T(8,128)(2,1)}, u32[]{:S(2)}, u32[]{:S(2)}) collective-permute-start(bf16[512,900]{0,1:T(8,128)(2,1)S(1)} %copy.49), channel_id=1, source_target_pairs={{0,16},{8,24},{16,0},{24,8},{1,17},{9,25},{17,1},{25,9},{2,18},{10... | collective-permute-start | bytes 2764808 | tf_op jit(solution)/shard_map/ppermute | solution.py:205
  6.1 1.6 %collective-permute-start.1 = (bf16[512,900]{0,1:T(8,128)(2,1)S(1)}, bf16[512,900]{0,1:T(8,128)(2,1)}, u32[]{:S(2)}, u32[]{:S(2)}) collective-permute-start(bf16[512,900]{0,1:T(8,128)(2,1)S(1)} %copy.49), channel_id=1, source_target_pairs={{2,4},{4,2},{3,5},{5,3},{10,12},{12,10},{11,13},{13,11},{18,20},{2... | collective-permute-start | bytes 2764808 | tf_op jit(solution)/shard_map/ppermute | solution.py:219
  7.7 17.5 %collective-permute-done = bf16[512,900]{0,1:T(8,128)(2,1)} collective-permute-done((bf16[512,900]{0,1:T(8,128)(2,1)S(1)}, bf16[512,900]{0,1:T(8,128)(2,1)}, u32[]{:S(2)}, u32[]{:S(2)}) %collective-permute-start) | collective-permute-done | bytes 921632 | tf_op jit(solution)/shard_map/ppermute | solution.py:205
  25.2 1.6 %collective-permute-start.11 = (bf16[512,900]{0,1:T(8,128)(2,1)}, bf16[512,900]{0,1:T(8,128)(2,1)}, u32[]{:S(2)}, u32[]{:S(2)}) collective-permute-start(bf16[512,900]{0,1:T(8,128)(2,1)} %collective-permute-done), channel_id=1, source_target_pairs={{2,18},{4,20},{10,26},{12,28},{18,2},{20,4},{26,10},{28,12},{3,19}... | collective-permute-start | bytes 2764808 | tf_op jit(solution)/shard_map/ppermute | solution.py:230
  26.8 1.7 %collective-permute-start.5 = (bf16[10,16,16]{2,1,0:T(8,128)(2,1)}, bf16[10,16,16]{2,1,0:T(8,128)(2,1)S(1)}, u32[]{:S(2)}, u32[]{:S(2)}) collective-permute-start(bf16[10,16,16]{2,1,0:T(8,128)(2,1)} %param.7), channel_id=1, source_target_pairs={{0,1},{1,0},{2,3},{3,2},{4,5},{5,4},{6,7},{7,6},{8,9},{9,8},{10,11... | collective-permute-start | bytes 15368 | tf_op jit(solution)/shard_map/ppermute | solution.py:205
  34.3 1.6 %collective-permute-start.7 = (bf16[512,900]{0,1:T(8,128)(2,1)}, bf16[512,900]{0,1:T(8,128)(2,1)}, u32[]{:S(2)}, u32[]{:S(2)}) collective-permute-start(bf16[512,900]{0,1:T(8,128)(2,1)} %collective-permute-done), channel_id=1, source_target_pairs={{2,4},{4,2},{3,5},{5,3},{10,12},{12,10},{11,13},{13,11},{18,20},{2... | collective-permute-start | bytes 2764808 | tf_op jit(solution)/shard_map/ppermute | solution.py:224
  36.0 1.6 %collective-permute-start.10 = (bf16[512,900]{0,1:T(8,128)(2,1)}, bf16[512,900]{0,1:T(8,128)(2,1)}, u32[]{:S(2)}, u32[]{:S(2)}) collective-permute-start(bf16[512,900]{0,1:T(8,128)(2,1)} %collective-permute-done), channel_id=1, source_target_pairs={{2,10},{4,12},{10,2},{12,4},{18,26},{20,28},{26,18},{28,20},{3,11}... | collective-permute-start | bytes 2764808 | tf_op jit(solution)/shard_map/ppermute | solution.py:230
  38.9 1.6 %collective-permute-start.12 = (bf16[512,900]{0,1:T(8,128)(2,1)}, bf16[512,900]{0,1:T(8,128)(2,1)}, u32[]{:S(2)}, u32[]{:S(2)}) collective-permute-start(bf16[512,900]{0,1:T(8,128)(2,1)} %collective-permute-done.11), channel_id=1, source_target_pairs={{2,10},{4,12},{10,2},{12,4},{18,26},{20,28},{26,18},{28,20},{3,11}... | collective-permute-start | bytes 2764808 | tf_op jit(solution)/shard_map/ppermute | solution.py:230
  42.0 1.6 %copy.56.middle = bf16[512,900]{1,0:T(8,128)(2,1)S(1)} copy(bf16[512,900]{0,1:T(8,128)(2,1)} %collective-permute-done.1) | data formatting | bytes 1843200 | tf_op jit(solution)/shard_map/ppermute | solution.py:219
  43.6 2.3 %copy.58.by_x = bf16[512,900]{1,0:T(8,128)(2,1)} copy(bf16[512,900]{0,1:T(8,128)(2,1)} %collective-permute-done.3) | data formatting | bytes 1843200 | tf_op jit(solution)/shard_map/ppermute | solution.py:205
  45.8 2.3 %copy.57.by_core = bf16[512,900]{1,0:T(8,128)(2,1)} copy(bf16[512,900]{0,1:T(8,128)(2,1)} %copy-done.11) | data formatting | bytes 1843200 | tf_op jit(solution)/shard_map/ppermute | solution.py:205
  48.1 2.2 %copy.59.by_both = bf16[512,900]{1,0:T(8,128)(2,1)} copy(bf16[512,900]{0,1:T(8,128)(2,1)} %collective-permute-done.4) | data formatting | bytes 1843200 | tf_op jit(solution)/shard_map/ppermute | solution.py:205
  54.1 17.7 %shard_map.64 = (f32[3,10,32,128]{3,2,1,0:T(8,128)S(1)}, f32[3,10,32,128]{3,2,1,0:T(8,128)}, bf16[16,4,32,900]{3,2,1,0:T(8,128)(2,1)S(1)}) custom-call(bf16[512,900]{1,0:T(8,128)(2,1)S(1)} %bitcast.12, bf16[512,900]{1,0:T(8,128)(2,1)S(1)} %copy.55.facing, bf16[512,900]{1,0:T(8,128)(2,1)S(1)} %copy.56.middle, bf16[512,900]{1,0:T(8,128)(2,1)S(1)} %copy-done.3, ...), custom_call_target="tpu_custom_call" | custom-call | flops 7549747200 | bytes 3686400 | tf_op jit(solution)/shard_map/pallas_call | solution.py:271
  72.6 2.0 %copy-done.9 = bf16[16,4,32,900]{3,2,1,0:T(8,128)(2,1)} copy-done((bf16[16,4,32,900]{3,2,1,0:T(8,128)(2,1)}, bf16[16,4,32,900]{3,2,1,0:T(8,128)(2,1)S(1)}, u32[]{:S(2)}) %copy-start.9) | copy-done | bytes 3686424
  74.9 2.3 %copy.65.by_x = bf16[512,900]{1,0:T(8,128)(2,1)} copy(bf16[512,900]{0,1:T(8,128)(2,1)} %collective-permute-done.11) | data formatting | bytes 1843200 | tf_op jit(solution)/shard_map/ppermute | solution.py:230
  80.2 2.3 %copy.64.by_core = bf16[512,900]{1,0:T(8,128)(2,1)} copy(bf16[512,900]{0,1:T(8,128)(2,1)} %collective-permute-done.10) | data formatting | bytes 1843200 | tf_op jit(solution)/shard_map/ppermute | solution.py:230
  82.4 2.3 %copy.66.by_both = bf16[512,900]{1,0:T(8,128)(2,1)} copy(bf16[512,900]{0,1:T(8,128)(2,1)} %collective-permute-done.12) | data formatting | bytes 1843200 | tf_op jit(solution)/shard_map/ppermute | solution.py:230
  90.6 7.0 %shard_map.65 = (f32[10,32,128]{2,1,0:T(8,128)S(1)}, f32[10,32,128]{2,1,0:T(8,128)S(1)}) custom-call(bf16[512,900]{1,0:T(8,128)(2,1)S(1)} %copy.60.far, bf16[512,900]{1,0:T(8,128)(2,1)S(1)} %copy.61.passed, bf16[16,4,32,900]{3,2,1,0:T(8,128)(2,1)S(1)} %copy-done.10, bf16[32,512]{1,0:T(8,128)(2,1)S(1)} %pad_maximum_fusion.weights), custom_call_target="tpu_custom_call" | custom-call | flops 1887436800 | bytes 3686400 | tf_op jit(solution)/shard_map/pallas_call | solution.py:308
  97.5 1.7 %collective-permute-start.9 = (f32[10,32,128]{2,1,0:T(8,128)S(1)}, f32[10,32,128]{2,1,0:T(8,128)S(1)}, u32[]{:S(2)}, u32[]{:S(2)}) collective-permute-start(f32[10,32,128]{2,1,0:T(8,128)S(1)} %get-tuple-element.16), channel_id=1, source_target_pairs={{0,1},{1,0},{2,3},{3,2},{4,5},{5,4},{6,7},{7,6},{8,9},{9,8},{10,11... | collective-permute-start | bytes 491528 | tf_op jit(solution)/shard_map/ppermute | solution.py:205
  100.7 3.2 %collective-permute-done.9.got_late = f32[10,32,128]{2,1,0:T(8,128)S(1)} collective-permute-done((f32[10,32,128]{2,1,0:T(8,128)S(1)}, f32[10,32,128]{2,1,0:T(8,128)S(1)}, u32[]{:S(2)}, u32[]{:S(2)}) %collective-permute-start.9) | collective-permute-done | bytes 163872 | tf_op jit(solution)/shard_map/ppermute | solution.py:205
  103.9 30.6 %collective-permute-done.14.across = f32[10,32,128]{2,1,0:T(8,128)S(1)} collective-permute-done((f32[10,32,128]{2,1,0:T(8,128)S(1)}, f32[10,32,128]{2,1,0:T(8,128)S(1)}, u32[]{:S(2)}, u32[]{:S(2)}) %collective-permute-start.14) | collective-permute-done | bytes 163872 | tf_op jit(solution)/shard_map/ppermute | solution.py:306
  134.5 2.2 %shard_map.67 = f32[10,128,128]{2,1,0:T(8,128)} custom-call(s32[10]{0:T(128)S(1)} %get-tuple-element.20.symmetry, s32[128,128]{1,0:T(8,128)S(1)} %broadcast_xor_fusion.pair_sym, f32[3,10,32,128]{3,2,1,0:T(8,128)S(1)} %copy-done.8, f32[3,10,32,128]{3,2,1,0:T(8,128)} %collective-permute-done.6.got_early, f32[10,32,128]{2,1,0:T(8,128)S(1)} %get-tuple-element.15.keep_late, ...), custom_call_target="tpu_custom_call" | custom-call | tf_op jit(solution)/shard_map/pallas_call | solution.py:325
  (62 shorter events, 23.6 us)
Async XLA Ops:
  1.5 23.7 %collective-permute-start = (bf16[512,900]{0,1:T(8,128)(2,1)S(1)}, bf16[512,900]{0,1:T(8,128)(2,1)}, u32[]{:S(2)}, u32[]{:S(2)}) collective-permute-start(bf16[512,900]{0,1:T(8,128)(2,1)S(1)} %copy.49), channel_id=1, source_target_pairs={{0,2},{2,0},{4,6},{6,4},{1,3},{3,1},{5,7},{7,5},{8,10},{10,8},{12,... | collective-permute-start | bytes 2764808 | tf_op jit(solution)/shard_map/ppermute | solution.py:205
  4.6 23.9 %collective-permute-start.3 = (bf16[512,900]{0,1:T(8,128)(2,1)S(1)}, bf16[512,900]{0,1:T(8,128)(2,1)}, u32[]{:S(2)}, u32[]{:S(2)}) collective-permute-start(bf16[512,900]{0,1:T(8,128)(2,1)S(1)} %copy.49), channel_id=1, source_target_pairs={{0,16},{8,24},{16,0},{24,8},{1,17},{9,25},{17,1},{25,9},{2,18},{10... | collective-permute-start | bytes 2764808 | tf_op jit(solution)/shard_map/ppermute | solution.py:205
  6.1 29.9 %collective-permute-start.1 = (bf16[512,900]{0,1:T(8,128)(2,1)S(1)}, bf16[512,900]{0,1:T(8,128)(2,1)}, u32[]{:S(2)}, u32[]{:S(2)}) collective-permute-start(bf16[512,900]{0,1:T(8,128)(2,1)S(1)} %copy.49), channel_id=1, source_target_pairs={{2,4},{4,2},{3,5},{5,3},{10,12},{12,10},{11,13},{13,11},{18,20},{2... | collective-permute-start | bytes 2764808 | tf_op jit(solution)/shard_map/ppermute | solution.py:219
  7.7 29.9 %collective-permute-start.2 = (bf16[512,900]{0,1:T(8,128)(2,1)S(1)}, bf16[512,900]{0,1:T(8,128)(2,1)S(1)}, u32[]{:S(2)}, u32[]{:S(2)}) collective-permute-start(bf16[512,900]{0,1:T(8,128)(2,1)S(1)} %copy.49), channel_id=1, source_target_pairs={{0,8},{8,0},{16,24},{24,16},{1,9},{9,1},{17,25},{25,17},{2,10},{10... | collective-permute-start | bytes 2764808 | tf_op jit(solution)/shard_map/ppermute | solution.py:205
  25.2 13.7 %collective-permute-start.11 = (bf16[512,900]{0,1:T(8,128)(2,1)}, bf16[512,900]{0,1:T(8,128)(2,1)}, u32[]{:S(2)}, u32[]{:S(2)}) collective-permute-start(bf16[512,900]{0,1:T(8,128)(2,1)} %collective-permute-done), channel_id=1, source_target_pairs={{2,18},{4,20},{10,26},{12,28},{18,2},{20,4},{26,10},{28,12},{3,19}... | collective-permute-start | bytes 2764808 | tf_op jit(solution)/shard_map/ppermute | solution.py:230
  26.8 6.2 %collective-permute-start.5 = (bf16[10,16,16]{2,1,0:T(8,128)(2,1)}, bf16[10,16,16]{2,1,0:T(8,128)(2,1)S(1)}, u32[]{:S(2)}, u32[]{:S(2)}) collective-permute-start(bf16[10,16,16]{2,1,0:T(8,128)(2,1)} %param.7), channel_id=1, source_target_pairs={{0,1},{1,0},{2,3},{3,2},{4,5},{5,4},{6,7},{7,6},{8,9},{9,8},{10,11... | collective-permute-start | bytes 15368 | tf_op jit(solution)/shard_map/ppermute | solution.py:205
  28.5 19.6 %collective-permute-start.4 = (bf16[512,900]{0,1:T(8,128)(2,1)}, bf16[512,900]{0,1:T(8,128)(2,1)}, u32[]{:S(2)}, u32[]{:S(2)}) collective-permute-start(bf16[512,900]{0,1:T(8,128)(2,1)} %collective-permute-done.3), channel_id=1, source_target_pairs={{0,8},{8,0},{16,24},{24,16},{1,9},{9,1},{17,25},{25,17},{2,10},{10... | collective-permute-start | bytes 2764808 | tf_op jit(solution)/shard_map/ppermute | solution.py:205
  34.3 42.9 %collective-permute-start.7 = (bf16[512,900]{0,1:T(8,128)(2,1)}, bf16[512,900]{0,1:T(8,128)(2,1)}, u32[]{:S(2)}, u32[]{:S(2)}) collective-permute-start(bf16[512,900]{0,1:T(8,128)(2,1)} %collective-permute-done), channel_id=1, source_target_pairs={{2,4},{4,2},{3,5},{5,3},{10,12},{12,10},{11,13},{13,11},{18,20},{2... | collective-permute-start | bytes 2764808 | tf_op jit(solution)/shard_map/ppermute | solution.py:224
  36.0 44.2 %collective-permute-start.10 = (bf16[512,900]{0,1:T(8,128)(2,1)}, bf16[512,900]{0,1:T(8,128)(2,1)}, u32[]{:S(2)}, u32[]{:S(2)}) collective-permute-start(bf16[512,900]{0,1:T(8,128)(2,1)} %collective-permute-done), channel_id=1, source_target_pairs={{2,10},{4,12},{10,2},{12,4},{18,26},{20,28},{26,18},{28,20},{3,11}... | collective-permute-start | bytes 2764808 | tf_op jit(solution)/shard_map/ppermute | solution.py:230
  37.6 2.9 %copy-start.11 = (bf16[512,900]{0,1:T(8,128)(2,1)}, bf16[512,900]{0,1:T(8,128)(2,1)S(1)}, u32[]{:S(2)}) copy-start(bf16[512,900]{0,1:T(8,128)(2,1)S(1)} %collective-permute-done.2) | copy-start | bytes 2764804
  37.6 41.1 %collective-permute-start.8 = (bf16[512,900]{0,1:T(8,128)(2,1)}, bf16[512,900]{0,1:T(8,128)(2,1)}, u32[]{:S(2)}, u32[]{:S(2)}) collective-permute-start(bf16[512,900]{0,1:T(8,128)(2,1)} %collective-permute-done.1), channel_id=1, source_target_pairs={{2,0},{4,6},{3,1},{5,7},{10,8},{12,14},{11,9},{13,15},{18,16},{20,... | collective-permute-start | bytes 2764808 | tf_op jit(solution)/shard_map/ppermute | solution.py:225
  38.9 43.6 %collective-permute-start.12 = (bf16[512,900]{0,1:T(8,128)(2,1)}, bf16[512,900]{0,1:T(8,128)(2,1)}, u32[]{:S(2)}, u32[]{:S(2)}) collective-permute-start(bf16[512,900]{0,1:T(8,128)(2,1)} %collective-permute-done.11), channel_id=1, source_target_pairs={{2,10},{4,12},{10,2},{12,4},{18,26},{20,28},{26,18},{28,20},{3,11}... | collective-permute-start | bytes 2764808 | tf_op jit(solution)/shard_map/ppermute | solution.py:230
  42.0 8.4 %copy-start = (bf16[900,32,16]{0,2,1:T(8,128)(2,1)S(1)}, bf16[900,32,16]{0,2,1:T(8,128)(2,1)}, u32[]{:S(2)}) copy-start(bf16[900,32,16]{0,2,1:T(8,128)(2,1)} %param.6) | copy-start | bytes 2764804
  50.4 1.2 copy-start.2
  52.8 1.2 copy-start.5
  72.6 2.0 %copy-start.9 = (bf16[16,4,32,900]{3,2,1,0:T(8,128)(2,1)}, bf16[16,4,32,900]{3,2,1,0:T(8,128)(2,1)S(1)}, u32[]{:S(2)}) copy-start(bf16[16,4,32,900]{3,2,1,0:T(8,128)(2,1)S(1)} %get-tuple-element.14.panel_in) | copy-start | bytes 11059204
  74.6 29.3 %collective-permute-start.6 = (f32[3,10,32,128]{3,2,1,0:T(8,128)}, f32[3,10,32,128]{3,2,1,0:T(8,128)}, u32[]{:S(2)}, u32[]{:S(2)}) collective-permute-start(f32[3,10,32,128]{3,2,1,0:T(8,128)} %get-tuple-element.13), channel_id=1, source_target_pairs={{0,1},{1,0},{2,3},{3,2},{4,5},{5,4},{6,7},{7,6},{8,9},{9,8},{10,11... | collective-permute-start | bytes 1474568 | tf_op jit(solution)/shard_map/ppermute | solution.py:205
  84.7 1.2 copy-start.1
  85.9 1.2 copy-start.4
  88.4 2.2 %copy-start.10 = (bf16[16,4,32,900]{3,2,1,0:T(8,128)(2,1)S(1)}, bf16[16,4,32,900]{3,2,1,0:T(8,128)(2,1)}, u32[]{:S(2)}) copy-start(bf16[16,4,32,900]{3,2,1,0:T(8,128)(2,1)} %copy-done.9) | copy-start | bytes 11059204
  88.4 46.1 %copy-start.8 = (f32[3,10,32,128]{3,2,1,0:T(8,128)S(1)}, f32[3,10,32,128]{3,2,1,0:T(8,128)}, u32[]{:S(2)}) copy-start(f32[3,10,32,128]{3,2,1,0:T(8,128)} %copy-done.7) | copy-start | bytes 1474564
  88.4 10.8 %collective-permute-start.13 = (f32[10,32,128]{2,1,0:T(8,128)S(1)}, f32[10,32,128]{2,1,0:T(8,128)S(1)}, u32[]{:S(2)}, u32[]{:S(2)}) collective-permute-start(f32[10,32,128]{2,1,0:T(8,128)S(1)} %get-tuple-element.18), channel_id=1, source_target_pairs={{2,3},{3,2},{4,5},{5,4},{10,11},{11,10},{12,13},{13,12},{18,19},{1... | collective-permute-start | bytes 491528 | tf_op jit(solution)/shard_map/ppermute | solution.py:305
  97.5 6.4 %collective-permute-start.9 = (f32[10,32,128]{2,1,0:T(8,128)S(1)}, f32[10,32,128]{2,1,0:T(8,128)S(1)}, u32[]{:S(2)}, u32[]{:S(2)}) collective-permute-start(f32[10,32,128]{2,1,0:T(8,128)S(1)} %get-tuple-element.16), channel_id=1, source_target_pairs={{0,1},{1,0},{2,3},{3,2},{4,5},{5,4},{6,7},{7,6},{8,9},{9,8},{10,11... | collective-permute-start | bytes 491528 | tf_op jit(solution)/shard_map/ppermute | solution.py:205
  99.3 35.2 %collective-permute-start.14 = (f32[10,32,128]{2,1,0:T(8,128)S(1)}, f32[10,32,128]{2,1,0:T(8,128)S(1)}, u32[]{:S(2)}, u32[]{:S(2)}) collective-permute-start(f32[10,32,128]{2,1,0:T(8,128)S(1)} %add.23), channel_id=1, source_target_pairs={{2,0},{4,6},{3,1},{5,7},{10,8},{12,14},{11,9},{13,15},{18,16},{20,... | collective-permute-start | bytes 491528 | tf_op jit(solution)/shard_map/ppermute | solution.py:306
  (3 other events, 3.2 us)

commit v2 on v1

v2 whole, which is shorter than its diff:
```python
import jax
import jax.numpy as jnp
from jax import lax
from jax.experimental import pallas as pl
from jax.experimental.pallas import tpu as pltpu
from jax.sharding import PartitionSpec as P

VMEM_LIMIT = 24 * 1024 * 1024
LANES = 128
NT = (((1,), (1,)), ((), ()))
NN = (((1,), (0,)), ((), ()))
TN = (((0,), (0,)), ((), ()))


def lookup_symmetry(occ_irreps, pair_list):
    labels = jnp.arange(occ_irreps.shape[0], dtype=jnp.int32)
    onehot = pair_list[:, :, None] == labels[None, None, :]
    picked = jnp.sum(jnp.where(onehot, occ_irreps[None, None, :], 0), axis=-1)
    return jnp.bitwise_xor(picked[:, 0], picked[:, 1])


def mask_amplitudes(amplitudes, win_irreps, symmetry):
    product = jnp.bitwise_xor(win_irreps[:, None], win_irreps[None, :])
    allowed = product[None, :, :] == symmetry[:, None, None]
    return jnp.where(allowed, amplitudes, jnp.zeros_like(amplitudes))


def gathered_body(factors, amplitudes, virt_irreps, win_irreps, occ_irreps, pair_list):
    per_device = factors.shape[1]
    n_rows = lax.axis_size("row")
    n_cols = lax.axis_size("col")
    block_a = per_device * n_cols
    slab = amplitudes.shape[0]
    symmetry = lookup_symmetry(occ_irreps, pair_list)
    own_symmetry = lax.dynamic_slice_in_dim(symmetry, lax.axis_index("pair") * slab, slab)
    every = lax.all_gather(amplitudes, "pair", axis=0, tiled=True)
    weights = mask_amplitudes(every, win_irreps, symmetry).astype(jnp.float32)
    n_fitting, _, width = factors.shape
    b_rows = lax.all_gather(factors, "row", axis=1, tiled=True)
    a_rows = lax.all_gather(factors, "col", axis=1, tiled=True)
    integral = lax.dot_general(
        a_rows.reshape(n_fitting, block_a * width),
        b_rows.reshape(n_fitting, n_rows * per_device * width),
        (((0,), (0,)), ((), ())),
        preferred_element_type=jnp.float32,
    )
    integral = integral.reshape(block_a, width, n_rows * per_device, width)
    part = jnp.einsum("acbd,pcd->pab", integral, weights, precision=lax.Precision.HIGHEST)
    full = lax.psum_scatter(part, "pair", scatter_dimension=0, tiled=True)
    full = full.reshape(slab, block_a, n_rows, per_device)
    a_labels = lax.dynamic_slice_in_dim(virt_irreps, lax.axis_index("row") * block_a, block_a)
    b_labels = lax.dynamic_slice_in_dim(
        virt_irreps.reshape(n_rows, -1), lax.axis_index("col") * per_device, per_device, 1
    )
    pair_sym = jnp.bitwise_xor(a_labels[:, None, None], b_labels[None, :, :])
    allowed = pair_sym[None, :, :, :] == own_symmetry[:, None, None, None]
    return jnp.where(allowed, full, 0.0)


def is_middle():
    col = lax.axis_index("col")
    return jnp.logical_or(col == 1, col == 2)


def one_hot(shape, wanted):
    first = lax.broadcasted_iota(jnp.int32, shape, 0)
    second = lax.broadcasted_iota(jnp.int32, shape, 1)
    return wanted(first, second).astype(jnp.bfloat16)


def multiply(left, right, dims):
    return lax.dot_general(left, right, dims, preferred_element_type=jnp.float32)


def pack_kernel(rest, own, out):
    n, n_fit = own.shape
    whole = n_fit - rest
    out[:n, :] = own[:, :whole]
    below = out.shape[0] - n
    turned = jnp.zeros((below, LANES), jnp.float32)
    for j in range(n // LANES):
        pick = one_hot((below, rest), lambda r, q: r == j * rest + q)
        turned = turned + multiply(pick, own[j * LANES : (j + 1) * LANES, whole:], NT)
    out[n:, :] = jnp.zeros((below, whole), jnp.bfloat16)
    out[n:, :LANES] = turned.astype(jnp.bfloat16)


def fetch(packed, rows, tail, sems):
    n, depth = rows.shape
    whole = depth - LANES
    copies = (
        pltpu.make_async_copy(packed.at[pl.ds(0, n)], rows.at[:, pl.ds(0, whole)], sems.at[0]),
        pltpu.make_async_copy(packed.at[pl.ds(n, tail.shape[0]), pl.ds(0, LANES)], tail, sems.at[1]),
    )
    for copy in copies:
        copy.start()
    return copies


def unpack(copies, rows, tail, rest):
    for copy in copies:
        copy.wait()
    n, depth = rows.shape
    for j in range(n // LANES):
        pick = one_hot(tail.shape, lambda r, q: jnp.logical_and(r == j * rest + q, q < rest))
        back = multiply(tail[...], pick, TN).astype(jnp.bfloat16)
        rows[j * LANES : (j + 1) * LANES, depth - LANES :] = back


def window_major(width, per_device):
    n = width * per_device
    return one_hot((n, n), lambda i, j: lax.rem(i, per_device) * width + lax.div(i, per_device) == j)


def place_rows(panel, order, rows, k):
    width, _, per_device, depth = panel.shape
    moved = multiply(order, rows[...], NN).astype(panel.dtype)
    panel[:, pl.ds(k, 1)] = moved.reshape(width, 1, per_device, depth)


def contract_block(rows, panel, weights, split, sums, keep, send):
    width, n_rows, per_device, depth = panel.shape
    n_b = n_rows * per_device
    n_a = rows.shape[0] // width
    half = keep.shape[0]
    n_p = weights.shape[0]

    def integrals(step, carry):
        two = panel[pl.ds(2 * step, 2)].reshape(2 * n_b, depth)
        acc = multiply(rows[...], two, NT)
        high = acc.astype(jnp.bfloat16)
        low = (acc - high.astype(jnp.float32)).astype(jnp.bfloat16)
        for j in range(2):
            lanes = slice(j * n_b, (j + 1) * n_b)
            split[:, 0, pl.ds(2 * step + j, 1)] = high[:, lanes].reshape(n_a, 1, width, n_b)
            split[:, 1, pl.ds(2 * step + j, 1)] = low[:, lanes].reshape(n_a, 1, width, n_b)
        return carry

    lax.fori_loop(0, width // 2, integrals, 0, unroll=True)

    def ladder(step, carry):
        two = [split[2 * step + j].reshape(2 * width * width, n_b) for j in range(2)]
        res = multiply(weights[...], jnp.concatenate(two, axis=1), NN)
        for j in range(2):
            sums[pl.ds((2 * step + j) * n_p, n_p), :] = res[:, j * n_b : (j + 1) * n_b]
        return carry

    lax.fori_loop(0, n_a // 2, ladder, 0, unroll=True)
    for p in range(half):
        keep[p] = sums[pl.ds(p, n_a, stride=n_p), :]
        send[p] = sums[pl.ds(n_p // 2 + p, n_a, stride=n_p), :]


def pair_symmetry(occ, pairs, p):
    return jnp.bitwise_xor(occ[pairs[0, p]], occ[pairs[1, p]])


def weight_rows(amplitudes, win, occ, pairs, first, n_p):
    n, width = amplitudes.shape
    slab = n // width
    lanes = width * width
    spread = multiply(amplitudes[...], one_hot((width, lanes), lambda d, l: d == lax.div(l, width)), NN)
    c_of_row = lax.rem(lax.broadcasted_iota(jnp.int32, (n, lanes), 0), width)
    c_of_lane = lax.rem(lax.broadcasted_iota(jnp.int32, (n, lanes), 1), width)
    spread = jnp.where(c_of_row == c_of_lane, spread, 0.0).astype(jnp.bfloat16)
    gathered = multiply(one_hot((n_p, n), lambda p, r: p == lax.div(r, width)), spread, NN)
    lane = lax.broadcasted_iota(jnp.int32, (n_p, lanes), 1)
    row = lax.broadcasted_iota(jnp.int32, (n_p, lanes), 0)
    product = jnp.zeros((n_p, lanes), jnp.int32)
    for w in range(width):
        label = win[w]
        product = jnp.bitwise_xor(product, jnp.where(lax.div(lane, width) == w, label, 0))
        product = jnp.bitwise_xor(product, jnp.where(lax.rem(lane, width) == w, label, 0))
    wanted = jnp.full((n_p, lanes), -1, jnp.int32)
    for p in range(slab):
        wanted = jnp.where(row == p, pair_symmetry(occ, pairs, first + p), wanted)
    masked = jnp.where(product == wanted, gathered, 0.0).astype(jnp.bfloat16)
    return jnp.concatenate([masked, masked], axis=1)


def early_kernel(
    rest, own, by_core, by_x, by_both, facing, turned, mine, others, win, occ, pairs,
    keep, send, panel_out, weights, panel, held, tails, split, sums, sems, panel_sem,
):
    middle = is_middle()
    row = lax.axis_index("row")
    width, _, per_device, _ = panel.shape
    sources = (own, by_core, None, by_both, facing, turned)
    copies = [
        None if src is None else fetch(src, held.at[i], tails.at[i], sems.at[i]) for i, src in enumerate(sources)
    ]

    @pl.when(middle)
    def _():
        fetch(by_x, held.at[2], tails.at[2], sems.at[2])

    @pl.when(jnp.logical_not(middle))
    def _():
        fetch(turned, held.at[2], tails.at[2], sems.at[2])

    copies[2] = wait_only(by_x, held.at[2], tails.at[2], sems.at[2])
    slab = mine.shape[0] // width
    n_p = weights.shape[0] // 2
    pair = lax.axis_index("pair")
    weights[:n_p] = weight_rows(mine, win, occ, pairs, pair * slab, n_p)
    weights[n_p:] = weight_rows(others, win, occ, pairs, (1 - pair) * slab, n_p)
    order = window_major(width, per_device)
    for i in range(4):
        unpack(copies[i], held.at[i], tails.at[i], rest)
        place_rows(panel, order, held.at[i], jnp.bitwise_xor(row, i))
    back = pltpu.make_async_copy(panel, panel_out, panel_sem)
    back.start()
    for i in (4, 5):
        unpack(copies[i], held.at[i], tails.at[i], rest)

    def block(s, carry):
        contract_block(held.at[jnp.where(s == 0, 0, 3 + s)], panel, weights, split, sums, keep.at[s], send.at[s])
        return carry

    lax.fori_loop(0, jnp.where(middle, 3, 2), block, 0)
    back.wait()


def wait_only(packed, rows, tail, sems):
    n, depth = rows.shape
    return (
        pltpu.make_async_copy(packed.at[pl.ds(0, n)], rows.at[:, pl.ds(0, depth - LANES)], sems.at[0]),
        pltpu.make_async_copy(packed.at[pl.ds(n, tail.shape[0]), pl.ds(0, LANES)], tail, sems.at[1]),
    )


def across_kernel(
    rest, far, facing, by_core, by_x, by_both, weights, keep, send, panel, held, tails, split, sums, sems
):
    @pl.when(is_middle())
    def _():
        sources = (facing, by_core, by_x, by_both, far)
        copies = [fetch(src, held.at[i], tails.at[i], sems.at[i]) for i, src in enumerate(sources)]
        row = lax.axis_index("row")
        width, _, per_device, _ = panel.shape
        order = window_major(width, per_device)
        for i in range(4):
            unpack(copies[i], held.at[i], tails.at[i], rest)
            place_rows(panel, order, held.at[i], jnp.bitwise_xor(row, i))
        unpack(copies[4], held.at[4], tails.at[4], rest)
        contract_block(held.at[4], panel, weights, split, sums, keep, send)


def late_kernel(rest, far, passed, panel_in, weights, keep, send, panel, held, tail, split, sums, sems, panel_sem):
    copy_panel = pltpu.make_async_copy(panel_in, panel, panel_sem)
    copy_panel.start()
    middle = is_middle()

    @pl.when(middle)
    def _():
        fetch(far, held, tail, sems)

    @pl.when(jnp.logical_not(middle))
    def _():
        fetch(passed, held, tail, sems)

    unpack(wait_only(far, held, tail, sems), held, tail, rest)
    copy_panel.wait()
    contract_block(held, panel, weights, split, sums, keep, send)


def finish_kernel(
    virt, occ, pairs, keep_early, got_early, keep_late, got_late, across, across_other, out, whole
):
    row = lax.axis_index("row")
    col = lax.axis_index("col")
    middle = is_middle()
    lower = col < 2
    n_p, n_a, n_b = keep_late.shape
    planes = (col, jnp.bitwise_xor(col, 1), jnp.where(lower, 2, 1), jnp.where(lower, 3, 0))

    def place(s):
        return pl.ds(pl.multiple_of(planes[s] * n_a, n_a), n_a)

    for s in range(2):
        whole[:, place(s), :] = keep_early[s] + got_early[s]

    @pl.when(middle)
    def _():
        whole[:, place(2), :] = keep_early[2] + got_early[2]
        whole[:, place(3), :] = keep_late[...] + got_late[...]

    @pl.when(jnp.logical_not(middle))
    def _():
        whole[:, place(2), :] = keep_late[...] + got_late[...]
        whole[:, place(3), :] = across[...] + across_other[...]

    n_rows, block_a = virt.shape
    spread = [jnp.broadcast_to(virt[k : k + 1, :], (n_a, block_a)) for k in range(n_rows)]
    lane = lax.broadcasted_iota(jnp.int32, (n_b, block_a), 1)
    place_b = lax.rem(lax.broadcasted_iota(jnp.int32, (n_b, block_a), 0), n_a) + col * n_a
    b_labels = jnp.sum(jnp.where(lane == place_b, jnp.concatenate(spread, axis=0), 0), axis=1, keepdims=True)
    pair_sym = jnp.bitwise_xor(b_labels, virt[pl.ds(row, 1), :])
    first = lax.axis_index("pair") * n_p
    for p in range(n_p):
        out[p] = jnp.where(pair_sym == pair_symmetry(occ, pairs, first + p), whole[p].T, 0.0)


def swap(array, axis, mask):
    size = lax.axis_size(axis)
    return lax.ppermute(array, axis, [(i, i ^ mask) for i in range(size)])


def staged_body(factors, amplitudes, virt_irreps, win_irreps, occ_irreps, pair_list):
    n_fit, per_device, width = factors.shape
    n_rows = lax.axis_size("row")
    n_cols = lax.axis_size("col")
    n_pair = lax.axis_size("pair")
    n_b = n_rows * per_device
    block_a = per_device * n_cols
    slab = amplitudes.shape[0]
    n = per_device * width
    rest = n_fit % LANES
    below = 16 * pl.cdiv(rest * (n // LANES), 16)
    depth = n_fit - rest + LANES

    anywhere = pl.BlockSpec(memory_space=pl.ANY)
    vmem = pl.BlockSpec(memory_space=pltpu.VMEM)
    smem = pl.BlockSpec(memory_space=pltpu.SMEM)
    params = pltpu.CompilerParams(vmem_limit_bytes=VMEM_LIMIT)

    own = pl.pallas_call(
        lambda *refs: pack_kernel(rest, *refs),
        out_shape=jax.ShapeDtypeStruct((n + below, n_fit - rest), jnp.bfloat16),
        in_specs=[vmem],
        out_specs=vmem,
        compiler_params=params,
        name="pack",
    )(jnp.transpose(factors, (1, 2, 0)).reshape(n, n_fit))

    def at(r, c):
        return r * n_cols + c

    facing = swap(own, "col", 1)
    turned = lax.ppermute(
        own,
        ("row", "col"),
        [(at(r, c), at(r, 3 - c) if c in (1, 2) else at(r ^ 2, c)) for r in range(n_rows) for c in range(n_cols)],
    )
    by_x = lax.ppermute(own, ("row", "col"), [(at(r, c), at(r ^ 2, c)) for r in range(n_rows) for c in (1, 2)])
    by_core = swap(own, "row", 1)
    other_amplitudes = swap(amplitudes, "pair", 1)

    far = lax.ppermute(facing, "col", [(1, 2), (2, 1)])
    passed = swap(turned, "col", 1)
    x_rows = jnp.where(is_middle(), by_x, turned)
    by_both = swap(x_rows, "row", 1)

    def middle_core_swap(array):
        return lax.ppermute(array, ("row", "col"), [(at(r, c), at(r ^ 1, c)) for r in range(n_rows) for c in (1, 2)])

    facing_core = middle_core_swap(facing)
    passed_core = middle_core_swap(passed)

    block = jax.ShapeDtypeStruct((slab, per_device, n_b), jnp.float32)
    blocks = jax.ShapeDtypeStruct((3, slab, per_device, n_b), jnp.float32)
    panel_shape = (width, n_rows, per_device, depth)
    panel_scratch = pltpu.VMEM(panel_shape, jnp.bfloat16)
    split_scratch = pltpu.VMEM((per_device, 2, width, width, n_b), jnp.bfloat16)
    n_p = 16 * pl.cdiv(slab, 16)
    sums_scratch = pltpu.VMEM((per_device * 2 * n_p, n_b), jnp.float32)
    pairs = jnp.transpose(pair_list)

    def held(*count):
        return [pltpu.VMEM(count + (n, depth), jnp.bfloat16), pltpu.VMEM(count + (below, LANES), jnp.bfloat16)]

    def cost(n_blocks):
        flops = 2 * n_blocks * n * n_b * width * depth
        return pl.CostEstimate(flops=flops, bytes_accessed=8 * n * depth, transcendentals=0)

    keep_early, send_early, panel, weights = pl.pallas_call(
        lambda *refs: early_kernel(rest, *refs),
        out_shape=(
            blocks,
            blocks,
            jax.ShapeDtypeStruct(panel_shape, jnp.bfloat16),
            jax.ShapeDtypeStruct((2 * n_p, 2 * width * width), jnp.bfloat16),
        ),
        in_specs=[anywhere] * 6 + [vmem] * 2 + [smem] * 3,
        out_specs=(vmem, vmem, anywhere, vmem),
        scratch_shapes=[
            panel_scratch,
            *held(6),
            split_scratch,
            sums_scratch,
            pltpu.SemaphoreType.DMA((6, 2)),
            pltpu.SemaphoreType.DMA,
        ],
        compiler_params=params,
        cost_estimate=cost(3),
        name="early",
    )(
        own, by_core, by_x, by_both, facing, turned,
        amplitudes.reshape(slab * width, width), other_amplitudes.reshape(slab * width, width),
        win_irreps, occ_irreps, pairs,
    )
    got_early = swap(send_early, "pair", 1)

    keep_across, send_across = pl.pallas_call(
        lambda *refs: across_kernel(rest, *refs),
        out_shape=(block, block),
        in_specs=[anywhere] * 5 + [vmem],
        out_specs=(vmem, vmem),
        scratch_shapes=[panel_scratch, *held(5), split_scratch, sums_scratch, pltpu.SemaphoreType.DMA((5, 2))],
        compiler_params=params,
        cost_estimate=cost(1),
        name="across",
    )(far, facing, facing_core, passed, passed_core, weights)
    outwards = [(c, y, 0 if c == 1 else 3) for c in (1, 2) for y in range(n_pair)]
    across = lax.ppermute(keep_across, "col", [(1, 0), (2, 3)])
    across_other = lax.ppermute(
        send_across, ("col", "pair"), [(c * n_pair + y, to * n_pair + (y ^ 1)) for c, y, to in outwards]
    )

    keep_late, send_late = pl.pallas_call(
        lambda *refs: late_kernel(rest, *refs),
        out_shape=(block, block),
        in_specs=[anywhere] * 3 + [vmem],
        out_specs=(vmem, vmem),
        scratch_shapes=[
            panel_scratch,
            *held(),
            split_scratch,
            sums_scratch,
            pltpu.SemaphoreType.DMA((2,)),
            pltpu.SemaphoreType.DMA,
        ],
        compiler_params=params,
        cost_estimate=cost(1),
        name="late",
    )(far, passed, panel, weights)
    got_late = swap(send_late, "pair", 1)

    out = pl.pallas_call(
        finish_kernel,
        out_shape=jax.ShapeDtypeStruct((slab, n_b, block_a), jnp.float32),
        in_specs=[vmem] + [smem] * 2 + [vmem] * 6,
        out_specs=vmem,
        scratch_shapes=[pltpu.VMEM((slab, block_a, n_b), jnp.float32)],
        compiler_params=params,
        name="finish",
    )(
        virt_irreps.reshape(n_rows, block_a), occ_irreps, pairs,
        keep_early, got_early, keep_late, got_late, across, across_other,
    )
    return jnp.transpose(out.reshape(slab, n_rows, per_device, block_a), (0, 3, 1, 2))


def solution(mesh):
    staged = (mesh.shape["row"], mesh.shape["col"], mesh.shape["pair"]) == (4, 4, 2)
    body = staged_body if staged else gathered_body
    in_specs = (P("pair", ("row", "col"), None), P("pair", None, None), P(), P(), P(), P())
    out_specs = P("pair", "row", None, "col")
    return jax.shard_map(body, mesh=mesh, in_specs=in_specs, out_specs=out_specs, check_vma=False)
```

time: 138 us -> 94.5 us (0.68)
  local copies, waits for them, and re-layouts: 35.4 us -> 1.27 us
  Pallas kernels: 26.9 us -> 17.6 us
  waiting for transfers between devices: 51.4 us -> 56.5 us
  other arithmetic: 3 us -> 0.16 us
  starting transfers between devices: 19.8 us -> 18.4 us
    ppermute x10 -> x0, local copies, waits for them, and re-layouts: 19.6 us -> none  [the longest x4 8.3 us: swap(): return lax.ppermute(array, axis, [(i, i ^ mask) for i in range(size)])]
    unnamed x25 -> x12, local copies, waits for them, and re-layouts: 12.2 us -> 1.27 us
    pallas_call x3 -> x4, Pallas kernels: 24.7 us -> 15.9 us  [the longest x1 11.9 us: staged_body(): pl.pallas_call(lambda *refs: early_kernel(rest, *refs), out_shape=(blocks...]
    ppermute x7, waiting for transfers between devices: 20.8 us -> 26.5 us  [swap(): return lax.ppermute(array, axis, [(i, i ^ mask) for i in range(size)])]
    ppermute x7 -> x6, starting transfers between devices: 9.81 us -> 7.65 us  [the longest x1 2.94 us: staged_body(): lax.ppermute(own, ('row', 'col'), [(at(r, c), at(r, 3 - c) if c in (1, 2)...]
    reshape x3 -> x0, local copies, waits for them, and re-layouts: 1.7 us -> none  [the longest x1 1.47 us: staged_body(): own = jnp.transpose(factors, (1, 2, 0)).reshape(rows_shape)]
    ppermute x7, starting transfers between devices: 8.36 us -> 10 us  [swap(): return lax.ppermute(array, axis, [(i, i ^ mask) for i in range(size)])]
    dynamic_slice x3 -> x0, local copies, waits for them, and re-layouts: 1.63 us -> none  [the longest x1 0.76 us: staged_body(): lax.dynamic_slice_in_dim(virt_irreps.reshape(n_rows, -1), lax.axis_index(...]
  transfers between devices with their start and end apart: 15 -> 14, of which waited for: 3 -> 7; matrix products, arithmetic and copies ran while one was open for 19% -> 0% of each run, Pallas kernels for 18% -> 17%
where the time goes in v2:
time: 94.5 us; the launch traced here: 94.2 us
  waiting for transfers between devices  56.5 us (60%)
  starting transfers between devices  18.4 us (19%)
  Pallas kernels  17.6 us (19%)
  local copies, waits for them, and re-layouts  1.27 us (1%)
    ppermute x7, waiting for transfers between devices, swap(): return lax.ppermute(array, axis, [(i, i ^ mask) for i in range(size)])  26.5 us
    ppermute x1, waiting for transfers between devices, staged_body(): lax.ppermute(own, ('row', 'col'), [(at(r, c), at(r, 3 - c) if c in (1, 2)...  15.8 us
    pallas_call x1, Pallas kernels, staged_body(): pl.pallas_call(lambda *refs: early_kernel(rest, *refs), out_shape=(blocks...  11.9 us
    ppermute x1, waiting for transfers between devices, staged_body(): across = lax.ppermute(keep_across, 'col', [(1, 0), (2, 3)])  10.5 us
    ppermute x7, starting transfers between devices, swap(): return lax.ppermute(array, axis, [(i, i ^ mask) for i in range(size)])  10 us
    ppermute x1, waiting for transfers between devices, staged_body(): lax.ppermute(send_across, ('col', 'pair'), [(c * n_pair + y, to * n_pair...  3.76 us
    pallas_call x1, Pallas kernels, staged_body(): pl.pallas_call(lambda *refs: late_kernel(rest, *refs), out_shape=(block,...  3.74 us
    ppermute x1, starting transfers between devices, staged_body(): lax.ppermute(own, ('row', 'col'), [(at(r, c), at(r, 3 - c) if c in (1, 2)...  2.94 us
  transfers between devices with their start and end apart: 14, of which 7 were waited for; matrix products, arithmetic and copies ran while one was open for 0% of the time, Pallas kernels for 17%

profile of v2, /device:TPU:0, one launch (start us, length us, event | category | flops | bytes accessed | tf_op | source)
XLA Modules:
  0.0 94.2 jit_solution(10507116410085387937)
XLA Ops:
  0.0 1.2 %copy-done = bf16[900,32,16]{0,2,1:T(8,128)(2,1)S(1)} copy-done((bf16[900,32,16]{0,2,1:T(8,128)(2,1)S(1)}, bf16[900,32,16]{0,2,1:T(8,128)(2,1)}, u32[]{:S(2)}) %copy-start) | copy-done | bytes 921624
  1.3 0.2 pack.1.refs_0_
  1.4 2.9 %collective-permute-start.2 = (bf16[528,896]{1,0:T(8,128)(2,1)S(1)}, bf16[528,896]{1,0:T(8,128)(2,1)S(1)}, u32[]{:S(2)}, u32[]{:S(2)}) collective-permute-start(bf16[528,896]{1,0:T(8,128)(2,1)S(1)} %pack.1.refs_0_), channel_id=1, source_target_pairs={{0,16},{2,4},{4,2},{6,22},{8,24},{10,12},{12,10},{14,30},{16,0},{1... | collective-permute-start | bytes 2838536 | tf_op jit(solution)/shard_map/ppermute | solution.py:340
  4.4 0.7 collective-permute-start.1
  5.1 4.4 %collective-permute-start.4 = (bf16[528,896]{1,0:T(8,128)(2,1)S(1)}, bf16[528,896]{1,0:T(8,128)(2,1)}, u32[]{:S(2)}, u32[]{:S(2)}) collective-permute-start(bf16[528,896]{1,0:T(8,128)(2,1)S(1)} %pack.1.refs_0_), channel_id=1, source_target_pairs={{0,2},{2,0},{4,6},{6,4},{1,3},{3,1},{5,7},{7,5},{8,10},{10,8},{12,... | collective-permute-start | bytes 2838536 | tf_op jit(solution)/shard_map/ppermute | solution.py:306
  9.5 15.8 %collective-permute-done.2.refs_5_ = bf16[528,896]{1,0:T(8,128)(2,1)S(1)} collective-permute-done((bf16[528,896]{1,0:T(8,128)(2,1)S(1)}, bf16[528,896]{1,0:T(8,128)(2,1)S(1)}, u32[]{:S(2)}, u32[]{:S(2)}) %collective-permute-start.2) | collective-permute-done | bytes 946208 | tf_op jit(solution)/shard_map/ppermute | solution.py:340
  25.4 1.8 %collective-permute-start.8 = (bf16[528,896]{1,0:T(8,128)(2,1)S(1)}, bf16[528,896]{1,0:T(8,128)(2,1)S(1)}, u32[]{:S(2)}, u32[]{:S(2)}) collective-permute-start(bf16[528,896]{1,0:T(8,128)(2,1)S(1)} %collective-permute-done.2.refs_5_), channel_id=1, source_target_pairs={{0,2},{2,0},{4,6},{6,4},{1,3},{3,1},{5,7},{7,5},{8,10},{10,8},{12,... | collective-permute-start | bytes 2838536 | tf_op jit(solution)/shard_map/ppermute | solution.py:306
  27.4 4.1 %collective-permute-done.4.refs_4_.refs_1_ = bf16[528,896]{1,0:T(8,128)(2,1)} collective-permute-done((bf16[528,896]{1,0:T(8,128)(2,1)S(1)}, bf16[528,896]{1,0:T(8,128)(2,1)}, u32[]{:S(2)}, u32[]{:S(2)}) %collective-permute-start.4) | collective-permute-done | bytes 946208 | tf_op jit(solution)/shard_map/ppermute | solution.py:306
  31.5 0.7 collective-permute-start.7
  32.2 1.6 %collective-permute-start.5 = (bf16[10,16,16]{2,1,0:T(8,128)(2,1)S(1)}, bf16[10,16,16]{2,1,0:T(8,128)(2,1)S(1)}, u32[]{:S(2)}, u32[]{:S(2)}) collective-permute-start(bf16[10,16,16]{2,1,0:T(8,128)(2,1)S(1)} %copy-done.4), channel_id=1, source_target_pairs={{0,1},{1,0},{2,3},{3,2},{4,5},{5,4},{6,7},{7,6},{8,9},{9,8},{10,11... | collective-permute-start | bytes 15368 | tf_op jit(solution)/shard_map/ppermute | solution.py:306
  33.8 2.5 %collective-permute-done.5 = bf16[10,16,16]{2,1,0:T(8,128)(2,1)S(1)} collective-permute-done((bf16[10,16,16]{2,1,0:T(8,128)(2,1)S(1)}, bf16[10,16,16]{2,1,0:T(8,128)(2,1)S(1)}, u32[]{:S(2)}, u32[]{:S(2)}) %collective-permute-start.5) | collective-permute-done | bytes 5152 | tf_op jit(solution)/shard_map/ppermute | solution.py:306
  36.3 0.7 collective-permute-start.10
  37.0 13.2 %collective-permute-done.8.refs_1_.refs_3_ = bf16[528,896]{1,0:T(8,128)(2,1)S(1)} collective-permute-done((bf16[528,896]{1,0:T(8,128)(2,1)S(1)}, bf16[528,896]{1,0:T(8,128)(2,1)S(1)}, u32[]{:S(2)}, u32[]{:S(2)}) %collective-permute-start.8) | collective-permute-done | bytes 946208 | tf_op jit(solution)/shard_map/ppermute | solution.py:306
  50.2 0.7 collective-permute-start.11
  51.0 11.9 %early.1 = (f32[3,10,32,128]{3,2,1,0:T(8,128)S(1)}, f32[3,10,32,128]{3,2,1,0:T(8,128)S(1)}, bf16[16,4,32,1024]{3,2,1,0:T(8,128)(2,1)S(1)}, bf16[32,512]{1,0:T(8,128)(2,1)S(1)}) custom-call(bf16[528,896]{1,0:T(8,128)(2,1)S(1)} %pack.1.refs_0_, bf16[528,896]{1,0:T(8,128)(2,1)} %collective-permute-done.refs_1_, ...), custom_call_target="tpu_custom_call" | custom-call | flops 6442450944 | bytes 4194304 | tf_op jit(solution)/shard_map/early/pallas_call | solution.py:376
  62.8 1.6 %collective-permute-start.6 = (f32[3,10,32,128]{3,2,1,0:T(8,128)S(1)}, f32[3,10,32,128]{3,2,1,0:T(8,128)S(1)}, u32[]{:S(2)}, u32[]{:S(2)}) collective-permute-start(f32[3,10,32,128]{3,2,1,0:T(8,128)S(1)} %get-tuple-element.14), channel_id=1, source_target_pairs={{0,1},{1,0},{2,3},{3,2},{4,5},{5,4},{6,7},{7,6},{8,9},{9,8},{10,11... | collective-permute-start | bytes 1474568 | tf_op jit(solution)/shard_map/ppermute | solution.py:306
  64.4 3.7 %late.1 = (f32[10,32,128]{2,1,0:T(8,128)S(1)}, f32[10,32,128]{2,1,0:T(8,128)S(1)}) custom-call(bf16[528,896]{1,0:T(8,128)(2,1)S(1)} %collective-permute-done.7.refs_0_, bf16[528,896]{1,0:T(8,128)(2,1)S(1)} %collective-permute-done.8.refs_1_.refs_3_, bf16[16,4,32,1024]{3,2,1,0:T(8,128)(2,1)S(1)} %get-tuple-element.15.refs_2_, ...), custom_call_target="tpu_custom_call" | custom-call | flops 2147483648 | bytes 4194304 | tf_op jit(solution)/shard_map/late/pallas_call | solution.py:420
  68.2 0.6 collective-permute-start.9
  68.9 1.3 %collective-permute-start.12 = (f32[10,32,128]{2,1,0:T(8,128)S(1)}, f32[10,32,128]{2,1,0:T(8,128)S(1)}, u32[]{:S(2)}, u32[]{:S(2)}) collective-permute-start(f32[10,32,128]{2,1,0:T(8,128)S(1)} %get-tuple-element.19), channel_id=1, source_target_pairs={{2,0},{4,6},{3,1},{5,7},{10,8},{12,14},{11,9},{13,15},{18,16},{20,... | collective-permute-start | bytes 491528 | tf_op jit(solution)/shard_map/ppermute | solution.py:415
  70.2 1.3 %collective-permute-start.13 = (f32[10,32,128]{2,1,0:T(8,128)S(1)}, f32[10,32,128]{2,1,0:T(8,128)S(1)}, u32[]{:S(2)}, u32[]{:S(2)}) collective-permute-start(f32[10,32,128]{2,1,0:T(8,128)S(1)} %get-tuple-element.20), channel_id=1, source_target_pairs={{2,1},{3,0},{4,7},{5,6},{10,9},{11,8},{12,15},{13,14},{18,17},{19,... | collective-permute-start | bytes 491528 | tf_op jit(solution)/shard_map/ppermute | solution.py:416
  71.5 6.7 %collective-permute-done.9.got_late = f32[10,32,128]{2,1,0:T(8,128)S(1)} collective-permute-done((f32[10,32,128]{2,1,0:T(8,128)S(1)}, f32[10,32,128]{2,1,0:T(8,128)S(1)}, u32[]{:S(2)}, u32[]{:S(2)}) %collective-permute-start.9) | collective-permute-done | bytes 163872 | tf_op jit(solution)/shard_map/ppermute | solution.py:306
  78.2 10.5 %collective-permute-done.12.across = f32[10,32,128]{2,1,0:T(8,128)S(1)} collective-permute-done((f32[10,32,128]{2,1,0:T(8,128)S(1)}, f32[10,32,128]{2,1,0:T(8,128)S(1)}, u32[]{:S(2)}, u32[]{:S(2)}) %collective-permute-start.12) | collective-permute-done | bytes 163872 | tf_op jit(solution)/shard_map/ppermute | solution.py:415
  88.6 3.8 %collective-permute-done.13.across_other = f32[10,32,128]{2,1,0:T(8,128)S(1)} collective-permute-done((f32[10,32,128]{2,1,0:T(8,128)S(1)}, f32[10,32,128]{2,1,0:T(8,128)S(1)}, u32[]{:S(2)}, u32[]{:S(2)}) %collective-permute-start.13) | collective-permute-done | bytes 163872 | tf_op jit(solution)/shard_map/ppermute | solution.py:416
  92.4 1.8 %finish.1 = f32[10,128,128]{2,1,0:T(8,128)} custom-call(s32[4,128]{1,0:T(4,128)S(1)} %bitcast.11, s32[120]{0:T(128)S(1)} %copy-done.3, s32[2,20]{1,0:T(2,128)S(1)} %bitcast.13, f32[3,10,32,128]{3,2,1,0:T(8,128)S(1)} %get-tuple-element.13.keep_early, f32[3,10,32,128]{3,2,1,0:T(8,128)S(1)} %collective-permute-done.6.got_early, ...), custom_call_target="tpu_custom_call" | custom-call | tf_op jit(solution)/shard_map/finish/pallas_call | solution.py:439
  (22 shorter events, 0.4 us)
Async XLA Ops:
  0.0 50.9 %copy-start.2 = (s32[20,2]{0,1:T(2,128)S(1)}, s32[20,2]{0,1:T(2,128)}, u32[]{:S(2)}) copy-start(s32[20,2]{0,1:T(2,128)} %param.11) | copy-start | bytes 484
  0.0 50.9 %copy-start.3 = (s32[120]{0:T(128)S(1)}, s32[120]{0:T(128)}, u32[]{:S(2)}) copy-start(s32[120]{0:T(128)} %occ.1) | copy-start | bytes 1444
  0.0 1.3 %copy-start = (bf16[900,32,16]{0,2,1:T(8,128)(2,1)S(1)}, bf16[900,32,16]{0,2,1:T(8,128)(2,1)}, u32[]{:S(2)}) copy-start(bf16[900,32,16]{0,2,1:T(8,128)(2,1)} %param.6) | copy-start | bytes 2764804
  1.3 30.9 %copy-start.4 = (bf16[10,16,16]{2,1,0:T(8,128)(2,1)S(1)}, bf16[10,16,16]{2,1,0:T(8,128)(2,1)}, u32[]{:S(2)}) copy-start(bf16[10,16,16]{2,1,0:T(8,128)(2,1)} %param.7) | copy-start | bytes 15364
  1.3 49.7 %copy-start.5 = (s32[16]{0:T(128)S(1)}, s32[16]{0:T(128)}, u32[]{:S(2)}) copy-start(s32[16]{0:T(128)} %refs_8_.1) | copy-start | bytes 196
  1.4 23.9 %collective-permute-start.2 = (bf16[528,896]{1,0:T(8,128)(2,1)S(1)}, bf16[528,896]{1,0:T(8,128)(2,1)S(1)}, u32[]{:S(2)}, u32[]{:S(2)}) collective-permute-start(bf16[528,896]{1,0:T(8,128)(2,1)S(1)} %pack.1.refs_0_), channel_id=1, source_target_pairs={{0,16},{2,4},{4,2},{6,22},{8,24},{10,12},{12,10},{14,30},{16,0},{1... | collective-permute-start | bytes 2838536 | tf_op jit(solution)/shard_map/ppermute | solution.py:340
  4.4 22.8 %collective-permute-start.1 = (bf16[528,896]{1,0:T(8,128)(2,1)S(1)}, bf16[528,896]{1,0:T(8,128)(2,1)S(1)}, u32[]{:S(2)}, u32[]{:S(2)}) collective-permute-start(bf16[528,896]{1,0:T(8,128)(2,1)S(1)} %pack.1.refs_0_), channel_id=1, source_target_pairs={{2,18},{4,20},{10,26},{12,28},{18,2},{20,4},{26,10},{28,12},{3,19}... | collective-permute-start | bytes 2838536 | tf_op jit(solution)/shard_map/ppermute | solution.py:345
  5.1 26.4 %collective-permute-start.4 = (bf16[528,896]{1,0:T(8,128)(2,1)S(1)}, bf16[528,896]{1,0:T(8,128)(2,1)}, u32[]{:S(2)}, u32[]{:S(2)}) collective-permute-start(bf16[528,896]{1,0:T(8,128)(2,1)S(1)} %pack.1.refs_0_), channel_id=1, source_target_pairs={{0,2},{2,0},{4,6},{6,4},{1,3},{3,1},{5,7},{7,5},{8,10},{10,8},{12,... | collective-permute-start | bytes 2838536 | tf_op jit(solution)/shard_map/ppermute | solution.py:306
  9.5 41.4 %collective-permute-start = (bf16[528,896]{1,0:T(8,128)(2,1)S(1)}, bf16[528,896]{1,0:T(8,128)(2,1)}, u32[]{:S(2)}, u32[]{:S(2)}) collective-permute-start(bf16[528,896]{1,0:T(8,128)(2,1)S(1)} %pack.1.refs_0_), channel_id=1, source_target_pairs={{0,8},{8,0},{16,24},{24,16},{1,9},{9,1},{17,25},{25,17},{2,10},{10... | collective-permute-start | bytes 2838536 | tf_op jit(solution)/shard_map/ppermute | solution.py:306
  25.4 24.8 %collective-permute-start.8 = (bf16[528,896]{1,0:T(8,128)(2,1)S(1)}, bf16[528,896]{1,0:T(8,128)(2,1)S(1)}, u32[]{:S(2)}, u32[]{:S(2)}) collective-permute-start(bf16[528,896]{1,0:T(8,128)(2,1)S(1)} %collective-permute-done.2.refs_5_), channel_id=1, source_target_pairs={{0,2},{2,0},{4,6},{6,4},{1,3},{3,1},{5,7},{7,5},{8,10},{10,8},{12,... | collective-permute-start | bytes 2838536 | tf_op jit(solution)/shard_map/ppermute | solution.py:306
  27.3 23.6 %collective-permute-start.3 = (bf16[528,896]{1,0:T(8,128)(2,1)S(1)}, bf16[528,896]{1,0:T(8,128)(2,1)S(1)}, u32[]{:S(2)}, u32[]{:S(2)}) collective-permute-start(bf16[528,896]{1,0:T(8,128)(2,1)S(1)} %broadcast_select_fusion), channel_id=1, source_target_pairs={{0,8},{8,0},{16,24},{24,16},{1,9},{9,1},{17,25},{25,17},{2,10},{10... | collective-permute-start | bytes 2838536 | tf_op jit(solution)/shard_map/ppermute | solution.py:306
  31.5 32.9 %collective-permute-start.7 = (bf16[528,896]{1,0:T(8,128)(2,1)}, bf16[528,896]{1,0:T(8,128)(2,1)S(1)}, u32[]{:S(2)}, u32[]{:S(2)}) collective-permute-start(bf16[528,896]{1,0:T(8,128)(2,1)} %collective-permute-done.4.refs_4_.refs_1_), channel_id=1, source_target_pairs={{2,4},{4,2},{3,5},{5,3},{10,12},{12,10},{11,13},{13,11},{18,20},{2... | collective-permute-start | bytes 2838536 | tf_op jit(solution)/shard_map/ppermute | solution.py:349
  32.2 4.1 %collective-permute-start.5 = (bf16[10,16,16]{2,1,0:T(8,128)(2,1)S(1)}, bf16[10,16,16]{2,1,0:T(8,128)(2,1)S(1)}, u32[]{:S(2)}, u32[]{:S(2)}) collective-permute-start(bf16[10,16,16]{2,1,0:T(8,128)(2,1)S(1)} %copy-done.4), channel_id=1, source_target_pairs={{0,1},{1,0},{2,3},{3,2},{4,5},{5,4},{6,7},{7,6},{8,9},{9,8},{10,11... | collective-permute-start | bytes 15368 | tf_op jit(solution)/shard_map/ppermute | solution.py:306
  36.3 32.5 %collective-permute-start.10 = (bf16[528,896]{1,0:T(8,128)(2,1)}, bf16[528,896]{1,0:T(8,128)(2,1)S(1)}, u32[]{:S(2)}, u32[]{:S(2)}) collective-permute-start(bf16[528,896]{1,0:T(8,128)(2,1)} %collective-permute-done.4.refs_4_.refs_1_), channel_id=1, source_target_pairs={{2,10},{4,12},{10,2},{12,4},{18,26},{20,28},{26,18},{28,20},{3,11}... | collective-permute-start | bytes 2838536 | tf_op jit(solution)/shard_map/ppermute | solution.py:355
  50.2 18.6 %collective-permute-start.11 = (bf16[528,896]{1,0:T(8,128)(2,1)S(1)}, bf16[528,896]{1,0:T(8,128)(2,1)S(1)}, u32[]{:S(2)}, u32[]{:S(2)}) collective-permute-start(bf16[528,896]{1,0:T(8,128)(2,1)S(1)} %collective-permute-done.8.refs_1_.refs_3_), channel_id=1, source_target_pairs={{2,10},{4,12},{10,2},{12,4},{18,26},{20,28},{26,18},{28,20},{3,11}... | collective-permute-start | bytes 2838536 | tf_op jit(solution)/shard_map/ppermute | solution.py:355
  62.8 15.3 %collective-permute-start.6 = (f32[3,10,32,128]{3,2,1,0:T(8,128)S(1)}, f32[3,10,32,128]{3,2,1,0:T(8,128)S(1)}, u32[]{:S(2)}, u32[]{:S(2)}) collective-permute-start(f32[3,10,32,128]{3,2,1,0:T(8,128)S(1)} %get-tuple-element.14), channel_id=1, source_target_pairs={{0,1},{1,0},{2,3},{3,2},{4,5},{5,4},{6,7},{7,6},{8,9},{9,8},{10,11... | collective-permute-start | bytes 1474568 | tf_op jit(solution)/shard_map/ppermute | solution.py:306
  68.2 24.2 %copy-start.1 = (s32[512]{0:T(512)S(1)}, s32[512]{0:T(512)}, u32[]{:S(2)}) copy-start(s32[512]{0:T(512)} %param.8) | copy-start | bytes 6148
  68.2 10.0 %collective-permute-start.9 = (f32[10,32,128]{2,1,0:T(8,128)S(1)}, f32[10,32,128]{2,1,0:T(8,128)S(1)}, u32[]{:S(2)}, u32[]{:S(2)}) collective-permute-start(f32[10,32,128]{2,1,0:T(8,128)S(1)} %get-tuple-element.18), channel_id=1, source_target_pairs={{0,1},{1,0},{2,3},{3,2},{4,5},{5,4},{6,7},{7,6},{8,9},{9,8},{10,11... | collective-permute-start | bytes 491528 | tf_op jit(solution)/shard_map/ppermute | solution.py:306
  68.9 19.8 %collective-permute-start.12 = (f32[10,32,128]{2,1,0:T(8,128)S(1)}, f32[10,32,128]{2,1,0:T(8,128)S(1)}, u32[]{:S(2)}, u32[]{:S(2)}) collective-permute-start(f32[10,32,128]{2,1,0:T(8,128)S(1)} %get-tuple-element.19), channel_id=1, source_target_pairs={{2,0},{4,6},{3,1},{5,7},{10,8},{12,14},{11,9},{13,15},{18,16},{20,... | collective-permute-start | bytes 491528 | tf_op jit(solution)/shard_map/ppermute | solution.py:415
  70.2 22.2 %collective-permute-start.13 = (f32[10,32,128]{2,1,0:T(8,128)S(1)}, f32[10,32,128]{2,1,0:T(8,128)S(1)}, u32[]{:S(2)}, u32[]{:S(2)}) collective-permute-start(f32[10,32,128]{2,1,0:T(8,128)S(1)} %get-tuple-element.20), channel_id=1, source_target_pairs={{2,1},{3,0},{4,7},{5,6},{10,9},{11,8},{12,15},{13,14},{18,17},{19,... | collective-permute-start | bytes 491528 | tf_op jit(solution)/shard_map/ppermute | solution.py:416

commit v3 on v2

--- a/solution.py
+++ b/solution.py
@@ -155,9 +155,11 @@
     return jnp.bitwise_xor(occ[pairs[0, p]], occ[pairs[1, p]])
 
 
-def weight_rows(amplitudes, win, occ, pairs, first, n_p):
-    n, width = amplitudes.shape
+def weight_rows(amplitudes, win, occ, pairs, place, n_p):
+    width = amplitudes.shape[1]
+    n = amplitudes.shape[0]
     slab = n // width
+    first = place * slab
     lanes = width * width
     spread = multiply(amplitudes[...], one_hot((width, lanes), lambda d, l: d == lax.div(l, width)), NN)
     c_of_row = lax.rem(lax.broadcasted_iota(jnp.int32, (n, lanes), 0), width)
@@ -178,43 +180,78 @@
     return jnp.concatenate([masked, masked], axis=1)
 
 
+def prep_kernel(
+    rest, own, by_core, mine, others, win, occ, pairs,
+    part, own_rows, weights, held, tail, sems,
+):
+    copies = [fetch(src, dst, tail.at[i], sems.at[i]) for i, (src, dst) in enumerate(((own, own_rows), (by_core, held)))]
+    width, _, per_device, _ = part.shape
+    n_p = weights.shape[0] // 2
+    pair = lax.axis_index("pair")
+    weights[:n_p] = weight_rows(mine, win, occ, pairs, pair, n_p)
+    weights[n_p:] = weight_rows(others, win, occ, pairs, 1 - pair, n_p)
+    order = window_major(width, per_device)
+    for i, rows in enumerate((own_rows, held)):
+        unpack(copies[i], rows, tail.at[i], rest)
+        place_rows(part, order, rows, i)
+
+
+def outer_kernel(rest, facing, by_core, part, held, tails, sems):
+    @pl.when(is_middle())
+    def _():
+        width, _, per_device, _ = part.shape
+        copies = [fetch(src, held.at[i], tails.at[i], sems.at[i]) for i, src in enumerate((facing, by_core))]
+        order = window_major(width, per_device)
+        for i in range(2):
+            unpack(copies[i], held.at[i], tails.at[i], rest)
+            place_rows(part, order, held.at[i], i)
+
+
+def fetch_part(part, panel, sems):
+    row = lax.axis_index("row")
+    copies = []
+    for i in range(part.shape[1]):
+        to = panel.at[:, pl.ds(jnp.bitwise_xor(row, i), 1)]
+        copies.append(pltpu.make_async_copy(part.at[:, pl.ds(i, 1)], to, sems.at[i]))
+        copies[-1].start()
+    return copies
+
+
 def early_kernel(
-    rest, own, by_core, by_x, by_both, facing, turned, mine, others, win, occ, pairs,
-    keep, send, panel_out, weights, panel, held, tails, split, sums, sems, panel_sem,
+    rest, own_rows, part, by_x, by_both, facing, turned, weights,
+    keep, send, panel_out, panel, held, tails, split, sums, sems, own_sem, part_sems, panel_sem,
 ):
     middle = is_middle()
     row = lax.axis_index("row")
     width, _, per_device, _ = panel.shape
-    sources = (own, by_core, None, by_both, facing, turned)
-    copies = [
-        None if src is None else fetch(src, held.at[i], tails.at[i], sems.at[i]) for i, src in enumerate(sources)
-    ]
+    both = fetch(by_both, held.at[1], tails.at[1], sems.at[1])
 
     @pl.when(middle)
     def _():
-        fetch(by_x, held.at[2], tails.at[2], sems.at[2])
+        fetch(by_x, held.at[0], tails.at[0], sems.at[0])
 
     @pl.when(jnp.logical_not(middle))
     def _():
-        fetch(turned, held.at[2], tails.at[2], sems.at[2])
-
-    copies[2] = wait_only(by_x, held.at[2], tails.at[2], sems.at[2])
-    slab = mine.shape[0] // width
-    n_p = weights.shape[0] // 2
-    pair = lax.axis_index("pair")
-    weights[:n_p] = weight_rows(mine, win, occ, pairs, pair * slab, n_p)
-    weights[n_p:] = weight_rows(others, win, occ, pairs, (1 - pair) * slab, n_p)
+        fetch(turned, held.at[0], tails.at[0], sems.at[0])
+
+    parts = fetch_part(part, panel, part_sems)
+    own = pltpu.make_async_copy(own_rows, held.at[2], own_sem)
+    own.start()
+    copies = [fetch(src, held.at[i], tails.at[i], sems.at[i]) for i, src in ((3, facing), (4, turned))]
     order = window_major(width, per_device)
-    for i in range(4):
-        unpack(copies[i], held.at[i], tails.at[i], rest)
-        place_rows(panel, order, held.at[i], jnp.bitwise_xor(row, i))
+    for i, waits in enumerate((wait_only(by_x, held.at[0], tails.at[0], sems.at[0]), both)):
+        unpack(waits, held.at[i], tails.at[i], rest)
+        place_rows(panel, order, held.at[i], jnp.bitwise_xor(row, 2 + i))
+    for copy in parts:
+        copy.wait()
     back = pltpu.make_async_copy(panel, panel_out, panel_sem)
     back.start()
-    for i in (4, 5):
-        unpack(copies[i], held.at[i], tails.at[i], rest)
+    own.wait()
+    for i, waits in enumerate(copies):
+        unpack(waits, held.at[3 + i], tails.at[3 + i], rest)
 
     def block(s, carry):
-        contract_block(held.at[jnp.where(s == 0, 0, 3 + s)], panel, weights, split, sums, keep.at[s], send.at[s])
+        contract_block(held.at[2 + s], panel, weights, split, sums, keep.at[s], send.at[s])
         return carry
 
     lax.fori_loop(0, jnp.where(middle, 3, 2), block, 0)
@@ -230,20 +267,22 @@
 
 
 def across_kernel(
-    rest, far, facing, by_core, by_x, by_both, weights, keep, send, panel, held, tails, split, sums, sems
+    rest, far, part, by_x, by_both, weights, keep, send, panel, held, tails, split, sums, sems, part_sems
 ):
     @pl.when(is_middle())
     def _():
-        sources = (facing, by_core, by_x, by_both, far)
-        copies = [fetch(src, held.at[i], tails.at[i], sems.at[i]) for i, src in enumerate(sources)]
+        copies = [fetch(src, held.at[i], tails.at[i], sems.at[i]) for i, src in enumerate((by_x, by_both, far))]
+        parts = fetch_part(part, panel, part_sems)
+        width, _, per_device, _ = panel.shape
         row = lax.axis_index("row")
-        width, _, per_device, _ = panel.shape
         order = window_major(width, per_device)
-        for i in range(4):
+        for i in range(2):
             unpack(copies[i], held.at[i], tails.at[i], rest)
-            place_rows(panel, order, held.at[i], jnp.bitwise_xor(row, i))
-        unpack(copies[4], held.at[4], tails.at[4], rest)
-        contract_block(held.at[4], panel, weights, split, sums, keep, send)
+            place_rows(panel, order, held.at[i], jnp.bitwise_xor(row, 2 + i))
+        unpack(copies[2], held.at[2], tails.at[2], rest)
+        for copy in parts:
+            copy.wait()
+        contract_block(held.at[2], panel, weights, split, sums, keep, send)
 
 
 def late_kernel(rest, far, passed, panel_in, weights, keep, send, panel, held, tail, split, sums, sems, panel_sem):
@@ -336,105 +375,129 @@
     def at(r, c):
         return r * n_cols + c
 
+    block = jax.ShapeDtypeStruct((slab, per_device, n_b), jnp.float32)
+    blocks = jax.ShapeDtypeStruct((3, slab, per_device, n_b), jnp.float32)
+    n_p = 16 * pl.cdiv(slab, 16)
+    split_scratch = pltpu.VMEM((per_device, 2, width, width, n_b), jnp.bfloat16)
+    sums_scratch = pltpu.VMEM((per_device * 2 * n_p, n_b), jnp.float32)
+    pairs = jnp.transpose(pair_list)
+
+    def panel(count):
+        return jax.ShapeDtypeStruct((width, count, per_device, depth), jnp.bfloat16)
+
+    panel_scratch = pltpu.VMEM(panel(n_rows).shape, jnp.bfloat16)
+
+    def held(*count):
+        return [pltpu.VMEM(count + (n, depth), jnp.bfloat16), pltpu.VMEM(count + (below, LANES), jnp.bfloat16)]
+
+    def sems(*count):
+        return pltpu.SemaphoreType.DMA(count)
+
+    def cost(n_blocks):
+        flops = 20 * n_blocks * n * n_b * width * depth
+        return pl.CostEstimate(flops=flops, bytes_accessed=8 * n * depth, transcendentals=0)
+
     facing = swap(own, "col", 1)
     turned = lax.ppermute(
         own,
         ("row", "col"),
         [(at(r, c), at(r, 3 - c) if c in (1, 2) else at(r ^ 2, c)) for r in range(n_rows) for c in range(n_cols)],
     )
-    by_x = lax.ppermute(own, ("row", "col"), [(at(r, c), at(r ^ 2, c)) for r in range(n_rows) for c in (1, 2)])
+    by_x = lax.ppermute(
+        own,
+        ("row", "col"),
+        [(at(r, c), at(r ^ 2 if c in (1, 2) else r ^ 1, c)) for r in range(n_rows) for c in range(n_cols)],
+    )
     by_core = swap(own, "row", 1)
-    other_amplitudes = swap(amplitudes, "pair", 1)
-
-    far = lax.ppermute(facing, "col", [(1, 2), (2, 1)])
+    others = swap(amplitudes, "pair", 1)
+
+    own_part, own_rows, weights = pl.pallas_call(
+        lambda *refs: prep_kernel(rest, *refs),
+        out_shape=(
+            panel(2),
+            jax.ShapeDtypeStruct((n, depth), jnp.bfloat16),
+            jax.ShapeDtypeStruct((2 * n_p, 2 * width * width), jnp.bfloat16),
+        ),
+        in_specs=[anywhere] * 2 + [vmem] * 2 + [smem] * 3,
+        out_specs=(vmem, vmem, vmem),
+        scratch_shapes=[
+            pltpu.VMEM((n, depth), jnp.bfloat16), pltpu.VMEM((2, below, LANES), jnp.bfloat16), sems(2, 2)
+        ],
+        compiler_params=params,
+        cost_estimate=cost(1),
+        name="prep",
+    )(
+        own, by_core,
+        amplitudes.reshape(slab * width, width), others.reshape(slab * width, width), win_irreps, occ_irreps, pairs,
+    )
+
+    def middle_or_core(array):
+        pairs = [(at(r, c), at(r, 3 - c) if c in (1, 2) else at(r ^ 1, c)) for r in range(n_rows) for c in range(n_cols)]
+        return lax.ppermute(array, ("row", "col"), pairs)
+
+    far = middle_or_core(facing)
     passed = swap(turned, "col", 1)
     x_rows = jnp.where(is_middle(), by_x, turned)
     by_both = swap(x_rows, "row", 1)
 
-    def middle_core_swap(array):
-        return lax.ppermute(array, ("row", "col"), [(at(r, c), at(r ^ 1, c)) for r in range(n_rows) for c in (1, 2)])
-
-    facing_core = middle_core_swap(facing)
-    passed_core = middle_core_swap(passed)
-
-    block = jax.ShapeDtypeStruct((slab, per_device, n_b), jnp.float32)
-    blocks = jax.ShapeDtypeStruct((3, slab, per_device, n_b), jnp.float32)
-    panel_shape = (width, n_rows, per_device, depth)
-    panel_scratch = pltpu.VMEM(panel_shape, jnp.bfloat16)
-    split_scratch = pltpu.VMEM((per_device, 2, width, width, n_b), jnp.bfloat16)
-    n_p = 16 * pl.cdiv(slab, 16)
-    sums_scratch = pltpu.VMEM((per_device * 2 * n_p, n_b), jnp.float32)
-    pairs = jnp.transpose(pair_list)
-
-    def held(*count):
-        return [pltpu.VMEM(count + (n, depth), jnp.bfloat16), pltpu.VMEM(count + (below, LANES), jnp.bfloat16)]
-
-    def cost(n_blocks):
-        flops = 2 * n_blocks * n * n_b * width * depth
-        return pl.CostEstimate(flops=flops, bytes_accessed=8 * n * depth, transcendentals=0)
-
-    keep_early, send_early, panel, weights = pl.pallas_call(
+    facing_core = swap(facing, "row", 1)
+
+    keep_early, send_early, own_panel = pl.pallas_call(
         lambda *refs: early_kernel(rest, *refs),
-        out_shape=(
-            blocks,
-            blocks,
-            jax.ShapeDtypeStruct(panel_shape, jnp.bfloat16),
-            jax.ShapeDtypeStruct((2 * n_p, 2 * width * width), jnp.bfloat16),
-        ),
-        in_specs=[anywhere] * 6 + [vmem] * 2 + [smem] * 3,
-        out_specs=(vmem, vmem, anywhere, vmem),
+        out_shape=(blocks, blocks, panel(n_rows)),
+        in_specs=[anywhere] * 6 + [vmem],
+        out_specs=(vmem, vmem, anywhere),
         scratch_shapes=[
-            panel_scratch,
-            *held(6),
-            split_scratch,
-            sums_scratch,
-            pltpu.SemaphoreType.DMA((6, 2)),
-            pltpu.SemaphoreType.DMA,
+            panel_scratch, *held(5), split_scratch, sums_scratch, sems(5, 2), sems(), sems(2), sems()
         ],
         compiler_params=params,
         cost_estimate=cost(3),
         name="early",
-    )(
-        own, by_core, by_x, by_both, facing, turned,
-        amplitudes.reshape(slab * width, width), other_amplitudes.reshape(slab * width, width),
-        win_irreps, occ_irreps, pairs,
-    )
+    )(own_rows, own_part, by_x, by_both, facing, turned, weights)
     got_early = swap(send_early, "pair", 1)
 
-    keep_across, send_across = pl.pallas_call(
-        lambda *refs: across_kernel(rest, *refs),
-        out_shape=(block, block),
-        in_specs=[anywhere] * 5 + [vmem],
-        out_specs=(vmem, vmem),
-        scratch_shapes=[panel_scratch, *held(5), split_scratch, sums_scratch, pltpu.SemaphoreType.DMA((5, 2))],
+    outer_part = pl.pallas_call(
+        lambda *refs: outer_kernel(rest, *refs),
+        out_shape=panel(2),
+        in_specs=[anywhere] * 2,
+        out_specs=vmem,
+        scratch_shapes=[*held(2), sems(2, 2)],
         compiler_params=params,
         cost_estimate=cost(1),
-        name="across",
-    )(far, facing, facing_core, passed, passed_core, weights)
-    outwards = [(c, y, 0 if c == 1 else 3) for c in (1, 2) for y in range(n_pair)]
-    across = lax.ppermute(keep_across, "col", [(1, 0), (2, 3)])
-    across_other = lax.ppermute(
-        send_across, ("col", "pair"), [(c * n_pair + y, to * n_pair + (y ^ 1)) for c, y, to in outwards]
-    )
-
+        name="outer",
+    )(facing, facing_core)
+
+    passed, _, _ = lax.optimization_barrier((passed, own_panel, outer_part))
+    passed_core = swap(passed, "row", 1)
     keep_late, send_late = pl.pallas_call(
         lambda *refs: late_kernel(rest, *refs),
         out_shape=(block, block),
         in_specs=[anywhere] * 3 + [vmem],
         out_specs=(vmem, vmem),
-        scratch_shapes=[
-            panel_scratch,
-            *held(),
-            split_scratch,
-            sums_scratch,
-            pltpu.SemaphoreType.DMA((2,)),
-            pltpu.SemaphoreType.DMA,
-        ],
+        scratch_shapes=[panel_scratch, *held(), split_scratch, sums_scratch, sems(2), sems()],
         compiler_params=params,
         cost_estimate=cost(1),
         name="late",
-    )(far, passed, panel, weights)
-    got_late = swap(send_late, "pair", 1)
+    )(far, passed, own_panel, weights)
+
+    passed_core, _ = lax.optimization_barrier((passed_core, keep_late))
+    keep_across, send_across = pl.pallas_call(
+        lambda *refs: across_kernel(rest, *refs),
+        out_shape=(block, block),
+        in_specs=[anywhere] * 4 + [vmem],
+        out_specs=(vmem, vmem),
+        scratch_shapes=[panel_scratch, *held(3), split_scratch, sums_scratch, sems(3, 2), sems(2)],
+        compiler_params=params,
+        cost_estimate=cost(1),
+        name="across",
+    )(far, outer_part, passed, passed_core, weights)
+    across = swap(keep_across, "col", 1)
+    across_other = lax.ppermute(
+        send_across,
+        ("col", "pair"),
+        [(c * n_pair + y, (c ^ 1) * n_pair + (y ^ 1)) for c in range(n_cols) for y in range(n_pair)],
+    )
+    got_late = swap(lax.optimization_barrier((send_late, keep_across))[0], "pair", 1)
 
     out = pl.pallas_call(
         finish_kernel,

time: 94.5 us -> 74.8 us (0.79)
  waiting for transfers between devices: 56.5 us -> 32.9 us
  starting transfers between devices: 18.4 us -> 21.9 us
    ppermute x6 -> x3, waiting for transfers between devices: 14.2 us -> 0.01 us  [the longest x1 0.01 us: staged_body(): lax.ppermute(own, ('row', 'col'), [(at(r, c), at(r ^ 2 if c in (1, 2) els...]
    ppermute x7 -> x10, waiting for transfers between devices: 26.5 us -> 16.6 us  [swap(): return lax.ppermute(array, axis, [(i, i ^ mask) for i in range(size)])]
    ppermute x7 -> x10, starting transfers between devices: 10 us -> 18.3 us  [swap(): return lax.ppermute(array, axis, [(i, i ^ mask) for i in range(size)])]
    ppermute x6 -> x3, starting transfers between devices: 5.42 us -> 0.61 us  [the longest x1 0.34 us: middle_or_core(): return lax.ppermute(array, ('row', 'col'), pairs)]
    pallas_call x0 -> x2, Pallas kernels: none -> 3.04 us  [the longest x1 2.98 us: staged_body(): pl.pallas_call(lambda *refs: prep_kernel(rest, *refs), out_shape=(panel(2...]
    pallas_call x1, Pallas kernels: 11.9 us -> 9.4 us  [staged_body(): pl.pallas_call(lambda *refs: early_kernel(rest, *refs), out_shape=(blocks...]
  transfers between devices with their start and end apart: 14 -> 14, of which waited for: 7 -> 3; matrix products, arithmetic and copies ran while one was open for 0% -> 0% of each run, Pallas kernels for 17% -> 22%
where the time goes in v3:
time: 74.8 us; the launch traced here: 74.7 us
  waiting for transfers between devices  32.9 us (44%)
  starting transfers between devices  21.9 us (29%)
  Pallas kernels  18.4 us (25%)
  local copies, waits for them, and re-layouts  1.25 us (2%)
    ppermute x10, starting transfers between devices, swap(): return lax.ppermute(array, axis, [(i, i ^ mask) for i in range(size)])  18.3 us
    ppermute x10, waiting for transfers between devices, swap(): return lax.ppermute(array, axis, [(i, i ^ mask) for i in range(size)])  16.6 us
    ppermute x1, waiting for transfers between devices, staged_body(): lax.ppermute(own, ('row', 'col'), [(at(r, c), at(r, 3 - c) if c in (1, 2)...  16.3 us
    pallas_call x1, Pallas kernels, staged_body(): pl.pallas_call(lambda *refs: early_kernel(rest, *refs), out_shape=(blocks...  9.4 us
    pallas_call x1, Pallas kernels, staged_body(): pl.pallas_call(lambda *refs: late_kernel(rest, *refs), out_shape=(block,...  3.74 us
    pallas_call x1, Pallas kernels, staged_body(): pl.pallas_call(lambda *refs: prep_kernel(rest, *refs), out_shape=(panel(2...  2.98 us
    ppermute x1, starting transfers between devices, staged_body(): lax.ppermute(own, ('row', 'col'), [(at(r, c), at(r, 3 - c) if c in (1, 2)...  2.94 us
    pallas_call x1, Pallas kernels, staged_body(): pl.pallas_call(finish_kernel, out_shape=jax.ShapeDtypeStruct((slab, n_b,...  1.77 us
  transfers between devices with their start and end apart: 14, of which 3 were waited for; matrix products, arithmetic and copies ran while one was open for 0% of the time, Pallas kernels for 22%

profile of v3, /device:TPU:0, one launch (start us, length us, event | category | flops | bytes accessed | tf_op | source)
XLA Modules:
  0.0 74.7 jit_solution(12200440808688403401)
XLA Ops:
  0.0 1.2 %copy-done = bf16[900,32,16]{0,2,1:T(8,128)(2,1)S(1)} copy-done((bf16[900,32,16]{0,2,1:T(8,128)(2,1)S(1)}, bf16[900,32,16]{0,2,1:T(8,128)(2,1)}, u32[]{:S(2)}) %copy-start) | copy-done | bytes 921624
  1.2 0.2 pack.1.refs_0_
  1.4 2.9 %collective-permute-start.3 = (bf16[528,896]{1,0:T(8,128)(2,1)S(1)}, bf16[528,896]{1,0:T(8,128)(2,1)S(1)}, u32[]{:S(2)}, u32[]{:S(2)}) collective-permute-start(bf16[528,896]{1,0:T(8,128)(2,1)S(1)} %pack.1.refs_0_), channel_id=1, source_target_pairs={{0,16},{2,4},{4,2},{6,22},{8,24},{10,12},{12,10},{14,30},{16,0},{1... | collective-permute-start | bytes 2838536 | tf_op jit(solution)/shard_map/ppermute | solution.py:401
  4.4 3.1 %collective-permute-start.5 = (bf16[528,896]{1,0:T(8,128)(2,1)S(1)}, bf16[528,896]{1,0:T(8,128)(2,1)}, u32[]{:S(2)}, u32[]{:S(2)}) collective-permute-start(bf16[528,896]{1,0:T(8,128)(2,1)S(1)} %pack.1.refs_0_), channel_id=1, source_target_pairs={{0,2},{2,0},{4,6},{6,4},{1,3},{3,1},{5,7},{7,5},{8,10},{10,8},{12,... | collective-permute-start | bytes 2838536 | tf_op jit(solution)/shard_map/ppermute | solution.py:345
  7.5 1.5 %collective-permute-start.1 = (bf16[10,16,16]{2,1,0:T(8,128)(2,1)}, bf16[10,16,16]{2,1,0:T(8,128)(2,1)S(1)}, u32[]{:S(2)}, u32[]{:S(2)}) collective-permute-start(bf16[10,16,16]{2,1,0:T(8,128)(2,1)} %param.7), channel_id=1, source_target_pairs={{0,1},{1,0},{2,3},{3,2},{4,5},{5,4},{6,7},{7,6},{8,9},{9,8},{10,11... | collective-permute-start | bytes 15368 | tf_op jit(solution)/shard_map/ppermute | solution.py:345
  9.0 16.3 %collective-permute-done.3.refs_5_ = bf16[528,896]{1,0:T(8,128)(2,1)S(1)} collective-permute-done((bf16[528,896]{1,0:T(8,128)(2,1)S(1)}, bf16[528,896]{1,0:T(8,128)(2,1)S(1)}, u32[]{:S(2)}, u32[]{:S(2)}) %collective-permute-start.3) | collective-permute-done | bytes 946208 | tf_op jit(solution)/shard_map/ppermute | solution.py:401
  25.3 0.2 broadcast_select_fusion
  25.5 0.1 collective-permute-start.4
  25.6 3.2 %collective-permute-start.8 = (bf16[528,896]{1,0:T(8,128)(2,1)S(1)}, bf16[528,896]{1,0:T(8,128)(2,1)S(1)}, u32[]{:S(2)}, u32[]{:S(2)}) collective-permute-start(bf16[528,896]{1,0:T(8,128)(2,1)S(1)} %collective-permute-done.3.refs_5_), channel_id=1, source_target_pairs={{0,2},{2,0},{4,6},{6,4},{1,3},{3,1},{5,7},{7,5},{8,10},{10,8},{12,... | collective-permute-start | bytes 2838536 | tf_op jit(solution)/shard_map/ppermute | solution.py:345
  28.8 0.2 collective-permute-start.9
  28.9 0.3 collective-permute-start.7
  29.3 3.0 %prep.1 = (bf16[16,2,32,1024]{3,2,1,0:T(8,128)(2,1)S(1)}, bf16[512,1024]{1,0:T(8,128)(2,1)S(1)}, bf16[32,512]{1,0:T(8,128)(2,1)S(1)}) custom-call(bf16[528,896]{1,0:T(8,128)(2,1)S(1)} %pack.1.refs_0_, bf16[528,896]{1,0:T(8,128)(2,1)} %collective-permute-done.refs_1_, bf16[160,16]{1,0:T(8,128)(2,1)S(1)} %bitcast.14, bf16[160,16]{1,0:T(8,128)(2,1)S(1)} %bitcast.15, ...), custom_call_target="tpu_custom_call" | custom-call | flops 21474836480 | bytes 4194304 | tf_op jit(solution)/shard_map/prep/pallas_call | solution.py:414
  32.3 9.4 %early.1 = (f32[3,10,32,128]{3,2,1,0:T(8,128)S(1)}, f32[3,10,32,128]{3,2,1,0:T(8,128)S(1)}, bf16[16,4,32,1024]{3,2,1,0:T(8,128)(2,1)S(1)}) custom-call(bf16[512,1024]{1,0:T(8,128)(2,1)S(1)} %get-tuple-element.18.refs_0_, bf16[16,2,32,1024]{3,2,1,0:T(8,128)(2,1)S(1)} %get-tuple-element.19.refs_1_, bf16[528,896]{1,0:T(8,128)(2,1)S(1)} %collective-permute-done.2.refs_2_, ...), custom_call_target="tpu_custom_call" | custom-call | flops 64424509440 | bytes 4194304 | tf_op jit(solution)/shard_map/early/pallas_call | solution.py:445
  41.7 0.1 outer.1.refs_1_
  41.8 8.5 %collective-permute-done.8.refs_1_.refs_2_ = bf16[528,896]{1,0:T(8,128)(2,1)S(1)} collective-permute-done((bf16[528,896]{1,0:T(8,128)(2,1)S(1)}, bf16[528,896]{1,0:T(8,128)(2,1)S(1)}, u32[]{:S(2)}, u32[]{:S(2)}) %collective-permute-start.8) | collective-permute-done | bytes 946208 | tf_op jit(solution)/shard_map/ppermute | solution.py:345
  50.3 1.5 %collective-permute-start.6 = (f32[3,10,32,128]{3,2,1,0:T(8,128)S(1)}, f32[3,10,32,128]{3,2,1,0:T(8,128)S(1)}, u32[]{:S(2)}, u32[]{:S(2)}) collective-permute-start(f32[3,10,32,128]{3,2,1,0:T(8,128)S(1)} %get-tuple-element.22), channel_id=1, source_target_pairs={{0,1},{1,0},{2,3},{3,2},{4,5},{5,4},{6,7},{7,6},{8,9},{9,8},{10,11... | collective-permute-start | bytes 1474568 | tf_op jit(solution)/shard_map/ppermute | solution.py:345
  51.8 3.7 %late.1 = (f32[10,32,128]{2,1,0:T(8,128)S(1)}, f32[10,32,128]{2,1,0:T(8,128)S(1)}) custom-call(bf16[528,896]{1,0:T(8,128)(2,1)S(1)} %collective-permute-done.7.refs_0_, bf16[528,896]{1,0:T(8,128)(2,1)S(1)} %collective-permute-done.8.refs_1_.refs_2_, bf16[16,4,32,1024]{3,2,1,0:T(8,128)(2,1)S(1)} %get-tuple-element.23.refs_2_, ...), custom_call_target="tpu_custom_call" | custom-call | flops 21474836480 | bytes 4194304 | tf_op jit(solution)/shard_map/late/pallas_call | solution.py:472
  55.6 0.0 copy-start.1
  55.6 0.3 across.1
  55.9 7.4 %collective-permute-start.12 = (f32[10,32,128]{2,1,0:T(8,128)S(1)}, f32[10,32,128]{2,1,0:T(8,128)S(1)}, u32[]{:S(2)}, u32[]{:S(2)}) collective-permute-start(f32[10,32,128]{2,1,0:T(8,128)S(1)} %get-tuple-element.28), channel_id=1, source_target_pairs={{0,2},{2,0},{4,6},{6,4},{1,3},{3,1},{5,7},{7,5},{8,10},{10,8},{12,... | collective-permute-start | bytes 491528 | tf_op jit(solution)/shard_map/ppermute | solution.py:345
  63.3 1.3 %collective-permute-start.11 = (f32[10,32,128]{2,1,0:T(8,128)S(1)}, f32[10,32,128]{2,1,0:T(8,128)S(1)}, u32[]{:S(2)}, u32[]{:S(2)}) collective-permute-start(f32[10,32,128]{2,1,0:T(8,128)S(1)} %get-tuple-element.29), channel_id=1, source_target_pairs={{0,1},{1,0},{2,3},{3,2},{4,5},{5,4},{6,7},{7,6},{8,9},{9,8},{10,11... | collective-permute-start | bytes 491528 | tf_op jit(solution)/shard_map/ppermute | solution.py:345
  64.6 0.3 collective-permute-start.13
  64.9 8.0 %collective-permute-done.11.got_late = f32[10,32,128]{2,1,0:T(8,128)S(1)} collective-permute-done((f32[10,32,128]{2,1,0:T(8,128)S(1)}, f32[10,32,128]{2,1,0:T(8,128)S(1)}, u32[]{:S(2)}, u32[]{:S(2)}) %collective-permute-start.11) | collective-permute-done | bytes 163872 | tf_op jit(solution)/shard_map/ppermute | solution.py:345
  72.9 1.8 %finish.1 = f32[10,128,128]{2,1,0:T(8,128)} custom-call(s32[4,128]{1,0:T(4,128)S(1)} %bitcast.11, s32[120]{0:T(128)S(1)} %copy-done.3, s32[2,20]{1,0:T(2,128)S(1)} %bitcast.13, f32[3,10,32,128]{3,2,1,0:T(8,128)S(1)} %get-tuple-element.21.keep_early, f32[3,10,32,128]{3,2,1,0:T(8,128)S(1)} %collective-permute-done.6.got_early, ...), custom_call_target="tpu_custom_call" | custom-call | tf_op jit(solution)/shard_map/finish/pallas_call | solution.py:502
  (24 shorter events, 0.1 us)
Async XLA Ops:
  0.0 1.2 %copy-start = (bf16[900,32,16]{0,2,1:T(8,128)(2,1)S(1)}, bf16[900,32,16]{0,2,1:T(8,128)(2,1)}, u32[]{:S(2)}) copy-start(bf16[900,32,16]{0,2,1:T(8,128)(2,1)} %param.6) | copy-start | bytes 2764804
  1.2 28.1 %copy-start.2 = (s32[20,2]{0,1:T(2,128)S(1)}, s32[20,2]{0,1:T(2,128)}, u32[]{:S(2)}) copy-start(s32[20,2]{0,1:T(2,128)} %param.11) | copy-start | bytes 484
  1.2 28.1 %copy-start.3 = (s32[120]{0:T(128)S(1)}, s32[120]{0:T(128)}, u32[]{:S(2)}) copy-start(s32[120]{0:T(128)} %occ.1) | copy-start | bytes 1444
  1.2 28.1 %copy-start.4 = (bf16[10,16,16]{2,1,0:T(8,128)(2,1)S(1)}, bf16[10,16,16]{2,1,0:T(8,128)(2,1)}, u32[]{:S(2)}) copy-start(bf16[10,16,16]{2,1,0:T(8,128)(2,1)} %param.7) | copy-start | bytes 15364
  1.2 28.1 %copy-start.5 = (s32[16]{0:T(128)S(1)}, s32[16]{0:T(128)}, u32[]{:S(2)}) copy-start(s32[16]{0:T(128)} %refs_4_.1) | copy-start | bytes 196
  1.4 23.9 %collective-permute-start.3 = (bf16[528,896]{1,0:T(8,128)(2,1)S(1)}, bf16[528,896]{1,0:T(8,128)(2,1)S(1)}, u32[]{:S(2)}, u32[]{:S(2)}) collective-permute-start(bf16[528,896]{1,0:T(8,128)(2,1)S(1)} %pack.1.refs_0_), channel_id=1, source_target_pairs={{0,16},{2,4},{4,2},{6,22},{8,24},{10,12},{12,10},{14,30},{16,0},{1... | collective-permute-start | bytes 2838536 | tf_op jit(solution)/shard_map/ppermute | solution.py:401
  4.4 21.0 %collective-permute-start.2 = (bf16[528,896]{1,0:T(8,128)(2,1)S(1)}, bf16[528,896]{1,0:T(8,128)(2,1)S(1)}, u32[]{:S(2)}, u32[]{:S(2)}) collective-permute-start(bf16[528,896]{1,0:T(8,128)(2,1)S(1)} %pack.1.refs_0_), channel_id=1, source_target_pairs={{0,8},{2,18},{4,20},{6,14},{8,0},{10,26},{12,28},{14,6},{16,24},{1... | collective-permute-start | bytes 2838536 | tf_op jit(solution)/shard_map/ppermute | solution.py:406
  4.4 24.4 %collective-permute-start.5 = (bf16[528,896]{1,0:T(8,128)(2,1)S(1)}, bf16[528,896]{1,0:T(8,128)(2,1)}, u32[]{:S(2)}, u32[]{:S(2)}) collective-permute-start(bf16[528,896]{1,0:T(8,128)(2,1)S(1)} %pack.1.refs_0_), channel_id=1, source_target_pairs={{0,2},{2,0},{4,6},{6,4},{1,3},{3,1},{5,7},{7,5},{8,10},{10,8},{12,... | collective-permute-start | bytes 2838536 | tf_op jit(solution)/shard_map/ppermute | solution.py:345
  7.5 21.8 %collective-permute-start = (bf16[528,896]{1,0:T(8,128)(2,1)S(1)}, bf16[528,896]{1,0:T(8,128)(2,1)}, u32[]{:S(2)}, u32[]{:S(2)}) collective-permute-start(bf16[528,896]{1,0:T(8,128)(2,1)S(1)} %pack.1.refs_0_), channel_id=1, source_target_pairs={{0,8},{8,0},{16,24},{24,16},{1,9},{9,1},{17,25},{25,17},{2,10},{10... | collective-permute-start | bytes 2838536 | tf_op jit(solution)/shard_map/ppermute | solution.py:345
  7.5 21.4 %collective-permute-start.1 = (bf16[10,16,16]{2,1,0:T(8,128)(2,1)}, bf16[10,16,16]{2,1,0:T(8,128)(2,1)S(1)}, u32[]{:S(2)}, u32[]{:S(2)}) collective-permute-start(bf16[10,16,16]{2,1,0:T(8,128)(2,1)} %param.7), channel_id=1, source_target_pairs={{0,1},{1,0},{2,3},{3,2},{4,5},{5,4},{6,7},{7,6},{8,9},{9,8},{10,11... | collective-permute-start | bytes 15368 | tf_op jit(solution)/shard_map/ppermute | solution.py:345
  25.5 6.8 %collective-permute-start.4 = (bf16[528,896]{1,0:T(8,128)(2,1)S(1)}, bf16[528,896]{1,0:T(8,128)(2,1)S(1)}, u32[]{:S(2)}, u32[]{:S(2)}) collective-permute-start(bf16[528,896]{1,0:T(8,128)(2,1)S(1)} %broadcast_select_fusion), channel_id=1, source_target_pairs={{0,8},{8,0},{16,24},{24,16},{1,9},{9,1},{17,25},{25,17},{2,10},{10... | collective-permute-start | bytes 2838536 | tf_op jit(solution)/shard_map/ppermute | solution.py:345
  25.6 24.7 %collective-permute-start.8 = (bf16[528,896]{1,0:T(8,128)(2,1)S(1)}, bf16[528,896]{1,0:T(8,128)(2,1)S(1)}, u32[]{:S(2)}, u32[]{:S(2)}) collective-permute-start(bf16[528,896]{1,0:T(8,128)(2,1)S(1)} %collective-permute-done.3.refs_5_), channel_id=1, source_target_pairs={{0,2},{2,0},{4,6},{6,4},{1,3},{3,1},{5,7},{7,5},{8,10},{10,8},{12,... | collective-permute-start | bytes 2838536 | tf_op jit(solution)/shard_map/ppermute | solution.py:345
  28.8 13.0 %collective-permute-start.9 = (bf16[528,896]{1,0:T(8,128)(2,1)}, bf16[528,896]{1,0:T(8,128)(2,1)S(1)}, u32[]{:S(2)}, u32[]{:S(2)}) collective-permute-start(bf16[528,896]{1,0:T(8,128)(2,1)} %collective-permute-done.5.refs_4_.refs_0_), channel_id=1, source_target_pairs={{0,8},{8,0},{16,24},{24,16},{1,9},{9,1},{17,25},{25,17},{2,10},{10... | collective-permute-start | bytes 2838536 | tf_op jit(solution)/shard_map/ppermute | solution.py:345
  28.9 22.9 %collective-permute-start.7 = (bf16[528,896]{1,0:T(8,128)(2,1)}, bf16[528,896]{1,0:T(8,128)(2,1)S(1)}, u32[]{:S(2)}, u32[]{:S(2)}) collective-permute-start(bf16[528,896]{1,0:T(8,128)(2,1)} %collective-permute-done.5.refs_4_.refs_0_), channel_id=1, source_target_pairs={{0,8},{2,4},{4,2},{6,14},{8,0},{10,12},{12,10},{14,6},{16,24},{18,... | collective-permute-start | bytes 2838536 | tf_op jit(solution)/shard_map/ppermute | solution.py:436
  50.3 5.3 %collective-permute-start.10 = (bf16[528,896]{1,0:T(8,128)(2,1)S(1)}, bf16[528,896]{1,0:T(8,128)(2,1)S(1)}, u32[]{:S(2)}, u32[]{:S(2)}) collective-permute-start(bf16[528,896]{1,0:T(8,128)(2,1)S(1)} %collective-permute-done.8.refs_1_.refs_2_), channel_id=1, source_target_pairs={{0,8},{8,0},{16,24},{24,16},{1,9},{9,1},{17,25},{25,17},{2,10},{10... | collective-permute-start | bytes 2838536 | tf_op jit(solution)/shard_map/ppermute | solution.py:345
  50.3 14.5 %collective-permute-start.6 = (f32[3,10,32,128]{3,2,1,0:T(8,128)S(1)}, f32[3,10,32,128]{3,2,1,0:T(8,128)S(1)}, u32[]{:S(2)}, u32[]{:S(2)}) collective-permute-start(f32[3,10,32,128]{3,2,1,0:T(8,128)S(1)} %get-tuple-element.22), channel_id=1, source_target_pairs={{0,1},{1,0},{2,3},{3,2},{4,5},{5,4},{6,7},{7,6},{8,9},{9,8},{10,11... | collective-permute-start | bytes 1474568 | tf_op jit(solution)/shard_map/ppermute | solution.py:345
  55.6 17.3 %copy-start.1 = (s32[512]{0:T(512)S(1)}, s32[512]{0:T(512)}, u32[]{:S(2)}) copy-start(s32[512]{0:T(512)} %param.8) | copy-start | bytes 6148
  55.9 17.0 %collective-permute-start.12 = (f32[10,32,128]{2,1,0:T(8,128)S(1)}, f32[10,32,128]{2,1,0:T(8,128)S(1)}, u32[]{:S(2)}, u32[]{:S(2)}) collective-permute-start(f32[10,32,128]{2,1,0:T(8,128)S(1)} %get-tuple-element.28), channel_id=1, source_target_pairs={{0,2},{2,0},{4,6},{6,4},{1,3},{3,1},{5,7},{7,5},{8,10},{10,8},{12,... | collective-permute-start | bytes 491528 | tf_op jit(solution)/shard_map/ppermute | solution.py:345
  63.3 9.6 %collective-permute-start.11 = (f32[10,32,128]{2,1,0:T(8,128)S(1)}, f32[10,32,128]{2,1,0:T(8,128)S(1)}, u32[]{:S(2)}, u32[]{:S(2)}) collective-permute-start(f32[10,32,128]{2,1,0:T(8,128)S(1)} %get-tuple-element.29), channel_id=1, source_target_pairs={{0,1},{1,0},{2,3},{3,2},{4,5},{5,4},{6,7},{7,6},{8,9},{9,8},{10,11... | collective-permute-start | bytes 491528 | tf_op jit(solution)/shard_map/ppermute | solution.py:345
  64.6 8.3 %collective-permute-start.13 = (f32[10,32,128]{2,1,0:T(8,128)S(1)}, f32[10,32,128]{2,1,0:T(8,128)S(1)}, u32[]{:S(2)}, u32[]{:S(2)}) collective-permute-start(f32[10,32,128]{2,1,0:T(8,128)S(1)} %get-tuple-element.30), channel_id=1, source_target_pairs={{0,3},{1,2},{2,1},{3,0},{4,7},{5,6},{6,5},{7,4},{8,11},{9,10},{10,... | collective-permute-start | bytes 491528 | tf_op jit(solution)/shard_map/ppermute | solution.py:495

commit v4 on v3

v4 whole, which is shorter than its diff:
```python
import jax
import jax.numpy as jnp
from jax import lax
from jax.experimental import pallas as pl
from jax.experimental.pallas import tpu as pltpu
from jax.sharding import PartitionSpec as P

VMEM_LIMIT = 24 * 1024 * 1024
LANES = 128
NT = (((1,), (1,)), ((), ()))
NN = (((1,), (0,)), ((), ()))
TN = (((0,), (0,)), ((), ()))


def lookup_symmetry(occ_irreps, pair_list):
    labels = jnp.arange(occ_irreps.shape[0], dtype=jnp.int32)
    onehot = pair_list[:, :, None] == labels[None, None, :]
    picked = jnp.sum(jnp.where(onehot, occ_irreps[None, None, :], 0), axis=-1)
    return jnp.bitwise_xor(picked[:, 0], picked[:, 1])


def mask_amplitudes(amplitudes, win_irreps, symmetry):
    product = jnp.bitwise_xor(win_irreps[:, None], win_irreps[None, :])
    allowed = product[None, :, :] == symmetry[:, None, None]
    return jnp.where(allowed, amplitudes, jnp.zeros_like(amplitudes))


def gathered_body(factors, amplitudes, virt_irreps, win_irreps, occ_irreps, pair_list):
    per_device = factors.shape[1]
    n_rows = lax.axis_size("row")
    n_cols = lax.axis_size("col")
    block_a = per_device * n_cols
    slab = amplitudes.shape[0]
    symmetry = lookup_symmetry(occ_irreps, pair_list)
    own_symmetry = lax.dynamic_slice_in_dim(symmetry, lax.axis_index("pair") * slab, slab)
    every = lax.all_gather(amplitudes, "pair", axis=0, tiled=True)
    weights = mask_amplitudes(every, win_irreps, symmetry).astype(jnp.float32)
    n_fitting, _, width = factors.shape
    b_rows = lax.all_gather(factors, "row", axis=1, tiled=True)
    a_rows = lax.all_gather(factors, "col", axis=1, tiled=True)
    integral = lax.dot_general(
        a_rows.reshape(n_fitting, block_a * width),
        b_rows.reshape(n_fitting, n_rows * per_device * width),
        (((0,), (0,)), ((), ())),
        preferred_element_type=jnp.float32,
    )
    integral = integral.reshape(block_a, width, n_rows * per_device, width)
    part = jnp.einsum("acbd,pcd->pab", integral, weights, precision=lax.Precision.HIGHEST)
    full = lax.psum_scatter(part, "pair", scatter_dimension=0, tiled=True)
    full = full.reshape(slab, block_a, n_rows, per_device)
    a_labels = lax.dynamic_slice_in_dim(virt_irreps, lax.axis_index("row") * block_a, block_a)
    b_labels = lax.dynamic_slice_in_dim(
        virt_irreps.reshape(n_rows, -1), lax.axis_index("col") * per_device, per_device, 1
    )
    pair_sym = jnp.bitwise_xor(a_labels[:, None, None], b_labels[None, :, :])
    allowed = pair_sym[None, :, :, :] == own_symmetry[:, None, None, None]
    return jnp.where(allowed, full, 0.0)


def is_middle():
    col = lax.axis_index("col")
    return jnp.logical_or(col == 1, col == 2)


def one_hot(shape, wanted):
    first = lax.broadcasted_iota(jnp.int32, shape, 0)
    second = lax.broadcasted_iota(jnp.int32, shape, 1)
    return wanted(first, second).astype(jnp.bfloat16)


def multiply(left, right, dims):
    return lax.dot_general(left, right, dims, preferred_element_type=jnp.float32)


def pack_kernel(rest, own, out):
    n, n_fit = own.shape
    whole = n_fit - rest
    below = out.shape[0] - n
    turned = jnp.zeros((below, LANES), jnp.float32)
    for j in range(n // LANES):
        pick = one_hot((below, rest), lambda r, q: r == j * rest + q)
        turned = turned + multiply(pick, own[j * LANES : (j + 1) * LANES, whole:], NT)
    out[:n, :] = own[:, :whole]
    out[n:, :] = jnp.zeros((below, whole), jnp.bfloat16)
    out[n:, :LANES] = turned.astype(jnp.bfloat16)


class Rows:
    def __init__(self, packed, rows, tail, sems, rest, start=0):
        n, depth = rows.shape
        below = tail.shape[0]
        all_rows = packed.shape[0] - below
        self.copies = (
            pltpu.make_async_copy(packed.at[pl.ds(start, n)], rows.at[:, pl.ds(0, depth - LANES)], sems.at[0]),
            pltpu.make_async_copy(packed.at[pl.ds(all_rows, below), pl.ds(0, LANES)], tail, sems.at[1]),
        )
        self.rows, self.tail, self.rest, self.segment = rows, tail, rest, start // LANES

    def start(self):
        for copy in self.copies:
            copy.start()
        return self

    def ready(self):
        for copy in self.copies:
            copy.wait()
        rows, tail, rest = self.rows, self.tail, self.rest
        n, depth = rows.shape
        for j in range(n // LANES):
            base = (self.segment + j) * rest
            pick = one_hot(tail.shape, lambda r, q: jnp.logical_and(r == base + q, q < rest))
            back = multiply(tail[...], pick, TN).astype(jnp.bfloat16)
            rows[j * LANES : (j + 1) * LANES, depth - LANES :] = back
        return rows


def window_major(width, per_device):
    n = width * per_device
    into = lax.broadcasted_iota(jnp.int32, (n, 1), 0)
    wanted = lax.rem(into, per_device) * width + lax.div(into, per_device)
    return (lax.broadcasted_iota(jnp.int32, (n, n), 1) == wanted).astype(jnp.bfloat16)


def place_rows(panel, order, rows, k):
    width, _, per_device, depth = panel.shape
    half = per_device // 2
    for h in range(2):
        moved = multiply(order, rows[h * half * width : (h + 1) * half * width, :], NN).astype(panel.dtype)
        panel[:, pl.ds(k, 1), h * half : (h + 1) * half] = moved.reshape(width, 1, half, depth)


def contract_block(rows, panel, weights, split, sums, keep, send, to=0):
    width, n_rows, per_device, depth = panel.shape
    n_b = n_rows * per_device
    n_a = rows.shape[0] // width
    slab = keep.shape[0]
    n_p = weights.shape[0]

    def integrals(step, carry):
        two = panel[pl.ds(2 * step, 2)].reshape(2 * n_b, depth)
        acc = multiply(rows[...], two, NT)
        high = acc.astype(jnp.bfloat16)
        low = (acc - high.astype(jnp.float32)).astype(jnp.bfloat16)
        for j in range(2):
            lanes = slice(j * n_b, (j + 1) * n_b)
            split[:n_a, 0, pl.ds(2 * step + j, 1)] = high[:, lanes].reshape(n_a, 1, width, n_b)
            split[:n_a, 1, pl.ds(2 * step + j, 1)] = low[:, lanes].reshape(n_a, 1, width, n_b)
        return carry

    lax.fori_loop(0, width // 2, integrals, 0, unroll=True)

    def ladder(step, carry):
        two = [split[2 * step + j].reshape(2 * width * width, n_b) for j in range(2)]
        res = multiply(weights[...], jnp.concatenate(two, axis=1), NN)
        for j in range(2):
            sums[pl.ds((2 * step + j) * n_p, n_p), :] = res[:, j * n_b : (j + 1) * n_b]
        return carry

    lax.fori_loop(0, n_a // 2, ladder, 0, unroll=True)
    for p in range(slab):
        keep[p, to : to + n_a] = sums[pl.ds(p, n_a, stride=n_p), :]
        send[p, to : to + n_a] = sums[pl.ds(n_p // 2 + p, n_a, stride=n_p), :]


def pair_symmetry(occ, pairs, p):
    return jnp.bitwise_xor(occ[pairs[0, p]], occ[pairs[1, p]])


def weight_rows(amplitudes, win, occ, pairs, place, n_p):
    width = amplitudes.shape[1]
    n = amplitudes.shape[0]
    slab = n // width
    first = place * slab
    lanes = width * width
    spread = multiply(amplitudes[...], one_hot((width, lanes), lambda d, l: d == lax.div(l, width)), NN)
    c_of_row = lax.rem(lax.broadcasted_iota(jnp.int32, (n, lanes), 0), width)
    c_of_lane = lax.rem(lax.broadcasted_iota(jnp.int32, (n, lanes), 1), width)
    spread = jnp.where(c_of_row == c_of_lane, spread, 0.0).astype(jnp.bfloat16)
    gathered = multiply(one_hot((n_p, n), lambda p, r: p == lax.div(r, width)), spread, NN)
    lane = lax.broadcasted_iota(jnp.int32, (n_p, lanes), 1)
    row = lax.broadcasted_iota(jnp.int32, (n_p, lanes), 0)
    product = jnp.zeros((n_p, lanes), jnp.int32)
    for w in range(width):
        label = win[w]
        product = jnp.bitwise_xor(product, jnp.where(lax.div(lane, width) == w, label, 0))
        product = jnp.bitwise_xor(product, jnp.where(lax.rem(lane, width) == w, label, 0))
    wanted = jnp.full((n_p, lanes), -1, jnp.int32)
    for p in range(slab):
        wanted = jnp.where(row == p, pair_symmetry(occ, pairs, first + p), wanted)
    masked = jnp.where(product == wanted, gathered, 0.0).astype(jnp.bfloat16)
    return jnp.concatenate([masked, masked], axis=1)


def prep_kernel(rest, own, by_core, mine, others, win, occ, pairs, part, own_rows, weights, held, tails, sems):
    fetched = [
        Rows(src, dst, tails.at[i], sems.at[i], rest).start() for i, (src, dst) in enumerate(((own, own_rows), (by_core, held)))
    ]
    width, _, per_device, _ = part.shape
    n_p = weights.shape[0] // 2
    pair = lax.axis_index("pair")
    weights[:n_p] = weight_rows(mine, win, occ, pairs, pair, n_p)
    weights[n_p:] = weight_rows(others, win, occ, pairs, 1 - pair, n_p)
    order = window_major(width, per_device // 2)
    for i in range(2):
        place_rows(part, order, fetched[i].ready(), i)


def outer_kernel(rest, facing, by_core, by_x, part, held, tails, sems):
    @pl.when(is_middle())
    def _():
        width, _, per_device, _ = part.shape
        fetched = [Rows(src, held.at[i], tails.at[i], sems.at[i], rest).start() for i, src in enumerate((facing, by_core, by_x))]
        order = window_major(width, per_device // 2)
        for i in range(3):
            place_rows(part, order, fetched[i].ready(), i)


def fetch_part(part, panel, sems):
    row = lax.axis_index("row")
    copies = []
    for i in range(part.shape[1]):
        to = panel.at[:, pl.ds(jnp.bitwise_xor(row, i), 1)]
        copies.append(pltpu.make_async_copy(part.at[:, pl.ds(i, 1)], to, sems.at[i]))
        copies[-1].start()
    return copies


def early_kernel(
    rest, own_rows, part, by_x, by_both, facing, turned, weights,
    keep, send, panel_out, panel, held, tails, split, sums, sems, own_sem, part_sems, panel_sem,
):
    middle = is_middle()
    row = lax.axis_index("row")
    width, _, per_device, _ = panel.shape
    x_rows = Rows(by_x, held.at[0], tails.at[0], sems.at[0], rest)
    both = Rows(by_both, held.at[1], tails.at[1], sems.at[1], rest).start()

    @pl.when(middle)
    def _():
        x_rows.start()

    @pl.when(jnp.logical_not(middle))
    def _():
        Rows(turned, held.at[0], tails.at[0], sems.at[0], rest).start()

    parts = fetch_part(part, panel, part_sems)
    own = pltpu.make_async_copy(own_rows, held.at[2], own_sem)
    own.start()
    facing_rows = Rows(facing, held.at[3], tails.at[3], sems.at[3], rest).start()
    order = window_major(width, per_device // 2)
    for i, rows in enumerate((x_rows, both)):
        place_rows(panel, order, rows.ready(), jnp.bitwise_xor(row, 2 + i))
    for copy in parts:
        copy.wait()
    back = pltpu.make_async_copy(panel, panel_out, panel_sem)
    back.start()
    own.wait()
    facing_rows.ready()

    def block(s, carry):
        contract_block(held.at[2 + s], panel, weights, split, sums, keep.at[s], send.at[s])
        return carry

    lax.fori_loop(0, 2, block, 0)
    back.wait()


def middle_kernel(rest, turned, panel_in, weights, keep, send, panel, held, tail, split, sums, sems, panel_sem):
    @pl.when(is_middle())
    def _():
        copy_panel = pltpu.make_async_copy(panel_in, panel, panel_sem)
        copy_panel.start()
        Rows(turned, held, tail, sems, rest).start().ready()
        copy_panel.wait()
        contract_block(held, panel, weights, split, sums, keep, send)


def late_kernel(
    rest, far, passed, panel_in, weights, keep, send, panel, held, tail, split, sums, sems, panel_sem
):
    copy_panel = pltpu.make_async_copy(panel_in, panel, panel_sem)
    copy_panel.start()
    middle = is_middle()
    rows = Rows(far, held, tail, sems, rest)

    @pl.when(middle)
    def _():
        rows.start()

    @pl.when(jnp.logical_not(middle))
    def _():
        Rows(passed, held, tail, sems, rest).start()

    rows.ready()
    copy_panel.wait()
    contract_block(held, panel, weights, split, sums, keep, send)


def across_kernel(
    rest, far, part, by_both, weights, keep, send, panel, held, tails, split, sums, sems, part_sems
):
    @pl.when(is_middle())
    def _():
        fetched = [Rows(src, held.at[i], tails.at[i], sems.at[i], rest).start() for i, src in enumerate((by_both, far))]
        parts = fetch_part(part, panel, part_sems)
        width, _, per_device, _ = panel.shape
        row = lax.axis_index("row")
        place_rows(panel, window_major(width, per_device // 2), fetched[0].ready(), jnp.bitwise_xor(row, 3))
        rows = fetched[1].ready()
        for copy in parts:
            copy.wait()
        contract_block(rows, panel, weights, split, sums, keep, send)


def add_kernel(first, second, out):
    out[...] = first[...] + second[...]


def finish_kernel(
    virt, occ, pairs, keep_early, got_early, keep_middle, got_middle, keep_late, got_late,
    across, out, whole,
):
    row = lax.axis_index("row")
    col = lax.axis_index("col")
    middle = is_middle()
    lower = col < 2
    n_p, n_a, n_b = keep_late.shape
    planes = (col, jnp.bitwise_xor(col, 1), jnp.where(lower, 2, 1), jnp.where(lower, 3, 0))

    def place(s):
        return pl.ds(pl.multiple_of(planes[s] * n_a, n_a), n_a)

    for s in range(2):
        whole[:, place(s), :] = keep_early[s] + got_early[s]

    @pl.when(middle)
    def _():
        whole[:, place(2), :] = keep_middle[...] + got_middle[...]
        whole[:, place(3), :] = keep_late[...] + got_late[...]

    @pl.when(jnp.logical_not(middle))
    def _():
        whole[:, place(2), :] = keep_late[...] + got_late[...]
        whole[:, place(3), :] = across[...]

    n_rows, block_a = virt.shape
    spread = [jnp.broadcast_to(virt[k : k + 1, :], (n_a, block_a)) for k in range(n_rows)]
    lane = lax.broadcasted_iota(jnp.int32, (n_b, block_a), 1)
    place_b = lax.rem(lax.broadcasted_iota(jnp.int32, (n_b, block_a), 0), n_a) + col * n_a
    b_labels = jnp.sum(jnp.where(lane == place_b, jnp.concatenate(spread, axis=0), 0), axis=1, keepdims=True)
    pair_sym = jnp.bitwise_xor(b_labels, virt[pl.ds(row, 1), :])
    first = lax.axis_index("pair") * n_p
    for p in range(n_p):
        out[p] = jnp.where(pair_sym == pair_symmetry(occ, pairs, first + p), whole[p].T, 0.0)


def swap(array, axis, mask):
    size = lax.axis_size(axis)
    return lax.ppermute(array, axis, [(i, i ^ mask) for i in range(size)])


def staged_body(factors, amplitudes, virt_irreps, win_irreps, occ_irreps, pair_list):
    n_fit, per_device, width = factors.shape
    n_rows = lax.axis_size("row")
    n_cols = lax.axis_size("col")
    n_pair = lax.axis_size("pair")
    n_b = n_rows * per_device
    block_a = per_device * n_cols
    slab = amplitudes.shape[0]
    n = per_device * width
    half = n // 2
    rest = n_fit % LANES
    below = 16 * pl.cdiv(rest * (n // LANES), 16)
    depth = n_fit - rest + LANES
    n_p = 16 * pl.cdiv(slab, 16)

    anywhere = pl.BlockSpec(memory_space=pl.ANY)
    vmem = pl.BlockSpec(memory_space=pltpu.VMEM)
    smem = pl.BlockSpec(memory_space=pltpu.SMEM)

    def array(*shape, dtype=jnp.bfloat16):
        return jax.ShapeDtypeStruct(shape, dtype)

    def sums_of(*shape):
        return array(*shape, n_b, dtype=jnp.float32)

    def panel(count):
        return array(width, count, per_device, depth)

    def sems(*count):
        return pltpu.SemaphoreType.DMA(count)

    def rows(*shape):
        return pltpu.VMEM(shape + (depth,), jnp.bfloat16)

    def tails(*count):
        return pltpu.VMEM(count + (below, LANES), jnp.bfloat16)

    panel_scratch = pltpu.VMEM(panel(n_rows).shape, jnp.bfloat16)
    work = [
        pltpu.VMEM((per_device, 2, width, width, n_b), jnp.bfloat16),
        pltpu.VMEM((per_device * 2 * n_p, n_b), jnp.float32),
    ]

    def call(kernel, name, out_shape, in_specs, out_specs, scratch, n_blocks=None):
        estimate = None
        if n_blocks is not None:
            flops = int(20 * n_blocks * n * n_b * width * depth)
            estimate = pl.CostEstimate(flops=flops, bytes_accessed=8 * n * depth, transcendentals=0)
        return pl.pallas_call(
            kernel,
            out_shape=out_shape,
            in_specs=in_specs,
            out_specs=out_specs,
            scratch_shapes=scratch,
            compiler_params=pltpu.CompilerParams(vmem_limit_bytes=VMEM_LIMIT),
            cost_estimate=estimate,
            name=name,
        )

    def permute(x, to):
        pairs = [
            (r * n_cols + c, to_r * n_cols + to_c)
            for r in range(n_rows)
            for c in range(n_cols)
            for to_r, to_c in [to(r, c, c in (1, 2))]
        ]
        return lax.ppermute(x, ("row", "col"), pairs)

    def face(x):
        return permute(x, lambda r, c, middle: (r, c ^ 1))

    def turn(x):
        return permute(x, lambda r, c, middle: (r, 3 - c) if middle else (r ^ 2, c))

    def cross(x):
        return permute(x, lambda r, c, middle: (r, 3 - c) if middle else (r ^ 1, c))

    def along_x(x):
        return permute(x, lambda r, c, middle: (r ^ 2, c) if middle else (r ^ 1, c))

    def along_x_to_core(x):
        return permute(x, lambda r, c, middle: (r ^ 3, c) if middle else (r ^ 1, c))

    def core(x):
        return permute(x, lambda r, c, middle: (r ^ 1, c))

    def after(x, *others):
        return lax.optimization_barrier((x, *others))[0]

    own = call(
        lambda *refs: pack_kernel(rest, *refs), "pack", array(n + below, n_fit - rest), [vmem], vmem, []
    )(jnp.transpose(factors, (1, 2, 0)).reshape(n, n_fit))

    turned = turn(own)
    facing = face(own)
    by_x = along_x(own)
    by_core = core(own)
    others = swap(amplitudes, "pair", 1)

    pairs = jnp.transpose(pair_list)
    own_part, own_rows, weights = call(
        lambda *refs: prep_kernel(rest, *refs),
        "prep",
        (panel(2), array(n, depth), array(2 * n_p, 2 * width * width)),
        [anywhere] * 2 + [vmem] * 2 + [smem] * 3,
        (vmem,) * 3,
        [rows(n), tails(2), sems(2, 2)],
        1,
    )(
        own, by_core,
        amplitudes.reshape(slab * width, width), others.reshape(slab * width, width),
        win_irreps, occ_irreps, pairs,
    )

    passed = face(turned)
    far = cross(facing)
    facing_both = along_x_to_core(facing)
    x_rows = jnp.where(is_middle(), by_x, turned)
    by_both = core(x_rows)
    facing_core = core(facing)

    early = sums_of(2, slab, per_device)
    keep_early, send_early, own_panel = call(
        lambda *refs: early_kernel(rest, *refs),
        "early",
        (early, early, panel(n_rows)),
        [anywhere] * 6 + [vmem],
        (vmem, vmem, anywhere),
        [panel_scratch, rows(4, n), tails(4), *work, sems(4, 2), sems(), sems(2), sems()],
        2,
    )(own_rows, own_part, by_x, by_both, facing, turned, weights)
    got_early = swap(send_early, "pair", 1)

    late = sums_of(slab, per_device)
    keep_middle, send_middle = call(
        lambda *refs: middle_kernel(rest, *refs),
        "middle",
        (late, late),
        [anywhere] * 2 + [vmem],
        (vmem, vmem),
        [panel_scratch, rows(n), tails(), *work, sems(2), sems()],
        1,
    )(turned, own_panel, weights)
    got_middle = swap(send_middle, "pair", 1)
    outer_part = call(
        lambda *refs: outer_kernel(rest, *refs),
        "outer",
        panel(3),
        [anywhere] * 3,
        vmem,
        [rows(3, n), tails(3), sems(3, 2)],
        1,
    )(facing, after(facing_core, keep_middle), passed)
    keep_across, send_across = call(
        lambda *refs: across_kernel(rest, *refs),
        "across",
        (late, late),
        [anywhere] * 3 + [vmem],
        (vmem, vmem),
        [panel_scratch, rows(2, n), tails(2), *work, sems(2, 2), sems(3)],
        1,
    )(far, after(outer_part, got_early), facing_both, weights)
    got_across = swap(send_across, "pair", 1)
    keep_late, send_late = call(
        lambda *refs: late_kernel(rest, *refs),
        "late",
        (late, late),
        [anywhere] * 3 + [vmem],
        (vmem, vmem),
        [panel_scratch, rows(n), tails(), *work, sems(2), sems()],
        1,
    )(far, passed, after(own_panel, keep_across, got_middle), weights)
    got_late = swap(send_late, "pair", 1)

    across = face(call(add_kernel, "add", late, [vmem] * 2, vmem, [])(keep_across, got_across))

    out = call(
        finish_kernel,
        "finish",
        sums_of(slab, block_a),
        [vmem] + [smem] * 2 + [vmem] * 7,
        vmem,
        [pltpu.VMEM((slab, block_a, n_b), jnp.float32)],
    )(
        virt_irreps.reshape(n_rows, block_a), occ_irreps, pairs,
        keep_early, got_early, keep_middle, got_middle, keep_late, got_late, across,
    )
    return jnp.transpose(out.reshape(slab, n_rows, per_device, block_a), (0, 3, 1, 2))


def solution(mesh):
    staged = (mesh.shape["row"], mesh.shape["col"], mesh.shape["pair"]) == (4, 4, 2)
    body = staged_body if staged else gathered_body
    in_specs = (P("pair", ("row", "col"), None), P("pair", None, None), P(), P(), P(), P())
    out_specs = P("pair", "row", None, "col")
    return jax.shard_map(body, mesh=mesh, in_specs=in_specs, out_specs=out_specs, check_vma=False)
```

time: 74.8 us -> 71.2 us (0.952)
  Pallas kernels: 18.4 us -> 17 us
  waiting for transfers between devices: 32.9 us -> 31.7 us
  starting transfers between devices: 21.9 us -> 20.8 us
    ppermute x10 -> x5, waiting for transfers between devices: 16.6 us -> 3.75 us  [swap(): return lax.ppermute(array, axis, [(i, i ^ mask) for i in range(size)])]
    ppermute x10 -> x5, starting transfers between devices: 18.3 us -> 5.77 us  [swap(): return lax.ppermute(array, axis, [(i, i ^ mask) for i in range(size)])]
    ppermute x4 -> x10, waiting for transfers between devices: 16.3 us -> 27.9 us  [permute(): return lax.ppermute(x, ('row', 'col'), pairs)]
    ppermute x4 -> x10, starting transfers between devices: 3.55 us -> 15 us  [permute(): return lax.ppermute(x, ('row', 'col'), pairs)]
    pallas_call x7 -> x9, Pallas kernels: 18.4 us -> 17 us  [the longest x1 8.45 us: staged_body(): call(lambda *refs: early_kernel(rest, *refs), 'early', (early, early, pan...]
  transfers between devices with their start and end apart: 14 -> 15, of which waited for: 3 -> 5; matrix products, arithmetic and copies ran while one was open for 0% -> 0% of each run, Pallas kernels for 22% -> 21%
where the time goes in v4:
time: 71.2 us; the launch traced here: 71 us
  waiting for transfers between devices  31.7 us (45%)
  starting transfers between devices  20.8 us (29%)
  Pallas kernels  17 us (24%)
  local copies, waits for them, and re-layouts  1.27 us (2%)
    ppermute x10, waiting for transfers between devices, permute(): return lax.ppermute(x, ('row', 'col'), pairs)  27.9 us
    ppermute x10, starting transfers between devices, permute(): return lax.ppermute(x, ('row', 'col'), pairs)  15 us
    pallas_call x1, Pallas kernels, staged_body(): call(lambda *refs: early_kernel(rest, *refs), 'early', (early, early, pan...  8.45 us
    ppermute x5, starting transfers between devices, swap(): return lax.ppermute(array, axis, [(i, i ^ mask) for i in range(size)])  5.77 us
    ppermute x5, waiting for transfers between devices, swap(): return lax.ppermute(array, axis, [(i, i ^ mask) for i in range(size)])  3.75 us
    pallas_call x1, Pallas kernels, staged_body(): call(lambda *refs: late_kernel(rest, *refs), 'late', (late, late), [anywh...  3.74 us
    pallas_call x1, Pallas kernels, staged_body(): call(lambda *refs: prep_kernel(rest, *refs), 'prep', (panel(2), array(n,...  2.74 us
    pallas_call x1, Pallas kernels, staged_body(): call(finish_kernel, 'finish', sums_of(slab, block_a), [vmem] + [smem] * 2...  1.75 us
  transfers between devices with their start and end apart: 15, of which 5 were waited for; matrix products, arithmetic and copies ran while one was open for 0% of the time, Pallas kernels for 21%

profile of v4, /device:TPU:0, one launch (start us, length us, event | category | flops | bytes accessed | tf_op | source)
XLA Modules:
  0.0 71.0 jit_solution(4541560249278244149)
XLA Ops:
  0.0 1.2 %copy-done = bf16[900,32,16]{0,2,1:T(8,128)(2,1)S(1)} copy-done((bf16[900,32,16]{0,2,1:T(8,128)(2,1)S(1)}, bf16[900,32,16]{0,2,1:T(8,128)(2,1)}, u32[]{:S(2)}) %copy-start) | copy-done | bytes 921624
  1.3 0.2 pack.1.refs_0_
  1.4 0.5 collective-permute-start.2
  1.9 2.5 %collective-permute-start.3 = (bf16[528,896]{1,0:T(8,128)(2,1)S(1)}, bf16[528,896]{1,0:T(8,128)(2,1)S(1)}, u32[]{:S(2)}, u32[]{:S(2)}) collective-permute-start(bf16[528,896]{1,0:T(8,128)(2,1)S(1)} %pack.1.refs_0_), channel_id=1, source_target_pairs={{0,16},{2,4},{4,2},{6,22},{8,24},{10,12},{12,10},{14,30},{16,0},{1... | collective-permute-start | bytes 2838536 | tf_op jit(solution)/shard_map/ppermute | solution.py:428
  4.4 3.1 %collective-permute-start.5 = (bf16[528,896]{1,0:T(8,128)(2,1)S(1)}, bf16[528,896]{1,0:T(8,128)(2,1)}, u32[]{:S(2)}, u32[]{:S(2)}) collective-permute-start(bf16[528,896]{1,0:T(8,128)(2,1)S(1)} %pack.1.refs_0_), channel_id=1, source_target_pairs={{0,2},{2,0},{4,6},{6,4},{8,10},{10,8},{12,14},{14,12},{16,18},{18,... | collective-permute-start | bytes 2838536 | tf_op jit(solution)/shard_map/ppermute | solution.py:428
  7.5 1.5 %collective-permute-start.1 = (bf16[10,16,16]{2,1,0:T(8,128)(2,1)}, bf16[10,16,16]{2,1,0:T(8,128)(2,1)S(1)}, u32[]{:S(2)}, u32[]{:S(2)}) collective-permute-start(bf16[10,16,16]{2,1,0:T(8,128)(2,1)} %param.7), channel_id=1, source_target_pairs={{0,1},{1,0},{2,3},{3,2},{4,5},{5,4},{6,7},{7,6},{8,9},{9,8},{10,11... | collective-permute-start | bytes 15368 | tf_op jit(solution)/shard_map/ppermute | solution.py:359
  9.1 17.0 %collective-permute-done.3.refs_5_.refs_0_ = bf16[528,896]{1,0:T(8,128)(2,1)S(1)} collective-permute-done((bf16[528,896]{1,0:T(8,128)(2,1)S(1)}, bf16[528,896]{1,0:T(8,128)(2,1)S(1)}, u32[]{:S(2)}, u32[]{:S(2)}) %collective-permute-start.3) | collective-permute-done | bytes 946208 | tf_op jit(solution)/shard_map/ppermute | solution.py:428
  26.3 2.4 %collective-permute-start.9 = (bf16[528,896]{1,0:T(8,128)(2,1)S(1)}, bf16[528,896]{1,0:T(8,128)(2,1)S(1)}, u32[]{:S(2)}, u32[]{:S(2)}) collective-permute-start(bf16[528,896]{1,0:T(8,128)(2,1)S(1)} %collective-permute-done.3.refs_5_.refs_0_), channel_id=1, source_target_pairs={{0,2},{2,0},{4,6},{6,4},{8,10},{10,8},{12,14},{14,12},{16,18},{18,... | collective-permute-start | bytes 2838536 | tf_op jit(solution)/shard_map/ppermute | solution.py:428
  28.7 0.2 collective-permute-start.8
  28.9 0.3 collective-permute-start.10
  29.2 0.2 collective-permute-start.11
  29.4 2.7 %prep.1 = (bf16[16,2,32,1024]{3,2,1,0:T(8,128)(2,1)S(1)}, bf16[512,1024]{1,0:T(8,128)(2,1)S(1)}, bf16[32,512]{1,0:T(8,128)(2,1)S(1)}) custom-call(bf16[528,896]{1,0:T(8,128)(2,1)S(1)} %pack.1.refs_0_, bf16[528,896]{1,0:T(8,128)(2,1)} %collective-permute-done.refs_1_, bf16[160,16]{1,0:T(8,128)(2,1)S(1)} %bitcast.14, bf16[160,16]{1,0:T(8,128)(2,1)S(1)} %bitcast.15, ...), custom_call_target="tpu_custom_call" | custom-call | flops 21474836480 | bytes 4194304 | tf_op jit(solution)/shard_map/prep/pallas_call | solution.py:462
  32.2 8.5 %early.1 = (f32[2,10,32,128]{3,2,1,0:T(8,128)S(1)}, f32[2,10,32,128]{3,2,1,0:T(8,128)S(1)}, bf16[16,4,32,1024]{3,2,1,0:T(8,128)(2,1)S(1)}) custom-call(bf16[512,1024]{1,0:T(8,128)(2,1)S(1)} %get-tuple-element.20.refs_0_, bf16[16,2,32,1024]{3,2,1,0:T(8,128)(2,1)S(1)} %get-tuple-element.21.refs_1_, bf16[528,896]{1,0:T(8,128)(2,1)S(1)} %collective-permute-done.2.refs_2_, ...), custom_call_target="tpu_custom_call" | custom-call | flops 42949672960 | bytes 4194304 | tf_op jit(solution)/shard_map/early/pallas_call | solution.py:484
  40.6 1.6 %collective-permute-start.6 = (f32[2,10,32,128]{3,2,1,0:T(8,128)S(1)}, f32[2,10,32,128]{3,2,1,0:T(8,128)S(1)}, u32[]{:S(2)}, u32[]{:S(2)}) collective-permute-start(f32[2,10,32,128]{3,2,1,0:T(8,128)S(1)} %get-tuple-element.24), channel_id=1, source_target_pairs={{0,1},{1,0},{2,3},{3,2},{4,5},{5,4},{6,7},{7,6},{8,9},{9,8},{10,11... | collective-permute-start | bytes 983048 | tf_op jit(solution)/shard_map/ppermute | solution.py:359
  42.2 0.6 collective-permute-start.7
  42.8 7.4 %collective-permute-done.9.refs_2_.refs_1_ = bf16[528,896]{1,0:T(8,128)(2,1)S(1)} collective-permute-done((bf16[528,896]{1,0:T(8,128)(2,1)S(1)}, bf16[528,896]{1,0:T(8,128)(2,1)S(1)}, u32[]{:S(2)}, u32[]{:S(2)}) %collective-permute-start.9) | collective-permute-done | bytes 946208 | tf_op jit(solution)/shard_map/ppermute | solution.py:428
  50.3 0.9 %collective-permute-done.6.got_early = f32[2,10,32,128]{3,2,1,0:T(8,128)S(1)} collective-permute-done((f32[2,10,32,128]{3,2,1,0:T(8,128)S(1)}, f32[2,10,32,128]{3,2,1,0:T(8,128)S(1)}, u32[]{:S(2)}, u32[]{:S(2)}) %collective-permute-start.6) | collective-permute-done | bytes 327712 | tf_op jit(solution)/shard_map/ppermute | solution.py:359
  51.3 2.9 %collective-permute-done.7.got_middle = f32[10,32,128]{2,1,0:T(8,128)S(1)} collective-permute-done((f32[10,32,128]{2,1,0:T(8,128)S(1)}, f32[10,32,128]{2,1,0:T(8,128)S(1)}, u32[]{:S(2)}, u32[]{:S(2)}) %collective-permute-start.7) | collective-permute-done | bytes 163872 | tf_op jit(solution)/shard_map/ppermute | solution.py:359
  54.1 1.5 %collective-permute-start.13 = (f32[10,32,128]{2,1,0:T(8,128)S(1)}, f32[10,32,128]{2,1,0:T(8,128)S(1)}, u32[]{:S(2)}, u32[]{:S(2)}) collective-permute-start(f32[10,32,128]{2,1,0:T(8,128)S(1)} %get-tuple-element.34), channel_id=1, source_target_pairs={{0,1},{1,0},{2,3},{3,2},{4,5},{5,4},{6,7},{7,6},{8,9},{9,8},{10,11... | collective-permute-start | bytes 491528 | tf_op jit(solution)/shard_map/ppermute | solution.py:359
  55.7 3.7 %late.1 = (f32[10,32,128]{2,1,0:T(8,128)S(1)}, f32[10,32,128]{2,1,0:T(8,128)S(1)}) custom-call(bf16[528,896]{1,0:T(8,128)(2,1)S(1)} %collective-permute-done.8.refs_0_, bf16[528,896]{1,0:T(8,128)(2,1)S(1)} %collective-permute-done.9.refs_2_.refs_1_, bf16[16,4,32,1024]{3,2,1,0:T(8,128)(2,1)S(1)} %get-tuple-element.31.refs_1_.refs_2_, ...), custom_call_target="tpu_custom_call" | custom-call | flops 21474836480 | bytes 4194304 | tf_op jit(solution)/shard_map/late/pallas_call | solution.py:525
  59.4 0.6 collective-permute-start.12
  60.0 5.7 %collective-permute-start.14 = (f32[10,32,128]{2,1,0:T(8,128)S(1)}, f32[10,32,128]{2,1,0:T(8,128)S(1)}, u32[]{:S(2)}, u32[]{:S(2)}) collective-permute-start(f32[10,32,128]{2,1,0:T(8,128)S(1)} %add.1), channel_id=1, source_target_pairs={{0,2},{2,0},{4,6},{6,4},{8,10},{10,8},{12,14},{14,12},{16,18},{18,... | collective-permute-start | bytes 491528 | tf_op jit(solution)/shard_map/ppermute | solution.py:428
  65.7 3.5 %collective-permute-done.14.across = f32[10,32,128]{2,1,0:T(8,128)S(1)} collective-permute-done((f32[10,32,128]{2,1,0:T(8,128)S(1)}, f32[10,32,128]{2,1,0:T(8,128)S(1)}, u32[]{:S(2)}, u32[]{:S(2)}) %collective-permute-start.14) | collective-permute-done | bytes 163872 | tf_op jit(solution)/shard_map/ppermute | solution.py:428
  69.3 1.8 %finish.1 = f32[10,128,128]{2,1,0:T(8,128)} custom-call(s32[4,128]{1,0:T(4,128)S(1)} %bitcast.11, s32[120]{0:T(128)S(1)} %copy-done.3, s32[2,20]{1,0:T(2,128)S(1)} %bitcast.13, f32[2,10,32,128]{3,2,1,0:T(8,128)S(1)} %get-tuple-element.23.keep_early, f32[2,10,32,128]{3,2,1,0:T(8,128)S(1)} %collective-permute-done.6.got_early, ...), custom_call_target="tpu_custom_call" | custom-call | tf_op jit(solution)/shard_map/finish/pallas_call | solution.py:538
  (28 shorter events, 0.4 us)
Async XLA Ops:
  0.0 29.4 %copy-start.3 = (s32[120]{0:T(128)S(1)}, s32[120]{0:T(128)}, u32[]{:S(2)}) copy-start(s32[120]{0:T(128)} %occ.1) | copy-start | bytes 1444
  0.0 29.4 %copy-start.2 = (s32[20,2]{0,1:T(2,128)S(1)}, s32[20,2]{0,1:T(2,128)}, u32[]{:S(2)}) copy-start(s32[20,2]{0,1:T(2,128)} %param.11) | copy-start | bytes 484
  0.0 1.3 %copy-start = (bf16[900,32,16]{0,2,1:T(8,128)(2,1)S(1)}, bf16[900,32,16]{0,2,1:T(8,128)(2,1)}, u32[]{:S(2)}) copy-start(bf16[900,32,16]{0,2,1:T(8,128)(2,1)} %param.6) | copy-start | bytes 2764804
  1.3 28.1 %copy-start.4 = (bf16[10,16,16]{2,1,0:T(8,128)(2,1)S(1)}, bf16[10,16,16]{2,1,0:T(8,128)(2,1)}, u32[]{:S(2)}) copy-start(bf16[10,16,16]{2,1,0:T(8,128)(2,1)} %param.7) | copy-start | bytes 15364
  1.3 28.1 %copy-start.5 = (s32[16]{0:T(128)S(1)}, s32[16]{0:T(128)}, u32[]{:S(2)}) copy-start(s32[16]{0:T(128)} %refs_4_.1) | copy-start | bytes 196
  1.4 7.6 %collective-permute-start.2 = (bf16[528,896]{1,0:T(8,128)(2,1)S(1)}, bf16[528,896]{1,0:T(8,128)(2,1)S(1)}, u32[]{:S(2)}, u32[]{:S(2)}) collective-permute-start(bf16[528,896]{1,0:T(8,128)(2,1)S(1)} %pack.1.refs_0_), channel_id=1, source_target_pairs={{0,8},{2,18},{4,20},{6,14},{8,0},{10,26},{12,28},{14,6},{16,24},{1... | collective-permute-start | bytes 2838536 | tf_op jit(solution)/shard_map/ppermute | solution.py:428
  1.9 24.1 %collective-permute-start.3 = (bf16[528,896]{1,0:T(8,128)(2,1)S(1)}, bf16[528,896]{1,0:T(8,128)(2,1)S(1)}, u32[]{:S(2)}, u32[]{:S(2)}) collective-permute-start(bf16[528,896]{1,0:T(8,128)(2,1)S(1)} %pack.1.refs_0_), channel_id=1, source_target_pairs={{0,16},{2,4},{4,2},{6,22},{8,24},{10,12},{12,10},{14,30},{16,0},{1... | collective-permute-start | bytes 2838536 | tf_op jit(solution)/shard_map/ppermute | solution.py:428
  4.4 24.3 %collective-permute-start.5 = (bf16[528,896]{1,0:T(8,128)(2,1)S(1)}, bf16[528,896]{1,0:T(8,128)(2,1)}, u32[]{:S(2)}, u32[]{:S(2)}) collective-permute-start(bf16[528,896]{1,0:T(8,128)(2,1)S(1)} %pack.1.refs_0_), channel_id=1, source_target_pairs={{0,2},{2,0},{4,6},{6,4},{8,10},{10,8},{12,14},{14,12},{16,18},{18,... | collective-permute-start | bytes 2838536 | tf_op jit(solution)/shard_map/ppermute | solution.py:428
  7.5 21.7 %collective-permute-start = (bf16[528,896]{1,0:T(8,128)(2,1)S(1)}, bf16[528,896]{1,0:T(8,128)(2,1)}, u32[]{:S(2)}, u32[]{:S(2)}) collective-permute-start(bf16[528,896]{1,0:T(8,128)(2,1)S(1)} %pack.1.refs_0_), channel_id=1, source_target_pairs={{0,8},{2,10},{4,12},{6,14},{8,0},{10,2},{12,4},{14,6},{16,24},{18,... | collective-permute-start | bytes 2838536 | tf_op jit(solution)/shard_map/ppermute | solution.py:428
  7.5 21.3 %collective-permute-start.1 = (bf16[10,16,16]{2,1,0:T(8,128)(2,1)}, bf16[10,16,16]{2,1,0:T(8,128)(2,1)S(1)}, u32[]{:S(2)}, u32[]{:S(2)}) collective-permute-start(bf16[10,16,16]{2,1,0:T(8,128)(2,1)} %param.7), channel_id=1, source_target_pairs={{0,1},{1,0},{2,3},{3,2},{4,5},{5,4},{6,7},{7,6},{8,9},{9,8},{10,11... | collective-permute-start | bytes 15368 | tf_op jit(solution)/shard_map/ppermute | solution.py:359
  26.2 6.0 %collective-permute-start.4 = (bf16[528,896]{1,0:T(8,128)(2,1)S(1)}, bf16[528,896]{1,0:T(8,128)(2,1)S(1)}, u32[]{:S(2)}, u32[]{:S(2)}) collective-permute-start(bf16[528,896]{1,0:T(8,128)(2,1)S(1)} %broadcast_select_fusion), channel_id=1, source_target_pairs={{0,8},{2,10},{4,12},{6,14},{8,0},{10,2},{12,4},{14,6},{16,24},{18,... | collective-permute-start | bytes 2838536 | tf_op jit(solution)/shard_map/ppermute | solution.py:428
  26.3 24.0 %collective-permute-start.9 = (bf16[528,896]{1,0:T(8,128)(2,1)S(1)}, bf16[528,896]{1,0:T(8,128)(2,1)S(1)}, u32[]{:S(2)}, u32[]{:S(2)}) collective-permute-start(bf16[528,896]{1,0:T(8,128)(2,1)S(1)} %collective-permute-done.3.refs_5_.refs_0_), channel_id=1, source_target_pairs={{0,2},{2,0},{4,6},{6,4},{8,10},{10,8},{12,14},{14,12},{16,18},{18,... | collective-permute-start | bytes 2838536 | tf_op jit(solution)/shard_map/ppermute | solution.py:428
  28.7 22.5 %collective-permute-start.8 = (bf16[528,896]{1,0:T(8,128)(2,1)}, bf16[528,896]{1,0:T(8,128)(2,1)S(1)}, u32[]{:S(2)}, u32[]{:S(2)}) collective-permute-start(bf16[528,896]{1,0:T(8,128)(2,1)} %collective-permute-done.5.refs_4_.refs_0_), channel_id=1, source_target_pairs={{0,8},{2,4},{4,2},{6,14},{8,0},{10,12},{12,10},{14,6},{16,24},{18,... | collective-permute-start | bytes 2838536 | tf_op jit(solution)/shard_map/ppermute | solution.py:428
  28.9 13.4 %collective-permute-start.10 = (bf16[528,896]{1,0:T(8,128)(2,1)}, bf16[528,896]{1,0:T(8,128)(2,1)S(1)}, u32[]{:S(2)}, u32[]{:S(2)}) collective-permute-start(bf16[528,896]{1,0:T(8,128)(2,1)} %collective-permute-done.5.refs_4_.refs_0_), channel_id=1, source_target_pairs={{0,8},{2,10},{4,12},{6,14},{8,0},{10,2},{12,4},{14,6},{16,24},{18,... | collective-permute-start | bytes 2838536 | tf_op jit(solution)/shard_map/ppermute | solution.py:428
  29.2 22.0 %collective-permute-start.11 = (bf16[528,896]{1,0:T(8,128)(2,1)}, bf16[528,896]{1,0:T(8,128)(2,1)S(1)}, u32[]{:S(2)}, u32[]{:S(2)}) collective-permute-start(bf16[528,896]{1,0:T(8,128)(2,1)} %collective-permute-done.5.refs_4_.refs_0_), channel_id=1, source_target_pairs={{0,8},{2,26},{4,28},{6,14},{8,0},{10,18},{12,20},{14,6},{16,24},{1... | collective-permute-start | bytes 2838536 | tf_op jit(solution)/shard_map/ppermute | solution.py:428
  40.6 10.6 %collective-permute-start.6 = (f32[2,10,32,128]{3,2,1,0:T(8,128)S(1)}, f32[2,10,32,128]{3,2,1,0:T(8,128)S(1)}, u32[]{:S(2)}, u32[]{:S(2)}) collective-permute-start(f32[2,10,32,128]{3,2,1,0:T(8,128)S(1)} %get-tuple-element.24), channel_id=1, source_target_pairs={{0,1},{1,0},{2,3},{3,2},{4,5},{5,4},{6,7},{7,6},{8,9},{9,8},{10,11... | collective-permute-start | bytes 983048 | tf_op jit(solution)/shard_map/ppermute | solution.py:359
  42.2 11.9 %collective-permute-start.7 = (f32[10,32,128]{2,1,0:T(8,128)S(1)}, f32[10,32,128]{2,1,0:T(8,128)S(1)}, u32[]{:S(2)}, u32[]{:S(2)}) collective-permute-start(f32[10,32,128]{2,1,0:T(8,128)S(1)} %get-tuple-element.27), channel_id=1, source_target_pairs={{0,1},{1,0},{2,3},{3,2},{4,5},{5,4},{6,7},{7,6},{8,9},{9,8},{10,11... | collective-permute-start | bytes 491528 | tf_op jit(solution)/shard_map/ppermute | solution.py:359
  54.1 15.1 %copy-start.1 = (s32[512]{0:T(512)S(1)}, s32[512]{0:T(512)}, u32[]{:S(2)}) copy-start(s32[512]{0:T(512)} %param.8) | copy-start | bytes 6148
  54.1 5.8 %collective-permute-start.13 = (f32[10,32,128]{2,1,0:T(8,128)S(1)}, f32[10,32,128]{2,1,0:T(8,128)S(1)}, u32[]{:S(2)}, u32[]{:S(2)}) collective-permute-start(f32[10,32,128]{2,1,0:T(8,128)S(1)} %get-tuple-element.34), channel_id=1, source_target_pairs={{0,1},{1,0},{2,3},{3,2},{4,5},{5,4},{6,7},{7,6},{8,9},{9,8},{10,11... | collective-permute-start | bytes 491528 | tf_op jit(solution)/shard_map/ppermute | solution.py:359
  59.4 6.3 %collective-permute-start.12 = (f32[10,32,128]{2,1,0:T(8,128)S(1)}, f32[10,32,128]{2,1,0:T(8,128)S(1)}, u32[]{:S(2)}, u32[]{:S(2)}) collective-permute-start(f32[10,32,128]{2,1,0:T(8,128)S(1)} %get-tuple-element.33), channel_id=1, source_target_pairs={{0,1},{1,0},{2,3},{3,2},{4,5},{5,4},{6,7},{7,6},{8,9},{9,8},{10,11... | collective-permute-start | bytes 491528 | tf_op jit(solution)/shard_map/ppermute | solution.py:359
  60.0 9.3 %collective-permute-start.14 = (f32[10,32,128]{2,1,0:T(8,128)S(1)}, f32[10,32,128]{2,1,0:T(8,128)S(1)}, u32[]{:S(2)}, u32[]{:S(2)}) collective-permute-start(f32[10,32,128]{2,1,0:T(8,128)S(1)} %add.1), channel_id=1, source_target_pairs={{0,2},{2,0},{4,6},{6,4},{8,10},{10,8},{12,14},{14,12},{16,18},{18,... | collective-permute-start | bytes 491528 | tf_op jit(solution)/shard_map/ppermute | solution.py:428

commit v5 on v4

v5 whole, which is shorter than its diff:
```python
import jax
import jax.numpy as jnp
from jax import lax
from jax.experimental import pallas as pl
from jax.experimental.pallas import tpu as pltpu
from jax.sharding import PartitionSpec as P

VMEM_LIMIT = 16 * 1024 * 1024
LANES = 128
NT = (((1,), (1,)), ((), ()))
NN = (((1,), (0,)), ((), ()))
TN = (((0,), (0,)), ((), ()))


def lookup_symmetry(occ_irreps, pair_list):
    labels = jnp.arange(occ_irreps.shape[0], dtype=jnp.int32)
    onehot = pair_list[:, :, None] == labels[None, None, :]
    picked = jnp.sum(jnp.where(onehot, occ_irreps[None, None, :], 0), axis=-1)
    return jnp.bitwise_xor(picked[:, 0], picked[:, 1])


def mask_amplitudes(amplitudes, win_irreps, symmetry):
    product = jnp.bitwise_xor(win_irreps[:, None], win_irreps[None, :])
    allowed = product[None, :, :] == symmetry[:, None, None]
    return jnp.where(allowed, amplitudes, jnp.zeros_like(amplitudes))


def gathered_body(factors, amplitudes, virt_irreps, win_irreps, occ_irreps, pair_list):
    per_device = factors.shape[1]
    n_rows = lax.axis_size("row")
    n_cols = lax.axis_size("col")
    block_a = per_device * n_cols
    slab = amplitudes.shape[0]
    symmetry = lookup_symmetry(occ_irreps, pair_list)
    own_symmetry = lax.dynamic_slice_in_dim(symmetry, lax.axis_index("pair") * slab, slab)
    every = lax.all_gather(amplitudes, "pair", axis=0, tiled=True)
    weights = mask_amplitudes(every, win_irreps, symmetry).astype(jnp.float32)
    n_fitting, _, width = factors.shape
    b_rows = lax.all_gather(factors, "row", axis=1, tiled=True)
    a_rows = lax.all_gather(factors, "col", axis=1, tiled=True)
    integral = lax.dot_general(
        a_rows.reshape(n_fitting, block_a * width),
        b_rows.reshape(n_fitting, n_rows * per_device * width),
        (((0,), (0,)), ((), ())),
        preferred_element_type=jnp.float32,
    )
    integral = integral.reshape(block_a, width, n_rows * per_device, width)
    part = jnp.einsum("acbd,pcd->pab", integral, weights, precision=lax.Precision.HIGHEST)
    full = lax.psum_scatter(part, "pair", scatter_dimension=0, tiled=True)
    full = full.reshape(slab, block_a, n_rows, per_device)
    a_labels = lax.dynamic_slice_in_dim(virt_irreps, lax.axis_index("row") * block_a, block_a)
    b_labels = lax.dynamic_slice_in_dim(
        virt_irreps.reshape(n_rows, -1), lax.axis_index("col") * per_device, per_device, 1
    )
    pair_sym = jnp.bitwise_xor(a_labels[:, None, None], b_labels[None, :, :])
    allowed = pair_sym[None, :, :, :] == own_symmetry[:, None, None, None]
    return jnp.where(allowed, full, 0.0)


def is_middle():
    col = lax.axis_index("col")
    return jnp.logical_or(col == 1, col == 2)


def one_hot(shape, wanted):
    first = lax.broadcasted_iota(jnp.int32, shape, 0)
    second = lax.broadcasted_iota(jnp.int32, shape, 1)
    return wanted(first, second).astype(jnp.bfloat16)


def multiply(left, right, dims):
    return lax.dot_general(left, right, dims, preferred_element_type=jnp.float32)


def pack_kernel(rest, own, out):
    n, n_fit = own.shape
    whole = n_fit - rest
    above = out.shape[0] - n
    turned = jnp.zeros((above, LANES), jnp.float32)
    for j in range(n // LANES):
        pick = one_hot((above, rest), lambda r, q: r == j * rest + q)
        turned = turned + multiply(pick, own[j * LANES : (j + 1) * LANES, whole:], NT)
    out[:above, :] = jnp.zeros((above, whole), jnp.bfloat16)
    out[:above, :LANES] = turned.astype(jnp.bfloat16)
    out[above:, :] = own[:, :whole]


def unpack(pieces, packed, rows, rest, segment=0):
    n, depth = rows.shape
    whole = depth - LANES
    to = 0
    for piece, start, count in pieces:
        rows[to : to + count, :whole] = piece[start : start + count, :]
        to += count
    tail = packed[: packed.shape[0] % LANES, :LANES]
    for j in range(n // LANES):
        base = (segment + j) * rest
        pick = one_hot(tail.shape, lambda r, q: jnp.logical_and(r == base + q, q < rest))
        rows[j * LANES : (j + 1) * LANES, whole:] = multiply(tail, pick, TN).astype(jnp.bfloat16)


def unpack_all(packed, rows, rest):
    unpack([(packed, packed.shape[0] % LANES, rows.shape[0])], packed, rows, rest)


def unpack_cut(first, second, rows, rest):
    above = first.shape[0] % LANES
    unpack([(first, above, first.shape[0] - above), (second, 0, second.shape[0])], first, rows, rest)


def window_major(width, per_device):
    n = width * per_device
    into = lax.broadcasted_iota(jnp.int32, (n, 1), 0)
    wanted = lax.rem(into, per_device) * width + lax.div(into, per_device)
    return (lax.broadcasted_iota(jnp.int32, (n, n), 1) == wanted).astype(jnp.bfloat16)


def place_rows(part, order, rows, k):
    width, _, per_device, depth = part.shape
    half = per_device // 2
    for h in range(2):
        moved = multiply(order, rows[h * half * width : (h + 1) * half * width, :], NN).astype(part.dtype)
        part[:, k : k + 1, h * half : (h + 1) * half] = moved.reshape(width, 1, half, depth)


def contract_block(rows, parts, weights, split, sums, keep, send, to=0):
    width, _, per_device, depth = parts[0].shape
    n_b = sum(part.shape[1] for part in parts) * per_device
    n_a = rows.shape[0] // width
    slab = keep.shape[0]
    n_p = weights.shape[0]

    def integrals(step, carry):
        pieces = [part[2 * step + j].reshape(-1, depth) for j in range(2) for part in parts]
        acc = multiply(rows[...], jnp.concatenate(pieces, axis=0), NT)
        high = acc.astype(jnp.bfloat16)
        low = (acc - high.astype(jnp.float32)).astype(jnp.bfloat16)
        for j in range(2):
            lanes = slice(j * n_b, (j + 1) * n_b)
            split[:n_a, 0, pl.ds(2 * step + j, 1)] = high[:, lanes].reshape(n_a, 1, width, n_b)
            split[:n_a, 1, pl.ds(2 * step + j, 1)] = low[:, lanes].reshape(n_a, 1, width, n_b)
        return carry

    lax.fori_loop(0, width // 2, integrals, 0, unroll=True)

    def ladder(step, carry):
        two = [split[2 * step + j].reshape(2 * width * width, n_b) for j in range(2)]
        res = multiply(weights[...], jnp.concatenate(two, axis=1), NN)
        for j in range(2):
            sums[pl.ds((2 * step + j) * n_p, n_p), :] = res[:, j * n_b : (j + 1) * n_b]
        return carry

    lax.fori_loop(0, n_a // 2, ladder, 0, unroll=True)
    for p in range(slab):
        keep[p, to : to + n_a] = sums[pl.ds(p, n_a, stride=n_p), :]
        send[p, to : to + n_a] = sums[pl.ds(n_p // 2 + p, n_a, stride=n_p), :]


def pair_symmetry(occ, pairs, p):
    return jnp.bitwise_xor(occ[pairs[0, p]], occ[pairs[1, p]])


def weight_rows(amplitudes, win, occ, pairs, place, n_p):
    width = amplitudes.shape[1]
    n = amplitudes.shape[0]
    slab = n // width
    first = place * slab
    lanes = width * width
    spread = multiply(amplitudes[...], one_hot((width, lanes), lambda d, l: d == lax.div(l, width)), NN)
    c_of_row = lax.rem(lax.broadcasted_iota(jnp.int32, (n, lanes), 0), width)
    c_of_lane = lax.rem(lax.broadcasted_iota(jnp.int32, (n, lanes), 1), width)
    spread = jnp.where(c_of_row == c_of_lane, spread, 0.0).astype(jnp.bfloat16)
    gathered = multiply(one_hot((n_p, n), lambda p, r: p == lax.div(r, width)), spread, NN)
    lane = lax.broadcasted_iota(jnp.int32, (n_p, lanes), 1)
    row = lax.broadcasted_iota(jnp.int32, (n_p, lanes), 0)
    product = jnp.zeros((n_p, lanes), jnp.int32)
    for w in range(width):
        label = win[w]
        product = jnp.bitwise_xor(product, jnp.where(lax.div(lane, width) == w, label, 0))
        product = jnp.bitwise_xor(product, jnp.where(lax.rem(lane, width) == w, label, 0))
    wanted = jnp.full((n_p, lanes), -1, jnp.int32)
    for p in range(slab):
        wanted = jnp.where(row == p, pair_symmetry(occ, pairs, first + p), wanted)
    masked = jnp.where(product == wanted, gathered, 0.0).astype(jnp.bfloat16)
    return jnp.concatenate([masked, masked], axis=1)


def prep_kernel(rest, own, by_core, mine, others, win, occ, pairs, part, own_rows, weights, held):
    width, _, per_device, _ = part.shape
    n_p = weights.shape[0] // 2
    pair = lax.axis_index("pair")
    weights[:n_p] = weight_rows(mine, win, occ, pairs, pair, n_p)
    weights[n_p:] = weight_rows(others, win, occ, pairs, 1 - pair, n_p)
    order = window_major(width, per_device // 2)
    for i, (packed, rows) in enumerate(((own, own_rows), (by_core, held))):
        unpack_all(packed, rows, rest)
        place_rows(part, order, rows, i)


def early_kernel(
    rest, own_rows, own_part, by_x, by_both, facing, weights, keep, send, x_part, held, split, sums
):
    width, _, per_device, _ = x_part.shape
    order = window_major(width, per_device // 2)
    for i, packed in enumerate((by_x, by_both)):
        unpack_all(packed, held, rest)
        place_rows(x_part, order, held, i)
    parts = (own_part, x_part)
    contract_block(own_rows, parts, weights, split, sums, keep.at[0], send.at[0])
    unpack_all(facing, held, rest)
    contract_block(held, parts, weights, split, sums, keep.at[1], send.at[1])


def outer_x_kernel(rest, passed_first, x_second, part, held):
    @pl.when(is_middle())
    def _():
        width, _, per_device, _ = part.shape
        unpack_cut(passed_first, x_second, held, rest)
        place_rows(part, window_major(width, per_device // 2), held, 0)


def outer_own_kernel(rest, facing, by_core, part, held):
    @pl.when(is_middle())
    def _():
        width, _, per_device, _ = part.shape
        order = window_major(width, per_device // 2)
        for i, packed in enumerate((facing, by_core)):
            unpack_all(packed, held, rest)
            place_rows(part, order, held, i)


def middle_kernel(rest, turned, own_part, x_part, weights, keep, send, held, split, sums):
    @pl.when(is_middle())
    def _():
        unpack_all(turned, held, rest)
        contract_block(held, (own_part, x_part), weights, split, sums, keep, send)


def late_kernel(
    rest, far_first, far_second, passed_first, passed_second, own_part, x_part, weights,
    keep, send, held, split, sums,
):
    middle = is_middle()

    @pl.when(middle)
    def _():
        unpack_cut(far_first, far_second, held, rest)

    @pl.when(jnp.logical_not(middle))
    def _():
        unpack_cut(passed_first, passed_second, held, rest)

    contract_block(held, (own_part, x_part), weights, split, sums, keep, send)


def across_kernel(rest, part, far_first, far_second, own, x, both, weights, keep, send, held, split, sums):
    @pl.when(is_middle())
    def _():
        above = far_first.shape[0] % LANES
        n = far_first.shape[0] - above
        if part:
            unpack([(far_second, 0, far_second.shape[0])], far_first, held, rest, n // LANES)
        else:
            unpack([(far_first, above, n)], far_first, held, rest)
        contract_block(held, (own, x, both), weights, split, sums, keep, send)


def add_kernel(keep_first, got_first, keep_second, got_second, out):
    n = keep_first.shape[1]
    out[:, :n] = keep_first[...] + got_first[...]
    out[:, n:] = keep_second[...] + got_second[...]


def finish_kernel(
    virt, occ, pairs, keep_early, got_early, keep_middle, got_middle, keep_late, got_late, across, out, whole
):
    row = lax.axis_index("row")
    col = lax.axis_index("col")
    middle = is_middle()
    lower = col < 2
    n_p, n_a, n_b = across.shape
    planes = (col, jnp.bitwise_xor(col, 1), jnp.where(lower, 2, 1), jnp.where(lower, 3, 0))

    def place(s):
        return pl.ds(pl.multiple_of(planes[s] * n_a, n_a), n_a)

    for s in range(2):
        whole[:, place(s), :] = keep_early[s] + got_early[s]

    @pl.when(middle)
    def _():
        whole[:, place(2), :] = keep_middle[...] + got_middle[...]
        whole[:, place(3), :] = keep_late[...] + got_late[...]

    @pl.when(jnp.logical_not(middle))
    def _():
        whole[:, place(2), :] = keep_late[...] + got_late[...]
        whole[:, place(3), :] = across[...]

    n_rows, block_a = virt.shape
    rows = [jnp.bitwise_xor(row, i) for i in range(n_rows)]
    spread = [jnp.broadcast_to(virt[pl.ds(k, 1), :], (n_a, block_a)) for k in rows]
    lane = lax.broadcasted_iota(jnp.int32, (n_b, block_a), 1)
    place_b = lax.rem(lax.broadcasted_iota(jnp.int32, (n_b, 1), 0), n_a) + col * n_a
    b_labels = jnp.sum(jnp.where(lane == place_b, jnp.concatenate(spread, axis=0), 0), axis=1, keepdims=True)
    pair_sym = jnp.bitwise_xor(b_labels, virt[pl.ds(row, 1), :])
    first = lax.axis_index("pair") * n_p
    for p in range(n_p):
        masked = jnp.where(pair_sym == pair_symmetry(occ, pairs, first + p), whole[p].T, 0.0)
        for i, k in enumerate(rows):
            out[p, pl.ds(pl.multiple_of(k * n_a, n_a), n_a), :] = masked[i * n_a : (i + 1) * n_a]


def swap(array, axis, mask):
    size = lax.axis_size(axis)
    return lax.ppermute(array, axis, [(i, i ^ mask) for i in range(size)])


def staged_body(factors, amplitudes, virt_irreps, win_irreps, occ_irreps, pair_list):
    n_fit, per_device, width = factors.shape
    n_rows = lax.axis_size("row")
    n_cols = lax.axis_size("col")
    n_pair = lax.axis_size("pair")
    n_b = n_rows * per_device
    block_a = per_device * n_cols
    slab = amplitudes.shape[0]
    n = per_device * width
    rest = n_fit % LANES
    below = 16 * pl.cdiv(rest * (n // LANES), 16)
    depth = n_fit - rest + LANES
    n_p = 16 * pl.cdiv(slab, 16)

    vmem = pl.BlockSpec(memory_space=pltpu.VMEM)
    smem = pl.BlockSpec(memory_space=pltpu.SMEM)

    def array(*shape, dtype=jnp.bfloat16):
        return jax.ShapeDtypeStruct(shape, dtype)

    def sums_of(*shape):
        return array(*shape, n_b, dtype=jnp.float32)

    def panel(count):
        return array(width, count, per_device, depth)

    held = pltpu.VMEM((n, depth), jnp.bfloat16)
    work = [
        pltpu.VMEM((per_device, 2, width, width, n_b), jnp.bfloat16),
        pltpu.VMEM((per_device * 2 * n_p, n_b), jnp.float32),
    ]

    def call(kernel, name, out_shape, in_specs, out_specs, scratch, n_blocks=None):
        estimate = None
        if n_blocks is not None:
            flops = int(20 * n_blocks * n * n_b * width * depth)
            estimate = pl.CostEstimate(flops=flops, bytes_accessed=8 * n * depth, transcendentals=0)
        return pl.pallas_call(
            kernel,
            out_shape=out_shape,
            in_specs=in_specs,
            out_specs=out_specs,
            scratch_shapes=scratch,
            compiler_params=pltpu.CompilerParams(vmem_limit_bytes=VMEM_LIMIT),
            cost_estimate=estimate,
            name=name,
        )

    def permute(x, to):
        pairs = [
            (r * n_cols + c, to_r * n_cols + to_c)
            for r in range(n_rows)
            for c in range(n_cols)
            for to_r, to_c in [to(r, c, c in (1, 2))]
        ]
        return lax.ppermute(x, ("row", "col"), pairs)

    def face(x):
        return permute(x, lambda r, c, middle: (r, c ^ 1))

    def turn(x):
        return permute(x, lambda r, c, middle: (r, 3 - c) if middle else (r ^ 2, c))

    def cross(x):
        return permute(x, lambda r, c, middle: (r, 3 - c) if middle else (r ^ 1, c))

    def along_x(x):
        return permute(x, lambda r, c, middle: (r ^ 2, c) if middle else (r ^ 1, c))

    def core(x):
        return permute(x, lambda r, c, middle: (r ^ 1, c))

    def after(x, *others):
        return lax.optimization_barrier((x, *others))[0]

    own = call(
        lambda *refs: pack_kernel(rest, *refs), "pack", array(n + below, n_fit - rest), [vmem], vmem, []
    )(jnp.transpose(factors, (1, 2, 0)).reshape(n, n_fit))

    turned = turn(own)
    facing = face(own)
    by_x = along_x(own)
    by_core = core(own)
    others = swap(amplitudes, "pair", 1)

    pairs = jnp.transpose(pair_list)
    own_part, own_rows, weights = call(
        lambda *refs: prep_kernel(rest, *refs),
        "prep",
        (panel(2), array(n, depth), array(2 * n_p, 2 * width * width)),
        [vmem] * 4 + [smem] * 3,
        (vmem,) * 3,
        [held],
        1,
    )(
        own, by_core,
        amplitudes.reshape(slab * width, width), others.reshape(slab * width, width),
        win_irreps, occ_irreps, pairs,
    )

    def cut(x, where):
        return x[: below + where], x[below + where :]

    facing_first, facing_second = cut(facing, 3 * n // 4)
    turned_first, turned_second = cut(turned, n // 2)
    passed_first = face(turned_first)
    far_first = cross(facing_first)
    x_second = along_x(cut(facing, n // 2)[1])
    x_rows = jnp.where(is_middle(), by_x, turned)
    by_both = core(x_rows)
    facing_core = core(facing)

    own_panel = call(
        lambda *refs: outer_own_kernel(rest, *refs), "outer_own", panel(2), [vmem] * 2, vmem, [held], 0.2
    )(facing, facing_core)
    far_second = cross(after(facing_second, own_panel))
    passed_second = face(after(turned_second, own_panel))
    early = sums_of(2, slab, per_device)
    keep_early, send_early, x_part = call(
        lambda *refs: early_kernel(rest, *refs),
        "early",
        (early, early, panel(2)),
        [vmem] * 6,
        (vmem,) * 3,
        [held, *work],
        2,
    )(after(own_rows, own_panel), own_part, x_rows, by_both, facing, weights)
    got_early = swap(send_early, "pair", 1)

    x_panel = call(
        lambda *refs: outer_x_kernel(rest, *refs), "outer_x", panel(1), [vmem] * 2, vmem, [held], 0.0
    )(after(passed_first, keep_early), x_second)
    both_panel = core(x_panel)

    block = sums_of(slab, per_device)
    keep_middle, send_middle = call(
        lambda *refs: middle_kernel(rest, *refs), "middle", (block, block), [vmem] * 4, (vmem, vmem), [held, *work], 0.65
    )(turned, own_part, after(x_part, x_panel), weights)
    got_middle = swap(send_middle, "pair", 1)

    def across(part, both):
        count = (far_second if part else far_first).shape[0] // LANES * LANES
        sums = sums_of(slab, count // width)
        keep, send = call(
            lambda *refs: across_kernel(rest, part, *refs),
            "across",
            (sums, sums),
            [vmem] * 6,
            (vmem, vmem),
            [pltpu.VMEM((count, depth), jnp.bfloat16), *work],
            0.0,
        )(far_first, far_second if part else far_first, own_panel, x_panel, both, weights)
        return keep, send, swap(send, "pair", 1)

    keep_across, send_across, got_across = across(0, after(both_panel, keep_middle))
    keep_again, send_again, got_again = across(1, after(both_panel, keep_across, got_early))

    keep_late, send_late = call(
        lambda *refs: late_kernel(rest, *refs),
        "late",
        (block, block),
        [vmem] * 7,
        (vmem, vmem),
        [held, *work],
        0.1,
    )(far_first, far_second, passed_first, passed_second, own_part, after(x_part, keep_again, got_middle), weights)
    got_late = swap(send_late, "pair", 1)
    summed = call(add_kernel, "add", sums_of(slab, per_device), [vmem] * 4, vmem, [])(
        keep_across, got_across, keep_again, got_again
    )
    outwards = face(summed)

    out = call(
        finish_kernel,
        "finish",
        sums_of(slab, block_a),
        [vmem] + [smem] * 2 + [vmem] * 7,
        vmem,
        [pltpu.VMEM((slab, block_a, n_b), jnp.float32)],
    )(
        virt_irreps.reshape(n_rows, block_a), occ_irreps, pairs,
        keep_early, got_early, keep_middle, got_middle, keep_late, got_late, outwards,
    )
    return jnp.transpose(out.reshape(slab, n_rows, per_device, block_a), (0, 3, 1, 2))


def solution(mesh):
    staged = (mesh.shape["row"], mesh.shape["col"], mesh.shape["pair"]) == (4, 4, 2)
    body = staged_body if staged else gathered_body
    in_specs = (P("pair", ("row", "col"), None), P("pair", None, None), P(), P(), P(), P())
    out_specs = P("pair", "row", None, "col")
    return jax.shard_map(body, mesh=mesh, in_specs=in_specs, out_specs=out_specs, check_vma=False)
```

time: 71.2 us -> 69.3 us (0.973)
  starting transfers between devices: 20.8 us -> 24.4 us
  waiting for transfers between devices: 31.7 us -> 28.6 us
  Pallas kernels: 17 us -> 14.4 us
    ppermute x10 -> x13, waiting for transfers between devices: 27.9 us -> 19.6 us  [permute(): return lax.ppermute(x, ('row', 'col'), pairs)]
    ppermute x5 -> x6, waiting for transfers between devices: 3.75 us -> 9.01 us  [swap(): return lax.ppermute(array, axis, [(i, i ^ mask) for i in range(size)])]
    ppermute x5 -> x6, starting transfers between devices: 5.77 us -> 7.82 us  [swap(): return lax.ppermute(array, axis, [(i, i ^ mask) for i in range(size)])]
    pallas_call x1, Pallas kernels: 8.45 us -> 6.71 us  [staged_body(): call(lambda *refs: early_kernel(rest, *refs), 'early', (early, early, pan...]
    ppermute x10 -> x13, starting transfers between devices: 15 us -> 16.6 us  [permute(): return lax.ppermute(x, ('row', 'col'), pairs)]
    pallas_call x5 -> x7, Pallas kernels: 3.91 us -> 3.28 us  [the longest x1 3.26 us: staged_body(): call(lambda *refs: late_kernel(rest, *refs), 'late', (block, block), [vme...]
  transfers between devices with their start and end apart: 15 -> 19, of which waited for: 5 -> 7; matrix products, arithmetic and copies ran while one was open for 0% -> 0% of each run, Pallas kernels for 21% -> 18%
where the time goes in v5:
time: 69.3 us; the launch traced here: 69.1 us
  waiting for transfers between devices  28.6 us (41%)
  starting transfers between devices  24.4 us (35%)
  Pallas kernels  14.4 us (21%)
  local copies, waits for them, and re-layouts  1.45 us (2%)
    ppermute x13, waiting for transfers between devices, permute(): return lax.ppermute(x, ('row', 'col'), pairs)  19.6 us
    ppermute x13, starting transfers between devices, permute(): return lax.ppermute(x, ('row', 'col'), pairs)  16.6 us
    ppermute x6, waiting for transfers between devices, swap(): return lax.ppermute(array, axis, [(i, i ^ mask) for i in range(size)])  9.01 us
    ppermute x6, starting transfers between devices, swap(): return lax.ppermute(array, axis, [(i, i ^ mask) for i in range(size)])  7.82 us
    pallas_call x1, Pallas kernels, staged_body(): call(lambda *refs: early_kernel(rest, *refs), 'early', (early, early, pan...  6.71 us
    pallas_call x1, Pallas kernels, staged_body(): call(lambda *refs: late_kernel(rest, *refs), 'late', (block, block), [vme...  3.26 us
    pallas_call x1, Pallas kernels, staged_body(): call(lambda *refs: prep_kernel(rest, *refs), 'prep', (panel(2), array(n,...  2.44 us
    pallas_call x1, Pallas kernels, staged_body(): call(finish_kernel, 'finish', sums_of(slab, block_a), [vmem] + [smem] * 2...  1.76 us
  transfers between devices with their start and end apart: 19, of which 7 were waited for; matrix products, arithmetic and copies ran while one was open for 0% of the time, Pallas kernels for 18%

profile of v5, /device:TPU:0, one launch (start us, length us, event | category | flops | bytes accessed | tf_op | source)
XLA Modules:
  0.0 69.1 jit_solution(8296067606537831480)
XLA Ops:
  0.0 1.2 %copy-done = bf16[900,32,16]{0,2,1:T(8,128)(2,1)S(1)} copy-done((bf16[900,32,16]{0,2,1:T(8,128)(2,1)S(1)}, bf16[900,32,16]{0,2,1:T(8,128)(2,1)}, u32[]{:S(2)}) %copy-start) | copy-done | bytes 921624
  1.9 2.5 %collective-permute-start.5 = (bf16[528,896]{1,0:T(8,128)(2,1)S(1)}, bf16[528,896]{1,0:T(8,128)(2,1)S(1)}, u32[]{:S(2)}, u32[]{:S(2)}) collective-permute-start(bf16[528,896]{1,0:T(8,128)(2,1)S(1)} %pack.1.refs_0_), channel_id=1, source_target_pairs={{0,16},{2,4},{4,2},{6,22},{8,24},{10,12},{12,10},{14,30},{16,0},{1... | collective-permute-start | bytes 2838536 | tf_op jit(solution)/shard_map/ppermute | solution.py:374
  4.4 3.1 %collective-permute-start.2 = (bf16[528,896]{1,0:T(8,128)(2,1)S(1)}, bf16[528,896]{1,0:T(8,128)(2,1)S(1)}, u32[]{:S(2)}, u32[]{:S(2)}) collective-permute-start(bf16[528,896]{1,0:T(8,128)(2,1)S(1)} %pack.1.refs_0_), channel_id=1, source_target_pairs={{0,2},{2,0},{4,6},{6,4},{8,10},{10,8},{12,14},{14,12},{16,18},{18,... | collective-permute-start | bytes 2838536 | tf_op jit(solution)/shard_map/ppermute | solution.py:374
  7.5 1.5 %collective-permute-start.1 = (bf16[10,16,16]{2,1,0:T(8,128)(2,1)}, bf16[10,16,16]{2,1,0:T(8,128)(2,1)S(1)}, u32[]{:S(2)}, u32[]{:S(2)}) collective-permute-start(bf16[10,16,16]{2,1,0:T(8,128)(2,1)} %param.7), channel_id=1, source_target_pairs={{0,1},{1,0},{2,3},{3,2},{4,5},{5,4},{6,7},{7,6},{8,9},{9,8},{10,11... | collective-permute-start | bytes 15368 | tf_op jit(solution)/shard_map/ppermute | solution.py:316
  9.0 17.0 %collective-permute-done.5.refs_0_ = bf16[528,896]{1,0:T(8,128)(2,1)S(1)} collective-permute-done((bf16[528,896]{1,0:T(8,128)(2,1)S(1)}, bf16[528,896]{1,0:T(8,128)(2,1)S(1)}, u32[]{:S(2)}, u32[]{:S(2)}) %collective-permute-start.5) | collective-permute-done | bytes 946208 | tf_op jit(solution)/shard_map/ppermute | solution.py:374
  26.3 3.6 %collective-permute-start.8 = (bf16[272,896]{1,0:T(8,128)(2,1)S(1)}, bf16[272,896]{1,0:T(8,128)(2,1)S(1)}, u32[]{:S(2)}, u32[]{:S(2)}) collective-permute-start(bf16[272,896]{1,0:T(8,128)(2,1)S(1)} %slice.20), channel_id=1, source_target_pairs={{0,2},{2,0},{4,6},{6,4},{8,10},{10,8},{12,14},{14,12},{16,18},{18,... | collective-permute-start | bytes 1462280 | tf_op jit(solution)/shard_map/ppermute | solution.py:374
  30.9 2.4 %prep.1 = (bf16[16,2,32,1024]{3,2,1,0:T(8,128)(2,1)S(1)}, bf16[512,1024]{1,0:T(8,128)(2,1)S(1)}, bf16[32,512]{1,0:T(8,128)(2,1)S(1)}) custom-call(bf16[528,896]{1,0:T(8,128)(2,1)S(1)} %pack.1.refs_0_, bf16[528,896]{1,0:T(8,128)(2,1)} %collective-permute-done.refs_1_, bf16[160,16]{1,0:T(8,128)(2,1)S(1)} %bitcast.14, bf16[160,16]{1,0:T(8,128)(2,1)S(1)} %bitcast.15, ...), custom_call_target="tpu_custom_call" | custom-call | flops 21474836480 | bytes 4194304 | tf_op jit(solution)/shard_map/prep/pallas_call | solution.py:405
  33.4 0.8 %collective-permute-done.3.refs_1_ = bf16[528,896]{1,0:T(8,128)(2,1)S(1)} collective-permute-done((bf16[528,896]{1,0:T(8,128)(2,1)S(1)}, bf16[528,896]{1,0:T(8,128)(2,1)S(1)}, u32[]{:S(2)}, u32[]{:S(2)}) %collective-permute-start.3) | collective-permute-done | bytes 946208 | tf_op jit(solution)/shard_map/ppermute | solution.py:374
  34.2 6.7 %early.1 = (f32[2,10,32,128]{3,2,1,0:T(8,128)S(1)}, f32[2,10,32,128]{3,2,1,0:T(8,128)S(1)}, bf16[16,2,32,1024]{3,2,1,0:T(8,128)(2,1)S(1)}) custom-call(bf16[512,1024]{1,0:T(8,128)(2,1)S(1)} %get-tuple-element.28.refs_0_, bf16[16,2,32,1024]{3,2,1,0:T(8,128)(2,1)S(1)} %get-tuple-element.29.refs_1_.refs_4_, bf16[528,896]{1,0:T(8,128)(2,1)S(1)} %broadcast_select_fusion.refs_2_, ...), custom_call_target="tpu_custom_call" | custom-call | flops 42949672960 | bytes 4194304 | tf_op jit(solution)/shard_map/early/pallas_call | solution.py:437
  40.9 1.6 %collective-permute-start.7 = (f32[2,10,32,128]{3,2,1,0:T(8,128)S(1)}, f32[2,10,32,128]{3,2,1,0:T(8,128)S(1)}, u32[]{:S(2)}, u32[]{:S(2)}) collective-permute-start(f32[2,10,32,128]{3,2,1,0:T(8,128)S(1)} %get-tuple-element.32), channel_id=1, source_target_pairs={{0,1},{1,0},{2,3},{3,2},{4,5},{5,4},{6,7},{7,6},{8,9},{9,8},{10,11... | collective-permute-start | bytes 983048 | tf_op jit(solution)/shard_map/ppermute | solution.py:316
  42.5 0.5 collective-permute-start.12
  43.0 2.9 %collective-permute-start.13 = (bf16[256,896]{1,0:T(8,128)(2,1)S(1)}, bf16[256,896]{1,0:T(8,128)(2,1)S(1)}, u32[]{:S(2)}, u32[]{:S(2)}) collective-permute-start(bf16[256,896]{1,0:T(8,128)(2,1)S(1)} %slice.24), channel_id=1, source_target_pairs={{0,2},{2,0},{4,6},{6,4},{8,10},{10,8},{12,14},{14,12},{16,18},{18,... | collective-permute-start | bytes 1376264 | tf_op jit(solution)/shard_map/ppermute | solution.py:374
  45.9 1.3 %collective-permute-start.10 = (f32[10,32,128]{2,1,0:T(8,128)S(1)}, f32[10,32,128]{2,1,0:T(8,128)S(1)}, u32[]{:S(2)}, u32[]{:S(2)}) collective-permute-start(f32[10,32,128]{2,1,0:T(8,128)S(1)} %get-tuple-element.37), channel_id=1, source_target_pairs={{0,1},{1,0},{2,3},{3,2},{4,5},{5,4},{6,7},{7,6},{8,9},{9,8},{10,11... | collective-permute-start | bytes 491528 | tf_op jit(solution)/shard_map/ppermute | solution.py:316
  47.3 4.3 %collective-permute-done.7.got_early = f32[2,10,32,128]{3,2,1,0:T(8,128)S(1)} collective-permute-done((f32[2,10,32,128]{3,2,1,0:T(8,128)S(1)}, f32[2,10,32,128]{3,2,1,0:T(8,128)S(1)}, u32[]{:S(2)}, u32[]{:S(2)}) %collective-permute-start.7) | collective-permute-done | bytes 327712 | tf_op jit(solution)/shard_map/ppermute | solution.py:316
  51.5 2.8 %collective-permute-done.10.got_middle = f32[10,32,128]{2,1,0:T(8,128)S(1)} collective-permute-done((f32[10,32,128]{2,1,0:T(8,128)S(1)}, f32[10,32,128]{2,1,0:T(8,128)S(1)}, u32[]{:S(2)}, u32[]{:S(2)}) %collective-permute-start.10) | collective-permute-done | bytes 163872 | tf_op jit(solution)/shard_map/ppermute | solution.py:316
  54.3 1.5 %collective-permute-start.16 = (f32[10,24,128]{2,1,0:T(8,128)S(1)}, f32[10,24,128]{2,1,0:T(8,128)S(1)}, u32[]{:S(2)}, u32[]{:S(2)}) collective-permute-start(f32[10,24,128]{2,1,0:T(8,128)S(1)} %get-tuple-element.47), channel_id=1, source_target_pairs={{0,1},{1,0},{2,3},{3,2},{4,5},{5,4},{6,7},{7,6},{8,9},{9,8},{10,11... | collective-permute-start | bytes 368648 | tf_op jit(solution)/shard_map/ppermute | solution.py:316
  55.8 0.5 collective-permute-start.17
  56.4 0.5 collective-permute-done.13.refs_3_
  56.8 3.3 %late.1 = (f32[10,32,128]{2,1,0:T(8,128)S(1)}, f32[10,32,128]{2,1,0:T(8,128)S(1)}) custom-call(bf16[400,896]{1,0:T(8,128)(2,1)S(1)} %collective-permute-done.11.refs_0_.refs_1_, bf16[128,896]{1,0:T(8,128)(2,1)S(1)} %collective-permute-done.12.refs_1_, bf16[272,896]{1,0:T(8,128)(2,1)S(1)} %collective-permute-done.8.refs_0_.refs_2_, ...), custom_call_target="tpu_custom_call" | custom-call | flops 2147483648 | bytes 4194304 | tf_op jit(solution)/shard_map/late/pallas_call | solution.py:476
  60.1 1.3 %collective-permute-start.15 = (f32[10,32,128]{2,1,0:T(8,128)S(1)}, f32[10,32,128]{2,1,0:T(8,128)S(1)}, u32[]{:S(2)}, u32[]{:S(2)}) collective-permute-start(f32[10,32,128]{2,1,0:T(8,128)S(1)} %get-tuple-element.46), channel_id=1, source_target_pairs={{0,1},{1,0},{2,3},{3,2},{4,5},{5,4},{6,7},{7,6},{8,9},{9,8},{10,11... | collective-permute-start | bytes 491528 | tf_op jit(solution)/shard_map/ppermute | solution.py:316
  61.5 2.6 %collective-permute-start.18 = (f32[10,32,128]{2,1,0:T(8,128)S(1)}, f32[10,32,128]{2,1,0:T(8,128)S(1)}, u32[]{:S(2)}, u32[]{:S(2)}) collective-permute-start(f32[10,32,128]{2,1,0:T(8,128)S(1)} %add.1), channel_id=1, source_target_pairs={{0,2},{2,0},{4,6},{6,4},{8,10},{10,8},{12,14},{14,12},{16,18},{18,... | collective-permute-start | bytes 491528 | tf_op jit(solution)/shard_map/ppermute | solution.py:374
  64.0 2.0 %collective-permute-done.15.got_late = f32[10,32,128]{2,1,0:T(8,128)S(1)} collective-permute-done((f32[10,32,128]{2,1,0:T(8,128)S(1)}, f32[10,32,128]{2,1,0:T(8,128)S(1)}, u32[]{:S(2)}, u32[]{:S(2)}) %collective-permute-start.15) | collective-permute-done | bytes 163872 | tf_op jit(solution)/shard_map/ppermute | solution.py:316
  66.0 1.3 %collective-permute-done.18.across = f32[10,32,128]{2,1,0:T(8,128)S(1)} collective-permute-done((f32[10,32,128]{2,1,0:T(8,128)S(1)}, f32[10,32,128]{2,1,0:T(8,128)S(1)}, u32[]{:S(2)}, u32[]{:S(2)}) %collective-permute-start.18) | collective-permute-done | bytes 163872 | tf_op jit(solution)/shard_map/ppermute | solution.py:374
  67.3 1.8 %finish.1 = f32[10,128,128]{2,1,0:T(8,128)} custom-call(s32[4,128]{1,0:T(4,128)S(1)} %bitcast.11, s32[120]{0:T(128)S(1)} %copy-done.3, s32[2,20]{1,0:T(2,128)S(1)} %bitcast.13, f32[2,10,32,128]{3,2,1,0:T(8,128)S(1)} %get-tuple-element.31.keep_early, f32[2,10,32,128]{3,2,1,0:T(8,128)S(1)} %collective-permute-done.7.got_early, ...), custom_call_target="tpu_custom_call" | custom-call | tf_op jit(solution)/shard_map/finish/pallas_call | solution.py:491
  (43 shorter events, 2.0 us)
Async XLA Ops:
  1.4 7.6 %collective-permute-start.4 = (bf16[528,896]{1,0:T(8,128)(2,1)S(1)}, bf16[528,896]{1,0:T(8,128)(2,1)}, u32[]{:S(2)}, u32[]{:S(2)}) collective-permute-start(bf16[528,896]{1,0:T(8,128)(2,1)S(1)} %pack.1.refs_0_), channel_id=1, source_target_pairs={{0,8},{2,18},{4,20},{6,14},{8,0},{10,26},{12,28},{14,6},{16,24},{1... | collective-permute-start | bytes 2838536 | tf_op jit(solution)/shard_map/ppermute | solution.py:374
  1.9 24.1 %collective-permute-start.5 = (bf16[528,896]{1,0:T(8,128)(2,1)S(1)}, bf16[528,896]{1,0:T(8,128)(2,1)S(1)}, u32[]{:S(2)}, u32[]{:S(2)}) collective-permute-start(bf16[528,896]{1,0:T(8,128)(2,1)S(1)} %pack.1.refs_0_), channel_id=1, source_target_pairs={{0,16},{2,4},{4,2},{6,22},{8,24},{10,12},{12,10},{14,30},{16,0},{1... | collective-permute-start | bytes 2838536 | tf_op jit(solution)/shard_map/ppermute | solution.py:374
  4.4 25.5 %collective-permute-start.2 = (bf16[528,896]{1,0:T(8,128)(2,1)S(1)}, bf16[528,896]{1,0:T(8,128)(2,1)S(1)}, u32[]{:S(2)}, u32[]{:S(2)}) collective-permute-start(bf16[528,896]{1,0:T(8,128)(2,1)S(1)} %pack.1.refs_0_), channel_id=1, source_target_pairs={{0,2},{2,0},{4,6},{6,4},{8,10},{10,8},{12,14},{14,12},{16,18},{18,... | collective-permute-start | bytes 2838536 | tf_op jit(solution)/shard_map/ppermute | solution.py:374
  7.5 23.1 %collective-permute-start = (bf16[528,896]{1,0:T(8,128)(2,1)S(1)}, bf16[528,896]{1,0:T(8,128)(2,1)}, u32[]{:S(2)}, u32[]{:S(2)}) collective-permute-start(bf16[528,896]{1,0:T(8,128)(2,1)S(1)} %pack.1.refs_0_), channel_id=1, source_target_pairs={{0,8},{2,10},{4,12},{6,14},{8,0},{10,2},{12,4},{14,6},{16,24},{18,... | collective-permute-start | bytes 2838536 | tf_op jit(solution)/shard_map/ppermute | solution.py:374
  7.5 22.8 %collective-permute-start.1 = (bf16[10,16,16]{2,1,0:T(8,128)(2,1)}, bf16[10,16,16]{2,1,0:T(8,128)(2,1)S(1)}, u32[]{:S(2)}, u32[]{:S(2)}) collective-permute-start(bf16[10,16,16]{2,1,0:T(8,128)(2,1)} %param.7), channel_id=1, source_target_pairs={{0,1},{1,0},{2,3},{3,2},{4,5},{5,4},{6,7},{7,6},{8,9},{9,8},{10,11... | collective-permute-start | bytes 15368 | tf_op jit(solution)/shard_map/ppermute | solution.py:316
  26.1 4.8 %copy-start.2 = (s32[20,2]{0,1:T(2,128)S(1)}, s32[20,2]{0,1:T(2,128)}, u32[]{:S(2)}) copy-start(s32[20,2]{0,1:T(2,128)} %param.11) | copy-start | bytes 484
  26.1 4.8 %copy-start.3 = (s32[120]{0:T(128)S(1)}, s32[120]{0:T(128)}, u32[]{:S(2)}) copy-start(s32[120]{0:T(128)} %occ.1) | copy-start | bytes 1444
  26.1 4.7 %copy-start.4 = (bf16[10,16,16]{2,1,0:T(8,128)(2,1)S(1)}, bf16[10,16,16]{2,1,0:T(8,128)(2,1)}, u32[]{:S(2)}) copy-start(bf16[10,16,16]{2,1,0:T(8,128)(2,1)} %param.7) | copy-start | bytes 15364
  26.1 4.7 %copy-start.5 = (s32[16]{0:T(128)S(1)}, s32[16]{0:T(128)}, u32[]{:S(2)}) copy-start(s32[16]{0:T(128)} %refs_4_.1) | copy-start | bytes 196
  26.1 8.1 %collective-permute-start.6 = (bf16[528,896]{1,0:T(8,128)(2,1)S(1)}, bf16[528,896]{1,0:T(8,128)(2,1)S(1)}, u32[]{:S(2)}, u32[]{:S(2)}) collective-permute-start(bf16[528,896]{1,0:T(8,128)(2,1)S(1)} %broadcast_select_fusion.refs_2_), channel_id=1, source_target_pairs={{0,8},{2,10},{4,12},{6,14},{8,0},{10,2},{12,4},{14,6},{16,24},{18,... | collective-permute-start | bytes 2838536 | tf_op jit(solution)/shard_map/ppermute | solution.py:374
  26.3 16.2 %collective-permute-start.8 = (bf16[272,896]{1,0:T(8,128)(2,1)S(1)}, bf16[272,896]{1,0:T(8,128)(2,1)S(1)}, u32[]{:S(2)}, u32[]{:S(2)}) collective-permute-start(bf16[272,896]{1,0:T(8,128)(2,1)S(1)} %slice.20), channel_id=1, source_target_pairs={{0,2},{2,0},{4,6},{6,4},{8,10},{10,8},{12,14},{14,12},{16,18},{18,... | collective-permute-start | bytes 1462280 | tf_op jit(solution)/shard_map/ppermute | solution.py:374
  29.9 12.6 %collective-permute-start.9 = (bf16[256,896]{1,0:T(8,128)(2,1)S(1)}, bf16[256,896]{1,0:T(8,128)(2,1)S(1)}, u32[]{:S(2)}, u32[]{:S(2)}) collective-permute-start(bf16[256,896]{1,0:T(8,128)(2,1)S(1)} %slice.21), channel_id=1, source_target_pairs={{0,8},{2,18},{4,20},{6,14},{8,0},{10,26},{12,28},{14,6},{16,24},{1... | collective-permute-start | bytes 1376264 | tf_op jit(solution)/shard_map/ppermute | solution.py:374
  30.3 17.0 %collective-permute-start.11 = (bf16[400,896]{1,0:T(8,128)(2,1)S(1)}, bf16[400,896]{1,0:T(8,128)(2,1)S(1)}, u32[]{:S(2)}, u32[]{:S(2)}) collective-permute-start(bf16[400,896]{1,0:T(8,128)(2,1)S(1)} %slice.22), channel_id=1, source_target_pairs={{0,8},{2,4},{4,2},{6,14},{8,0},{10,12},{12,10},{14,6},{16,24},{18,... | collective-permute-start | bytes 2150408 | tf_op jit(solution)/shard_map/ppermute | solution.py:374
  30.7 3.5 %collective-permute-start.3 = (bf16[528,896]{1,0:T(8,128)(2,1)S(1)}, bf16[528,896]{1,0:T(8,128)(2,1)S(1)}, u32[]{:S(2)}, u32[]{:S(2)}) collective-permute-start(bf16[528,896]{1,0:T(8,128)(2,1)S(1)} %collective-permute-done.2.refs_0_.refs_4_), channel_id=1, source_target_pairs={{0,8},{2,10},{4,12},{6,14},{8,0},{10,2},{12,4},{14,6},{16,24},{18,... | collective-permute-start | bytes 2838536 | tf_op jit(solution)/shard_map/ppermute | solution.py:374
  40.9 10.6 %collective-permute-start.7 = (f32[2,10,32,128]{3,2,1,0:T(8,128)S(1)}, f32[2,10,32,128]{3,2,1,0:T(8,128)S(1)}, u32[]{:S(2)}, u32[]{:S(2)}) collective-permute-start(f32[2,10,32,128]{3,2,1,0:T(8,128)S(1)} %get-tuple-element.32), channel_id=1, source_target_pairs={{0,1},{1,0},{2,3},{3,2},{4,5},{5,4},{6,7},{7,6},{8,9},{9,8},{10,11... | collective-permute-start | bytes 983048 | tf_op jit(solution)/shard_map/ppermute | solution.py:316
  42.5 3.4 %collective-permute-start.14 = (bf16[16,1,32,1024]{3,2,1,0:T(8,128)(2,1)S(1)}, bf16[16,1,32,1024]{3,2,1,0:T(8,128)(2,1)S(1)}, u32[]{:S(2)}, u32[]{:S(2)}) collective-permute-start(bf16[16,1,32,1024]{3,2,1,0:T(8,128)(2,1)S(1)} %outer_x.1.refs_3_), channel_id=1, source_target_pairs={{0,8},{2,10},{4,12},{6,14},{8,0},{10,2},{12,4},{14,6},{16,24},{18,... | collective-permute-start | bytes 3145736 | tf_op jit(solution)/shard_map/ppermute | solution.py:374
  42.5 9.0 %collective-permute-start.12 = (bf16[128,896]{1,0:T(8,128)(2,1)S(1)}, bf16[128,896]{1,0:T(8,128)(2,1)S(1)}, u32[]{:S(2)}, u32[]{:S(2)}) collective-permute-start(bf16[128,896]{1,0:T(8,128)(2,1)S(1)} %slice.23), channel_id=1, source_target_pairs={{0,8},{2,4},{4,2},{6,14},{8,0},{10,12},{12,10},{14,6},{16,24},{18,... | collective-permute-start | bytes 688136 | tf_op jit(solution)/shard_map/ppermute | solution.py:374
  43.0 13.8 %collective-permute-start.13 = (bf16[256,896]{1,0:T(8,128)(2,1)S(1)}, bf16[256,896]{1,0:T(8,128)(2,1)S(1)}, u32[]{:S(2)}, u32[]{:S(2)}) collective-permute-start(bf16[256,896]{1,0:T(8,128)(2,1)S(1)} %slice.24), channel_id=1, source_target_pairs={{0,2},{2,0},{4,6},{6,4},{8,10},{10,8},{12,14},{14,12},{16,18},{18,... | collective-permute-start | bytes 1376264 | tf_op jit(solution)/shard_map/ppermute | solution.py:374
  45.9 8.4 %collective-permute-start.10 = (f32[10,32,128]{2,1,0:T(8,128)S(1)}, f32[10,32,128]{2,1,0:T(8,128)S(1)}, u32[]{:S(2)}, u32[]{:S(2)}) collective-permute-start(f32[10,32,128]{2,1,0:T(8,128)S(1)} %get-tuple-element.37), channel_id=1, source_target_pairs={{0,1},{1,0},{2,3},{3,2},{4,5},{5,4},{6,7},{7,6},{8,9},{9,8},{10,11... | collective-permute-start | bytes 491528 | tf_op jit(solution)/shard_map/ppermute | solution.py:316
  54.3 7.1 %collective-permute-start.16 = (f32[10,24,128]{2,1,0:T(8,128)S(1)}, f32[10,24,128]{2,1,0:T(8,128)S(1)}, u32[]{:S(2)}, u32[]{:S(2)}) collective-permute-start(f32[10,24,128]{2,1,0:T(8,128)S(1)} %get-tuple-element.47), channel_id=1, source_target_pairs={{0,1},{1,0},{2,3},{3,2},{4,5},{5,4},{6,7},{7,6},{8,9},{9,8},{10,11... | collective-permute-start | bytes 368648 | tf_op jit(solution)/shard_map/ppermute | solution.py:316
  55.8 11.5 %copy-start.1 = (s32[512]{0:T(512)S(1)}, s32[512]{0:T(512)}, u32[]{:S(2)}) copy-start(s32[512]{0:T(512)} %param.8) | copy-start | bytes 6148
  55.8 5.6 %collective-permute-start.17 = (f32[10,8,128]{2,1,0:T(8,128)S(1)}, f32[10,8,128]{2,1,0:T(8,128)S(1)}, u32[]{:S(2)}, u32[]{:S(2)}) collective-permute-start(f32[10,8,128]{2,1,0:T(8,128)S(1)} %get-tuple-element.48), channel_id=1, source_target_pairs={{0,1},{1,0},{2,3},{3,2},{4,5},{5,4},{6,7},{7,6},{8,9},{9,8},{10,11... | collective-permute-start | bytes 122888 | tf_op jit(solution)/shard_map/ppermute | solution.py:316
  60.1 5.9 %collective-permute-start.15 = (f32[10,32,128]{2,1,0:T(8,128)S(1)}, f32[10,32,128]{2,1,0:T(8,128)S(1)}, u32[]{:S(2)}, u32[]{:S(2)}) collective-permute-start(f32[10,32,128]{2,1,0:T(8,128)S(1)} %get-tuple-element.46), channel_id=1, source_target_pairs={{0,1},{1,0},{2,3},{3,2},{4,5},{5,4},{6,7},{7,6},{8,9},{9,8},{10,11... | collective-permute-start | bytes 491528 | tf_op jit(solution)/shard_map/ppermute | solution.py:316
  61.5 5.9 %collective-permute-start.18 = (f32[10,32,128]{2,1,0:T(8,128)S(1)}, f32[10,32,128]{2,1,0:T(8,128)S(1)}, u32[]{:S(2)}, u32[]{:S(2)}) collective-permute-start(f32[10,32,128]{2,1,0:T(8,128)S(1)} %add.1), channel_id=1, source_target_pairs={{0,2},{2,0},{4,6},{6,4},{8,10},{10,8},{12,14},{14,12},{16,18},{18,... | collective-permute-start | bytes 491528 | tf_op jit(solution)/shard_map/ppermute | solution.py:374
  (1 other events, 1.2 us)

commit v6 on v5

--- a/solution.py
+++ b/solution.py
@@ -211,6 +211,18 @@
     contract_block(held, parts, weights, split, sums, keep.at[1], send.at[1])
 
 
+def pick_kernel(by_x, turned, out):
+    middle = is_middle()
+
+    @pl.when(middle)
+    def _():
+        out[...] = by_x[...]
+
+    @pl.when(jnp.logical_not(middle))
+    def _():
+        out[...] = turned[...]
+
+
 def outer_x_kernel(rest, passed_first, x_second, part, held):
     @pl.when(is_middle())
     def _():
@@ -236,39 +248,65 @@
         contract_block(held, (own_part, x_part), weights, split, sums, keep, send)
 
 
-def late_kernel(
-    rest, far_first, far_second, passed_first, passed_second, own_part, x_part, weights,
-    keep, send, held, split, sums,
+def late_near_kernel(
+    rest, far_first, far_second, passed_first, own_part, x_part, weights, keep, send, held, split, sums
 ):
     middle = is_middle()
+    parts = (own_part, x_part)
 
     @pl.when(middle)
     def _():
         unpack_cut(far_first, far_second, held, rest)
+        contract_block(held, parts, weights, split, sums, keep, send)
 
     @pl.when(jnp.logical_not(middle))
     def _():
-        unpack_cut(passed_first, passed_second, held, rest)
-
-    contract_block(held, (own_part, x_part), weights, split, sums, keep, send)
-
-
-def across_kernel(rest, part, far_first, far_second, own, x, both, weights, keep, send, held, split, sums):
+        above = passed_first.shape[0] % LANES
+        n = passed_first.shape[0] - above
+        rows = held.at[pl.ds(0, n)]
+        unpack([(passed_first, above, n)], passed_first, rows, rest)
+        contract_block(rows, parts, weights, split, sums, keep, send)
+
+
+def late_last_kernel(
+    rest, passed_first, passed_second, keep_near, send_near, own_part, x_part, weights, keep, send, held, split, sums
+):
+    keep[...] = keep_near[...]
+    send[...] = send_near[...]
+
+    @pl.when(jnp.logical_not(is_middle()))
+    def _():
+        n = passed_second.shape[0]
+        segment = (passed_first.shape[0] - passed_first.shape[0] % LANES) // LANES
+        rows = held.at[pl.ds(0, n)]
+        unpack([(passed_second, 0, n)], passed_first, rows, rest, segment)
+        to = keep.shape[1] - n // own_part.shape[0]
+        contract_block(rows, (own_part, x_part), weights, split, sums, keep, send, to)
+
+
+def across_first_kernel(rest, far_first, own, x, both, weights, keep, send, held, split, sums):
     @pl.when(is_middle())
     def _():
+        unpack_all(far_first, held, rest)
+        contract_block(held, (own, x, both), weights, split, sums, keep, send)
+
+
+def across_second_kernel(
+    rest, far_first, far_second, own, x, both, weights, keep_first, send_first, keep, send, held, split, sums
+):
+    @pl.when(is_middle())
+    def _():
+        n_a = keep_first.shape[1]
+        keep[:, :n_a] = keep_first[...]
+        send[:, :n_a] = send_first[...]
         above = far_first.shape[0] % LANES
-        n = far_first.shape[0] - above
-        if part:
-            unpack([(far_second, 0, far_second.shape[0])], far_first, held, rest, n // LANES)
-        else:
-            unpack([(far_first, above, n)], far_first, held, rest)
-        contract_block(held, (own, x, both), weights, split, sums, keep, send)
-
-
-def add_kernel(keep_first, got_first, keep_second, got_second, out):
-    n = keep_first.shape[1]
-    out[:, :n] = keep_first[...] + got_first[...]
-    out[:, n:] = keep_second[...] + got_second[...]
+        segment = (far_first.shape[0] - above) // LANES
+        unpack([(far_second, 0, far_second.shape[0])], far_first, held, rest, segment)
+        contract_block(held, (own, x, both), weights, split, sums, keep, send, n_a)
+
+
+def add_kernel(keep, got, out):
+    out[...] = keep[...] + got[...]
 
 
 def finish_kernel(
@@ -424,12 +462,12 @@
     passed_first = face(turned_first)
     far_first = cross(facing_first)
     x_second = along_x(cut(facing, n // 2)[1])
-    x_rows = jnp.where(is_middle(), by_x, turned)
+    x_rows = call(pick_kernel, "pick", array(n + below, n_fit - rest), [vmem] * 2, vmem, [])(by_x, turned)
     by_both = core(x_rows)
     facing_core = core(facing)
 
     own_panel = call(
-        lambda *refs: outer_own_kernel(rest, *refs), "outer_own", panel(2), [vmem] * 2, vmem, [held], 0.2
+        lambda *refs: outer_own_kernel(rest, *refs), "outer_own", panel(2), [vmem] * 2, vmem, [held], 0.0
     )(facing, facing_core)
     far_second = cross(after(facing_second, own_panel))
     passed_second = face(after(turned_second, own_panel))
@@ -441,7 +479,7 @@
         [vmem] * 6,
         (vmem,) * 3,
         [held, *work],
-        2,
+        0.1,
     )(after(own_rows, own_panel), own_part, x_rows, by_both, facing, weights)
     got_early = swap(send_early, "pair", 1)
 
@@ -456,36 +494,50 @@
     )(turned, own_part, after(x_part, x_panel), weights)
     got_middle = swap(send_middle, "pair", 1)
 
-    def across(part, both):
-        count = (far_second if part else far_first).shape[0] // LANES * LANES
-        sums = sums_of(slab, count // width)
-        keep, send = call(
-            lambda *refs: across_kernel(rest, part, *refs),
-            "across",
-            (sums, sums),
-            [vmem] * 6,
-            (vmem, vmem),
-            [pltpu.VMEM((count, depth), jnp.bfloat16), *work],
-            0.0,
-        )(far_first, far_second if part else far_first, own_panel, x_panel, both, weights)
-        return keep, send, swap(send, "pair", 1)
-
-    keep_across, send_across, got_across = across(0, after(both_panel, keep_middle))
-    keep_again, send_again, got_again = across(1, after(both_panel, keep_across, got_early))
-
+    def rows(x):
+        return x.shape[0] // LANES * LANES
+
+    part = sums_of(slab, rows(far_first) // width)
+    keep_first, send_first = call(
+        lambda *refs: across_first_kernel(rest, *refs),
+        "across_first",
+        (part, part),
+        [vmem] * 5,
+        (vmem, vmem),
+        [pltpu.VMEM((rows(far_first), depth), jnp.bfloat16), *work],
+        0.0,
+    )(far_first, own_panel, x_panel, after(both_panel, keep_middle), weights)
+    keep_across, send_across = call(
+        lambda *refs: across_second_kernel(rest, *refs),
+        "across_second",
+        (block, block),
+        [vmem] * 8,
+        (vmem, vmem),
+        [pltpu.VMEM((rows(far_second), depth), jnp.bfloat16), *work],
+        0.0,
+    )(far_first, far_second, own_panel, x_panel, after(both_panel, keep_first, got_early), weights, keep_first, send_first)
+    got_across = swap(send_across, "pair", 1)
+
+    keep_near, send_near = call(
+        lambda *refs: late_near_kernel(rest, *refs),
+        "late_near",
+        (block, block),
+        [vmem] * 6,
+        (vmem, vmem),
+        [held, *work],
+        0.1,
+    )(far_first, far_second, passed_first, own_part, after(x_part, keep_across), weights)
     keep_late, send_late = call(
-        lambda *refs: late_kernel(rest, *refs),
-        "late",
+        lambda *refs: late_last_kernel(rest, *refs),
+        "late_last",
         (block, block),
         [vmem] * 7,
         (vmem, vmem),
         [held, *work],
         0.1,
-    )(far_first, far_second, passed_first, passed_second, own_part, after(x_part, keep_again, got_middle), weights)
+    )(passed_first, passed_second, keep_near, send_near, own_part, x_part, weights)
     got_late = swap(send_late, "pair", 1)
-    summed = call(add_kernel, "add", sums_of(slab, per_device), [vmem] * 4, vmem, [])(
-        keep_across, got_across, keep_again, got_again
-    )
+    summed = call(add_kernel, "add", block, [vmem] * 2, vmem, [])(keep_across, got_across)
     outwards = face(summed)
 
     out = call(

time: 69.3 us -> 66.9 us (0.965)
  starting transfers between devices: 24.4 us -> 22.2 us
    ppermute x13, waiting for transfers between devices: 19.6 us -> 22 us  [permute(): return lax.ppermute(x, ('row', 'col'), pairs)]
    ppermute x6 -> x5, waiting for transfers between devices: 9.01 us -> 6.84 us  [swap(): return lax.ppermute(array, axis, [(i, i ^ mask) for i in range(size)])]
    ppermute x6 -> x5, starting transfers between devices: 7.82 us -> 5.71 us  [swap(): return lax.ppermute(array, axis, [(i, i ^ mask) for i in range(size)])]
    pallas_call x4 -> x6, Pallas kernels: 3.28 us -> 3.6 us  [the longest x1 1.76 us: staged_body(): call(lambda *refs: late_last_kernel(rest, *refs), 'late_last', (block, bl...]
  transfers between devices with their start and end apart: 19 -> 18, of which waited for: 7 -> 6; matrix products, arithmetic and copies ran while one was open for 0% -> 0% of each run, Pallas kernels for 18% -> 18%
where the time goes in v6:
time: 66.9 us; the launch traced here: 66.8 us
  waiting for transfers between devices  28.9 us (43%)
  starting transfers between devices  22.2 us (33%)
  Pallas kernels  14.1 us (21%)
  local copies, waits for them, and re-layouts  1.45 us (2%)
    ppermute x13, waiting for transfers between devices, permute(): return lax.ppermute(x, ('row', 'col'), pairs)  22 us
    ppermute x13, starting transfers between devices, permute(): return lax.ppermute(x, ('row', 'col'), pairs)  16.5 us
    ppermute x5, waiting for transfers between devices, swap(): return lax.ppermute(array, axis, [(i, i ^ mask) for i in range(size)])  6.84 us
    pallas_call x1, Pallas kernels, staged_body(): call(lambda *refs: early_kernel(rest, *refs), 'early', (early, early, pan...  6.72 us
    ppermute x5, starting transfers between devices, swap(): return lax.ppermute(array, axis, [(i, i ^ mask) for i in range(size)])  5.71 us
    pallas_call x1, Pallas kernels, staged_body(): call(lambda *refs: prep_kernel(rest, *refs), 'prep', (panel(2), array(n,...  1.8 us
    pallas_call x1, Pallas kernels, staged_body(): call(lambda *refs: late_last_kernel(rest, *refs), 'late_last', (block, bl...  1.76 us
    pallas_call x1, Pallas kernels, staged_body(): call(finish_kernel, 'finish', sums_of(slab, block_a), [vmem] + [smem] * 2...  1.76 us
  transfers between devices with their start and end apart: 18, of which 6 were waited for; matrix products, arithmetic and copies ran while one was open for 0% of the time, Pallas kernels for 18%

profile of v6, /device:TPU:0, one launch (start us, length us, event | category | flops | bytes accessed | tf_op | source)
XLA Modules:
  0.0 66.8 jit_solution(1070524588765493482)
XLA Ops:
  0.0 1.2 %copy-done = bf16[900,32,16]{0,2,1:T(8,128)(2,1)S(1)} copy-done((bf16[900,32,16]{0,2,1:T(8,128)(2,1)S(1)}, bf16[900,32,16]{0,2,1:T(8,128)(2,1)}, u32[]{:S(2)}) %copy-start) | copy-done | bytes 921624
  1.4 0.5 collective-permute-start.4
  1.9 2.5 %collective-permute-start.5 = (bf16[528,896]{1,0:T(8,128)(2,1)S(1)}, bf16[528,896]{1,0:T(8,128)(2,1)S(1)}, u32[]{:S(2)}, u32[]{:S(2)}) collective-permute-start(bf16[528,896]{1,0:T(8,128)(2,1)S(1)} %pack.1.refs_0_), channel_id=1, source_target_pairs={{0,16},{2,4},{4,2},{6,22},{8,24},{10,12},{12,10},{14,30},{16,0},{1... | collective-permute-start | bytes 2838536 | tf_op jit(solution)/shard_map/ppermute | solution.py:412
  4.4 3.1 %collective-permute-start.2 = (bf16[528,896]{1,0:T(8,128)(2,1)S(1)}, bf16[528,896]{1,0:T(8,128)(2,1)S(1)}, u32[]{:S(2)}, u32[]{:S(2)}) collective-permute-start(bf16[528,896]{1,0:T(8,128)(2,1)S(1)} %pack.1.refs_0_), channel_id=1, source_target_pairs={{0,2},{2,0},{4,6},{6,4},{8,10},{10,8},{12,14},{14,12},{16,18},{18,... | collective-permute-start | bytes 2838536 | tf_op jit(solution)/shard_map/ppermute | solution.py:412
  7.5 1.5 %collective-permute-start.1 = (bf16[10,16,16]{2,1,0:T(8,128)(2,1)}, bf16[10,16,16]{2,1,0:T(8,128)(2,1)S(1)}, u32[]{:S(2)}, u32[]{:S(2)}) collective-permute-start(bf16[10,16,16]{2,1,0:T(8,128)(2,1)} %param.7), channel_id=1, source_target_pairs={{0,1},{1,0},{2,3},{3,2},{4,5},{5,4},{6,7},{7,6},{8,9},{9,8},{10,11... | collective-permute-start | bytes 15368 | tf_op jit(solution)/shard_map/ppermute | solution.py:354
  9.0 17.0 %collective-permute-done.5.turned.refs_0_ = bf16[528,896]{1,0:T(8,128)(2,1)S(1)} collective-permute-done((bf16[528,896]{1,0:T(8,128)(2,1)S(1)}, bf16[528,896]{1,0:T(8,128)(2,1)S(1)}, u32[]{:S(2)}, u32[]{:S(2)}) %collective-permute-start.5) | collective-permute-done | bytes 946208 | tf_op jit(solution)/shard_map/ppermute | solution.py:412
  26.2 2.4 %collective-permute-start.8 = (bf16[272,896]{1,0:T(8,128)(2,1)S(1)}, bf16[272,896]{1,0:T(8,128)(2,1)S(1)}, u32[]{:S(2)}, u32[]{:S(2)}) collective-permute-start(bf16[272,896]{1,0:T(8,128)(2,1)S(1)} %slice.20), channel_id=1, source_target_pairs={{0,2},{2,0},{4,6},{6,4},{8,10},{10,8},{12,14},{14,12},{16,18},{18,... | collective-permute-start | bytes 1462280 | tf_op jit(solution)/shard_map/ppermute | solution.py:412
  29.1 0.4 collective-permute-start.12
  29.7 1.8 %prep.1 = (bf16[16,2,32,1024]{3,2,1,0:T(8,128)(2,1)S(1)}, bf16[512,1024]{1,0:T(8,128)(2,1)S(1)}, bf16[32,512]{1,0:T(8,128)(2,1)S(1)}) custom-call(bf16[528,896]{1,0:T(8,128)(2,1)S(1)} %pack.1.refs_0_, bf16[528,896]{1,0:T(8,128)(2,1)S(1)} %collective-permute-done.refs_1_, bf16[160,16]{1,0:T(8,128)(2,1)S(1)} %bitcast.14, bf16[160,16]{1,0:T(8,128)(2,1)S(1)} %bitcast.15, ...), custom_call_target="tpu_custom_call" | custom-call | flops 21474836480 | bytes 4194304 | tf_op jit(solution)/shard_map/prep/pallas_call | solution.py:443
  31.5 1.4 %collective-permute-done.3.refs_1_ = bf16[528,896]{1,0:T(8,128)(2,1)S(1)} collective-permute-done((bf16[528,896]{1,0:T(8,128)(2,1)S(1)}, bf16[528,896]{1,0:T(8,128)(2,1)S(1)}, u32[]{:S(2)}, u32[]{:S(2)}) %collective-permute-start.3) | collective-permute-done | bytes 946208 | tf_op jit(solution)/shard_map/ppermute | solution.py:412
  33.0 6.7 %early.1 = (f32[2,10,32,128]{3,2,1,0:T(8,128)S(1)}, f32[2,10,32,128]{3,2,1,0:T(8,128)S(1)}, bf16[16,2,32,1024]{3,2,1,0:T(8,128)(2,1)S(1)}) custom-call(bf16[512,1024]{1,0:T(8,128)(2,1)S(1)} %get-tuple-element.30.refs_0_, bf16[16,2,32,1024]{3,2,1,0:T(8,128)(2,1)S(1)} %get-tuple-element.31.refs_1_.refs_3_.refs_4_, bf16[528,896]{1,0:T(8,128)(2,1)S(1)} %pick.1.refs_2_, ...), custom_call_target="tpu_custom_call" | custom-call | flops 2147483648 | bytes 4194304 | tf_op jit(solution)/shard_map/early/pallas_call | solution.py:475
  39.7 1.6 %collective-permute-start.7 = (f32[2,10,32,128]{3,2,1,0:T(8,128)S(1)}, f32[2,10,32,128]{3,2,1,0:T(8,128)S(1)}, u32[]{:S(2)}, u32[]{:S(2)}) collective-permute-start(f32[2,10,32,128]{3,2,1,0:T(8,128)S(1)} %get-tuple-element.34), channel_id=1, source_target_pairs={{0,1},{1,0},{2,3},{3,2},{4,5},{5,4},{6,7},{7,6},{8,9},{9,8},{10,11... | collective-permute-start | bytes 983048 | tf_op jit(solution)/shard_map/ppermute | solution.py:354
  41.3 4.3 %collective-permute-start.11 = (bf16[256,896]{1,0:T(8,128)(2,1)S(1)}, bf16[256,896]{1,0:T(8,128)(2,1)S(1)}, u32[]{:S(2)}, u32[]{:S(2)}) collective-permute-start(bf16[256,896]{1,0:T(8,128)(2,1)S(1)} %slice.22), channel_id=1, source_target_pairs={{0,2},{2,0},{4,6},{6,4},{8,10},{10,8},{12,14},{14,12},{16,18},{18,... | collective-permute-start | bytes 1376264 | tf_op jit(solution)/shard_map/ppermute | solution.py:412
  45.8 0.5 collective-permute-start.10
  46.3 4.0 %collective-permute-done.7.got_early = f32[2,10,32,128]{3,2,1,0:T(8,128)S(1)} collective-permute-done((f32[2,10,32,128]{3,2,1,0:T(8,128)S(1)}, f32[2,10,32,128]{3,2,1,0:T(8,128)S(1)}, u32[]{:S(2)}, u32[]{:S(2)}) %collective-permute-start.7) | collective-permute-done | bytes 327712 | tf_op jit(solution)/shard_map/ppermute | solution.py:354
  50.3 1.5 %collective-permute-start.16 = (f32[10,32,128]{2,1,0:T(8,128)S(1)}, f32[10,32,128]{2,1,0:T(8,128)S(1)}, u32[]{:S(2)}, u32[]{:S(2)}) collective-permute-start(f32[10,32,128]{2,1,0:T(8,128)S(1)} %get-tuple-element.52), channel_id=1, source_target_pairs={{0,1},{1,0},{2,3},{3,2},{4,5},{5,4},{6,7},{7,6},{8,9},{9,8},{10,11... | collective-permute-start | bytes 491528 | tf_op jit(solution)/shard_map/ppermute | solution.py:354
  51.9 1.7 %late_near.1 = (f32[10,32,128]{2,1,0:T(8,128)S(1)}, f32[10,32,128]{2,1,0:T(8,128)S(1)}) custom-call(bf16[400,896]{1,0:T(8,128)(2,1)S(1)} %collective-permute-done.12.refs_0_, bf16[128,896]{1,0:T(8,128)(2,1)S(1)} %collective-permute-done.13.refs_1_, bf16[272,896]{1,0:T(8,128)(2,1)S(1)} %collective-permute-done.8.refs_0_.refs_2_, ...), custom_call_target="tpu_custom_call" | custom-call | flops 2147483648 | bytes 4194304 | tf_op jit(solution)/shard_map/late_near/pallas_call | solution.py:521
  53.6 3.1 %collective-permute-done.11.refs_1_ = bf16[256,896]{1,0:T(8,128)(2,1)S(1)} collective-permute-done((bf16[256,896]{1,0:T(8,128)(2,1)S(1)}, bf16[256,896]{1,0:T(8,128)(2,1)S(1)}, u32[]{:S(2)}, u32[]{:S(2)}) %collective-permute-start.11) | collective-permute-done | bytes 458784 | tf_op jit(solution)/shard_map/ppermute | solution.py:412
  56.8 1.8 %late_last.1 = (f32[10,32,128]{2,1,0:T(8,128)S(1)}, f32[10,32,128]{2,1,0:T(8,128)S(1)}) custom-call(bf16[272,896]{1,0:T(8,128)(2,1)S(1)} %collective-permute-done.8.refs_0_.refs_2_, bf16[256,896]{1,0:T(8,128)(2,1)S(1)} %collective-permute-done.11.refs_1_, f32[10,32,128]{2,1,0:T(8,128)S(1)} %get-tuple-element.48.refs_2_, ...), custom_call_target="tpu_custom_call" | custom-call | flops 2147483648 | bytes 4194304 | tf_op jit(solution)/shard_map/late_last/pallas_call | solution.py:530
  58.5 0.6 collective-permute-start.15
  59.1 2.6 %collective-permute-start.17 = (f32[10,32,128]{2,1,0:T(8,128)S(1)}, f32[10,32,128]{2,1,0:T(8,128)S(1)}, u32[]{:S(2)}, u32[]{:S(2)}) collective-permute-start(f32[10,32,128]{2,1,0:T(8,128)S(1)} %add.1), channel_id=1, source_target_pairs={{0,2},{2,0},{4,6},{6,4},{8,10},{10,8},{12,14},{14,12},{16,18},{18,... | collective-permute-start | bytes 491528 | tf_op jit(solution)/shard_map/ppermute | solution.py:412
  61.7 2.8 %collective-permute-done.15.got_late = f32[10,32,128]{2,1,0:T(8,128)S(1)} collective-permute-done((f32[10,32,128]{2,1,0:T(8,128)S(1)}, f32[10,32,128]{2,1,0:T(8,128)S(1)}, u32[]{:S(2)}, u32[]{:S(2)}) %collective-permute-start.15) | collective-permute-done | bytes 163872 | tf_op jit(solution)/shard_map/ppermute | solution.py:354
  64.5 0.5 collective-permute-done.17.across
  65.0 1.8 %finish.1 = f32[10,128,128]{2,1,0:T(8,128)} custom-call(s32[4,128]{1,0:T(4,128)S(1)} %bitcast.11, s32[120]{0:T(128)S(1)} %copy-done.3, s32[2,20]{1,0:T(2,128)S(1)} %bitcast.13, f32[2,10,32,128]{3,2,1,0:T(8,128)S(1)} %get-tuple-element.33.keep_early, f32[2,10,32,128]{3,2,1,0:T(8,128)S(1)} %collective-permute-done.7.got_early, ...), custom_call_target="tpu_custom_call" | custom-call | tf_op jit(solution)/shard_map/finish/pallas_call | solution.py:543
  (42 shorter events, 1.3 us)
Async XLA Ops:
  0.0 1.2 %copy-start = (bf16[900,32,16]{0,2,1:T(8,128)(2,1)S(1)}, bf16[900,32,16]{0,2,1:T(8,128)(2,1)}, u32[]{:S(2)}) copy-start(bf16[900,32,16]{0,2,1:T(8,128)(2,1)} %param.6) | copy-start | bytes 2764804
  1.4 7.6 %collective-permute-start.4 = (bf16[528,896]{1,0:T(8,128)(2,1)S(1)}, bf16[528,896]{1,0:T(8,128)(2,1)S(1)}, u32[]{:S(2)}, u32[]{:S(2)}) collective-permute-start(bf16[528,896]{1,0:T(8,128)(2,1)S(1)} %pack.1.refs_0_), channel_id=1, source_target_pairs={{0,8},{2,18},{4,20},{6,14},{8,0},{10,26},{12,28},{14,6},{16,24},{1... | collective-permute-start | bytes 2838536 | tf_op jit(solution)/shard_map/ppermute | solution.py:412
  1.9 24.1 %collective-permute-start.5 = (bf16[528,896]{1,0:T(8,128)(2,1)S(1)}, bf16[528,896]{1,0:T(8,128)(2,1)S(1)}, u32[]{:S(2)}, u32[]{:S(2)}) collective-permute-start(bf16[528,896]{1,0:T(8,128)(2,1)S(1)} %pack.1.refs_0_), channel_id=1, source_target_pairs={{0,16},{2,4},{4,2},{6,22},{8,24},{10,12},{12,10},{14,30},{16,0},{1... | collective-permute-start | bytes 2838536 | tf_op jit(solution)/shard_map/ppermute | solution.py:412
  4.4 24.3 %collective-permute-start.2 = (bf16[528,896]{1,0:T(8,128)(2,1)S(1)}, bf16[528,896]{1,0:T(8,128)(2,1)S(1)}, u32[]{:S(2)}, u32[]{:S(2)}) collective-permute-start(bf16[528,896]{1,0:T(8,128)(2,1)S(1)} %pack.1.refs_0_), channel_id=1, source_target_pairs={{0,2},{2,0},{4,6},{6,4},{8,10},{10,8},{12,14},{14,12},{16,18},{18,... | collective-permute-start | bytes 2838536 | tf_op jit(solution)/shard_map/ppermute | solution.py:412
  7.5 21.9 %collective-permute-start = (bf16[528,896]{1,0:T(8,128)(2,1)S(1)}, bf16[528,896]{1,0:T(8,128)(2,1)S(1)}, u32[]{:S(2)}, u32[]{:S(2)}) collective-permute-start(bf16[528,896]{1,0:T(8,128)(2,1)S(1)} %pack.1.refs_0_), channel_id=1, source_target_pairs={{0,8},{2,10},{4,12},{6,14},{8,0},{10,2},{12,4},{14,6},{16,24},{18,... | collective-permute-start | bytes 2838536 | tf_op jit(solution)/shard_map/ppermute | solution.py:412
  7.5 21.6 %collective-permute-start.1 = (bf16[10,16,16]{2,1,0:T(8,128)(2,1)}, bf16[10,16,16]{2,1,0:T(8,128)(2,1)S(1)}, u32[]{:S(2)}, u32[]{:S(2)}) collective-permute-start(bf16[10,16,16]{2,1,0:T(8,128)(2,1)} %param.7), channel_id=1, source_target_pairs={{0,1},{1,0},{2,3},{3,2},{4,5},{5,4},{6,7},{7,6},{8,9},{9,8},{10,11... | collective-permute-start | bytes 15368 | tf_op jit(solution)/shard_map/ppermute | solution.py:354
  26.1 3.6 %copy-start.2 = (s32[20,2]{0,1:T(2,128)S(1)}, s32[20,2]{0,1:T(2,128)}, u32[]{:S(2)}) copy-start(s32[20,2]{0,1:T(2,128)} %param.11) | copy-start | bytes 484
  26.1 3.6 %copy-start.3 = (s32[120]{0:T(128)S(1)}, s32[120]{0:T(128)}, u32[]{:S(2)}) copy-start(s32[120]{0:T(128)} %occ.1) | copy-start | bytes 1444
  26.1 3.6 %copy-start.4 = (bf16[10,16,16]{2,1,0:T(8,128)(2,1)S(1)}, bf16[10,16,16]{2,1,0:T(8,128)(2,1)}, u32[]{:S(2)}) copy-start(bf16[10,16,16]{2,1,0:T(8,128)(2,1)} %param.7) | copy-start | bytes 15364
  26.1 3.6 %copy-start.5 = (s32[16]{0:T(128)S(1)}, s32[16]{0:T(128)}, u32[]{:S(2)}) copy-start(s32[16]{0:T(128)} %refs_4_.1) | copy-start | bytes 196
  26.1 6.9 %collective-permute-start.6 = (bf16[528,896]{1,0:T(8,128)(2,1)S(1)}, bf16[528,896]{1,0:T(8,128)(2,1)S(1)}, u32[]{:S(2)}, u32[]{:S(2)}) collective-permute-start(bf16[528,896]{1,0:T(8,128)(2,1)S(1)} %pick.1.refs_2_), channel_id=1, source_target_pairs={{0,8},{2,10},{4,12},{6,14},{8,0},{10,2},{12,4},{14,6},{16,24},{18,... | collective-permute-start | bytes 2838536 | tf_op jit(solution)/shard_map/ppermute | solution.py:412
  26.2 15.1 %collective-permute-start.8 = (bf16[272,896]{1,0:T(8,128)(2,1)S(1)}, bf16[272,896]{1,0:T(8,128)(2,1)S(1)}, u32[]{:S(2)}, u32[]{:S(2)}) collective-permute-start(bf16[272,896]{1,0:T(8,128)(2,1)S(1)} %slice.20), channel_id=1, source_target_pairs={{0,2},{2,0},{4,6},{6,4},{8,10},{10,8},{12,14},{14,12},{16,18},{18,... | collective-permute-start | bytes 1462280 | tf_op jit(solution)/shard_map/ppermute | solution.py:412
  28.7 12.6 %collective-permute-start.9 = (bf16[256,896]{1,0:T(8,128)(2,1)S(1)}, bf16[256,896]{1,0:T(8,128)(2,1)S(1)}, u32[]{:S(2)}, u32[]{:S(2)}) collective-permute-start(bf16[256,896]{1,0:T(8,128)(2,1)S(1)} %slice.21), channel_id=1, source_target_pairs={{0,8},{2,18},{4,20},{6,14},{8,0},{10,26},{12,28},{14,6},{16,24},{1... | collective-permute-start | bytes 1376264 | tf_op jit(solution)/shard_map/ppermute | solution.py:412
  29.1 17.2 %collective-permute-start.12 = (bf16[400,896]{1,0:T(8,128)(2,1)S(1)}, bf16[400,896]{1,0:T(8,128)(2,1)S(1)}, u32[]{:S(2)}, u32[]{:S(2)}) collective-permute-start(bf16[400,896]{1,0:T(8,128)(2,1)S(1)} %slice.23), channel_id=1, source_target_pairs={{0,8},{2,4},{4,2},{6,14},{8,0},{10,12},{12,10},{14,6},{16,24},{18,... | collective-permute-start | bytes 2150408 | tf_op jit(solution)/shard_map/ppermute | solution.py:412
  29.4 3.5 %collective-permute-start.3 = (bf16[528,896]{1,0:T(8,128)(2,1)S(1)}, bf16[528,896]{1,0:T(8,128)(2,1)S(1)}, u32[]{:S(2)}, u32[]{:S(2)}) collective-permute-start(bf16[528,896]{1,0:T(8,128)(2,1)S(1)} %collective-permute-done.2.refs_0_.refs_4_), channel_id=1, source_target_pairs={{0,8},{2,10},{4,12},{6,14},{8,0},{10,2},{12,4},{14,6},{16,24},{18,... | collective-permute-start | bytes 2838536 | tf_op jit(solution)/shard_map/ppermute | solution.py:412
  39.7 10.6 %collective-permute-start.7 = (f32[2,10,32,128]{3,2,1,0:T(8,128)S(1)}, f32[2,10,32,128]{3,2,1,0:T(8,128)S(1)}, u32[]{:S(2)}, u32[]{:S(2)}) collective-permute-start(f32[2,10,32,128]{3,2,1,0:T(8,128)S(1)} %get-tuple-element.34), channel_id=1, source_target_pairs={{0,1},{1,0},{2,3},{3,2},{4,5},{5,4},{6,7},{7,6},{8,9},{9,8},{10,11... | collective-permute-start | bytes 983048 | tf_op jit(solution)/shard_map/ppermute | solution.py:354
  41.3 4.5 %collective-permute-start.14 = (bf16[16,1,32,1024]{3,2,1,0:T(8,128)(2,1)S(1)}, bf16[16,1,32,1024]{3,2,1,0:T(8,128)(2,1)S(1)}, u32[]{:S(2)}, u32[]{:S(2)}) collective-permute-start(bf16[16,1,32,1024]{3,2,1,0:T(8,128)(2,1)S(1)} %outer_x.1.refs_2_.refs_3_), channel_id=1, source_target_pairs={{0,8},{2,10},{4,12},{6,14},{8,0},{10,2},{12,4},{14,6},{16,24},{18,... | collective-permute-start | bytes 3145736 | tf_op jit(solution)/shard_map/ppermute | solution.py:412
  41.3 15.4 %collective-permute-start.11 = (bf16[256,896]{1,0:T(8,128)(2,1)S(1)}, bf16[256,896]{1,0:T(8,128)(2,1)S(1)}, u32[]{:S(2)}, u32[]{:S(2)}) collective-permute-start(bf16[256,896]{1,0:T(8,128)(2,1)S(1)} %slice.22), channel_id=1, source_target_pairs={{0,2},{2,0},{4,6},{6,4},{8,10},{10,8},{12,14},{14,12},{16,18},{18,... | collective-permute-start | bytes 1376264 | tf_op jit(solution)/shard_map/ppermute | solution.py:412
  45.6 4.7 %collective-permute-start.13 = (bf16[128,896]{1,0:T(8,128)(2,1)S(1)}, bf16[128,896]{1,0:T(8,128)(2,1)S(1)}, u32[]{:S(2)}, u32[]{:S(2)}) collective-permute-start(bf16[128,896]{1,0:T(8,128)(2,1)S(1)} %slice.24), channel_id=1, source_target_pairs={{0,8},{2,4},{4,2},{6,14},{8,0},{10,12},{12,10},{14,6},{16,24},{18,... | collective-permute-start | bytes 688136 | tf_op jit(solution)/shard_map/ppermute | solution.py:412
  45.8 15.9 %collective-permute-start.10 = (f32[10,32,128]{2,1,0:T(8,128)S(1)}, f32[10,32,128]{2,1,0:T(8,128)S(1)}, u32[]{:S(2)}, u32[]{:S(2)}) collective-permute-start(f32[10,32,128]{2,1,0:T(8,128)S(1)} %get-tuple-element.39), channel_id=1, source_target_pairs={{0,1},{1,0},{2,3},{3,2},{4,5},{5,4},{6,7},{7,6},{8,9},{9,8},{10,11... | collective-permute-start | bytes 491528 | tf_op jit(solution)/shard_map/ppermute | solution.py:354
  50.3 8.8 %collective-permute-start.16 = (f32[10,32,128]{2,1,0:T(8,128)S(1)}, f32[10,32,128]{2,1,0:T(8,128)S(1)}, u32[]{:S(2)}, u32[]{:S(2)}) collective-permute-start(f32[10,32,128]{2,1,0:T(8,128)S(1)} %get-tuple-element.52), channel_id=1, source_target_pairs={{0,1},{1,0},{2,3},{3,2},{4,5},{5,4},{6,7},{7,6},{8,9},{9,8},{10,11... | collective-permute-start | bytes 491528 | tf_op jit(solution)/shard_map/ppermute | solution.py:354
  56.7 8.3 %copy-start.1 = (s32[512]{0:T(512)S(1)}, s32[512]{0:T(512)}, u32[]{:S(2)}) copy-start(s32[512]{0:T(512)} %param.8) | copy-start | bytes 6148
  58.5 6.0 %collective-permute-start.15 = (f32[10,32,128]{2,1,0:T(8,128)S(1)}, f32[10,32,128]{2,1,0:T(8,128)S(1)}, u32[]{:S(2)}, u32[]{:S(2)}) collective-permute-start(f32[10,32,128]{2,1,0:T(8,128)S(1)} %get-tuple-element.51), channel_id=1, source_target_pairs={{0,1},{1,0},{2,3},{3,2},{4,5},{5,4},{6,7},{7,6},{8,9},{9,8},{10,11... | collective-permute-start | bytes 491528 | tf_op jit(solution)/shard_map/ppermute | solution.py:354
  59.1 5.9 %collective-permute-start.17 = (f32[10,32,128]{2,1,0:T(8,128)S(1)}, f32[10,32,128]{2,1,0:T(8,128)S(1)}, u32[]{:S(2)}, u32[]{:S(2)}) collective-permute-start(f32[10,32,128]{2,1,0:T(8,128)S(1)} %add.1), channel_id=1, source_target_pairs={{0,2},{2,0},{4,6},{6,4},{8,10},{10,8},{12,14},{14,12},{16,18},{18,... | collective-permute-start | bytes 491528 | tf_op jit(solution)/shard_map/ppermute | solution.py:412
